TPU v7x, 32 devices: a whole 2x2x4 slice. The times are simulated.
32 devices in a mesh: fsdp: 16 (over z, y, core), tp: 2 (over x).
Axes of the slice: x: 2, y: 2, z: 4, core: 2. Of those that a mesh axis runs over, the one named last changes fastest.
Arguments:
- tokens: bfloat16 [16384, 1024], P(('fsdp', 'tp')), may hold values from -6 to 6
- segments: int32 [16384], P('fsdp'), may hold values from 0 to 2, as said below
- slots: int32 [16, 32, 256], P('fsdp', 'tp'), may hold values from -1 to 1023, as said below
- gate_values: float32 [16, 32, 256], P('fsdp', 'tp'), may hold values from 0.1 to 0.5
- gains: float32 [2, 1024], P(None, ('fsdp', 'tp')), may hold values from 0.5 to 1.5
- w_query: bfloat16 [1024, 1024], P('fsdp', 'tp'), may hold values from -0.1875 to 0.1875
- w_key: bfloat16 [1024, 512], P('fsdp', 'tp'), may hold values from -0.1875 to 0.1875
- w_value: bfloat16 [1024, 512], P('fsdp', 'tp'), may hold values from -0.1875 to 0.1875
- w_out: bfloat16 [1024, 1024], P('fsdp', 'tp'), may hold values from -2 to 2
- w_gate: bfloat16 [1024, 16384], P('fsdp', 'tp'), may hold values from -0.1875 to 0.1875
- w_up: bfloat16 [1024, 16384], P('fsdp', 'tp'), may hold values from -0.1875 to 0.1875
- w_down: bfloat16 [1024, 16384], P('fsdp', 'tp'), may hold values from -0.25 to 0.25
- cotangent: bfloat16 [16384, 1024], P(('fsdp', 'tp')), may hold values from -6 to 6
Outputs:
- mixed: bfloat16 [16384, 1024], P(('fsdp', 'tp'))
- grad_tokens: float32 [16384, 1024], P(('fsdp', 'tp'))
- grad_gains: float32 [2, 1024], P(None, ('fsdp', 'tp'))
- grad_query: float32 [1024, 1024], P('fsdp', 'tp')
- grad_key: float32 [1024, 512], P('fsdp', 'tp')
- grad_value: float32 [1024, 512], P('fsdp', 'tp')
- grad_out: float32 [1024, 1024], P('fsdp', 'tp')
- grad_gate: float32 [1024, 16384], P('fsdp', 'tp')
- grad_up: float32 [1024, 16384], P('fsdp', 'tp')
- grad_down: float32 [1024, 16384], P('fsdp', 'tp')
Inputs may be any that keep to these rules, and one draw needn't show every extreme that they name: `segments`: ids count documents within each packed sequence of 1024 tokens and never fall along it; every packed sequence holds documents 0, 1 and 2, the first ending within its first 512 tokens and the last starting within its last 512 tokens. `slots`: entries are token positions within the packed sequence; -1 marks an empty slot. A token stands at most once in a block and in at most 8 blocks of its sequence; the live entries of a block increase along it; in every packed sequence some expert's block has no empty slot.
All inputs are finite; a program needn't handle non-finite values.
Results may differ from a plain program's by a relative error of at most 0.018.
Values may be sent and summed in bfloat16 or wider, within the bound.
No kernel may reach another device: no remote copies, remote signals or barrier semaphores. Data moves between devices by JAX's collectives and lax.ppermute only.
A program may use at most 320 MiB of HBM per device.

v0:
```python
import jax
import jax.numpy as jnp
from jax import lax
from jax.sharding import PartitionSpec as P

D = 1024
Q_HEADS = 16
KV_HEADS = 8
HEAD_DIM = 64
FF = 512


EPS = 1e-06


def norm_forward(values, gain_row):
    rms_scale = lax.rsqrt(jnp.mean(values * values, axis=-1, keepdims=True) + EPS)
    return (values * rms_scale * gain_row, rms_scale)


def norm_backward(values, rms_scale, gain_row, gradient):
    weighted = gradient * gain_row
    centre = jnp.mean(weighted * values, axis=-1, keepdims=True)
    back_values = rms_scale * weighted - values * rms_scale * rms_scale * rms_scale * centre
    return (back_values, jnp.sum(gradient * values * rms_scale, axis=0))


def block_scores(query_block, key_heads, first_row, seg_query, seg_keys):
    scores = jnp.einsum(
        "qkgd,tkd->kgqt", query_block, key_heads, preferred_element_type=jnp.float32
    ) * HEAD_DIM ** (-0.5)
    query_pos = first_row + jnp.arange(query_block.shape[0], dtype=jnp.int32)
    key_pos = jnp.arange(key_heads.shape[0], dtype=jnp.int32)
    allowed = (query_pos[:, None] >= key_pos[None, :]) & (seg_query[:, None] == seg_keys[None, :])
    return jnp.where(allowed, scores, -1e30)


def contract_first(left, right):
    return lax.dot_general(
        left, right, (((0,), (0,)), ((), ())), preferred_element_type=jnp.float32
    )


def contract_last(left, right):
    return lax.dot_general(
        left, right, (((1,), (1,)), ((), ())), preferred_element_type=jnp.float32
    )


def expert_matrices(w_gate, w_up, w_down):
    return (
        lax.all_gather(w_gate, "fsdp", axis=0, tiled=True),
        lax.all_gather(w_up, "fsdp", axis=0, tiled=True),
        lax.all_gather(w_down, "fsdp", axis=0, tiled=True),
    )


def body(
    tokens,
    segments,
    slots,
    gate_values,
    gains,
    w_query,
    w_key,
    w_value,
    w_out,
    w_gate,
    w_up,
    w_down,
    cotangent,
):
    seq_length = segments.shape[0]
    block_rows = min(512, seq_length)
    block_count = seq_length // block_rows
    group_size = Q_HEADS // KV_HEADS
    all_gains = lax.all_gather(gains, ("fsdp", "tp"), axis=1, tiled=True)
    query_w, key_w, value_w, out_w = (
        lax.all_gather(w_query, "fsdp", axis=0, tiled=True),
        lax.all_gather(w_key, "fsdp", axis=0, tiled=True),
        lax.all_gather(w_value, "fsdp", axis=0, tiled=True),
        lax.all_gather(w_out, "fsdp", axis=0, tiled=True),
    )
    gate_w, up_w, down_w = expert_matrices(w_gate, w_up, w_down)
    heads_kv = key_w.shape[1] // HEAD_DIM
    slot_index = slots[0]
    local_experts = slot_index.shape[0]
    resid = tokens.astype(jnp.float32)
    normed_one, scale_one = norm_forward(resid, all_gains[0])
    whole_one = lax.all_gather(normed_one.astype(jnp.bfloat16), "tp", axis=0, tiled=True)
    queries = jnp.dot(whole_one, query_w, preferred_element_type=jnp.float32).astype(jnp.bfloat16)
    keys_flat = jnp.dot(whole_one, key_w, preferred_element_type=jnp.float32).astype(jnp.bfloat16)
    values_flat = jnp.dot(whole_one, value_w, preferred_element_type=jnp.float32).astype(
        jnp.bfloat16
    )
    query_blocks = queries.reshape(block_count, block_rows, heads_kv, group_size, HEAD_DIM)
    key_heads = keys_flat.reshape(seq_length, heads_kv, HEAD_DIM)
    value_heads = values_flat.reshape(seq_length, heads_kv, HEAD_DIM)
    seg_blocks = segments.reshape(block_count, block_rows)
    block_starts = jnp.arange(block_count, dtype=jnp.int32) * block_rows

    def attend(inputs):
        query_block, seg_query, first_row = inputs
        scores = block_scores(query_block, key_heads, first_row, seg_query, segments)
        row_top = jnp.max(scores, axis=-1, keepdims=True)
        expo_terms = jnp.exp(scores - row_top)
        exp_total = jnp.sum(expo_terms, axis=-1, keepdims=True)
        prob_low = (expo_terms / exp_total).astype(jnp.bfloat16)
        mixed_heads = jnp.einsum(
            "kgqt,tkd->qkgd", prob_low, value_heads, preferred_element_type=jnp.float32
        )
        return (mixed_heads.astype(jnp.bfloat16), row_top + jnp.log(exp_total))

    attended_blocks, log_totals = lax.map(attend, (query_blocks, seg_blocks, block_starts))
    attended = attended_blocks.reshape(seq_length, heads_kv * group_size * HEAD_DIM)
    attn_out = lax.psum_scatter(
        contract_last(attended, out_w), "tp", scatter_dimension=0, tiled=True
    )
    hidden = resid + attn_out
    normed_two, scale_two = norm_forward(hidden, all_gains[1])
    whole_two = lax.all_gather(normed_two.astype(jnp.bfloat16), "tp", axis=0, tiled=True)
    live_slot = slot_index >= 0
    flat_index = jnp.where(live_slot, slot_index, 0).reshape(-1)
    slot_weight = jnp.where(live_slot, gate_values[0], 0.0)[:, :, None]
    picked = jnp.take(whole_two, flat_index, axis=0).reshape(slot_index.shape + (D,))
    gate_cube = gate_w.reshape(D, local_experts, FF)
    up_cube = up_w.reshape(D, local_experts, FF)
    down_cube = down_w.reshape(D, local_experts, FF)
    gate_pre = jnp.einsum("ecd,def->ecf", picked, gate_cube, preferred_element_type=jnp.float32)
    up_pre = jnp.einsum("ecd,def->ecf", picked, up_cube, preferred_element_type=jnp.float32)
    sigmoid_gate = jax.nn.sigmoid(gate_pre)
    silu_gate = gate_pre * sigmoid_gate
    inner_act = (silu_gate * up_pre).astype(jnp.bfloat16)
    slot_out = jnp.einsum("ecf,def->ecd", inner_act, down_cube, preferred_element_type=jnp.float32)
    weighted = (slot_out * slot_weight).reshape(-1, D)
    local_sum = jnp.zeros((seq_length, D), jnp.float32).at[flat_index].add(weighted)
    expert_sum = lax.psum_scatter(
        local_sum.astype(jnp.bfloat16), "tp", scatter_dimension=0, tiled=True
    ).astype(jnp.float32)
    mixed_out = (hidden + expert_sum).astype(jnp.bfloat16)
    whole_grad = lax.all_gather(cotangent, "tp", axis=0, tiled=True)
    slot_grad = (
        jnp.take(whole_grad, flat_index, axis=0).reshape(picked.shape).astype(jnp.float32)
        * slot_weight
    ).astype(jnp.bfloat16)
    back_gate, back_up, back_down = expert_matrices(w_gate, w_up, w_down)
    back_gate = back_gate.reshape(D, local_experts, FF)
    back_up = back_up.reshape(D, local_experts, FF)
    back_down = back_down.reshape(D, local_experts, FF)
    grad_down = jnp.einsum(
        "ecf,ecd->def", inner_act, slot_grad, preferred_element_type=jnp.float32
    ).reshape(D, -1)
    inner_grad = jnp.einsum(
        "ecd,def->ecf", slot_grad, back_down, preferred_element_type=jnp.float32
    )
    gate_grad = (
        inner_grad * up_pre * sigmoid_gate * (1.0 + gate_pre * (1.0 - sigmoid_gate))
    ).astype(jnp.bfloat16)
    up_grad = (inner_grad * silu_gate).astype(jnp.bfloat16)
    grad_gate = jnp.einsum(
        "ecd,ecf->def", picked, gate_grad, preferred_element_type=jnp.float32
    ).reshape(D, -1)
    grad_up = jnp.einsum(
        "ecd,ecf->def", picked, up_grad, preferred_element_type=jnp.float32
    ).reshape(D, -1)
    picked_grad = jnp.einsum(
        "ecf,def->ecd", gate_grad, back_gate, preferred_element_type=jnp.float32
    )
    picked_grad = picked_grad + jnp.einsum(
        "ecf,def->ecd", up_grad, back_up, preferred_element_type=jnp.float32
    )
    local_grad = (
        jnp.zeros((seq_length, D), jnp.float32).at[flat_index].add(picked_grad.reshape(-1, D))
    )
    second_grad = lax.psum_scatter(local_grad, "tp", scatter_dimension=0, tiled=True)
    back_two, second_gain = norm_backward(hidden, scale_two, all_gains[1], second_grad)
    grad_hidden = cotangent.astype(jnp.float32) + back_two
    whole_hidden_grad = lax.all_gather(grad_hidden.astype(jnp.bfloat16), "tp", axis=0, tiled=True)
    grad_out = contract_first(whole_hidden_grad, attended)
    attended_grad = jnp.dot(whole_hidden_grad, out_w, preferred_element_type=jnp.float32).astype(
        jnp.bfloat16
    )
    attended_grad_blocks = attended_grad.reshape(
        block_count, block_rows, heads_kv, group_size, HEAD_DIM
    )

    def attend_back(totals, inputs):
        key_total, value_total = totals
        query_block, seg_query, first_row, log_block, grad_block = inputs
        scores = block_scores(query_block, key_heads, first_row, seg_query, segments)
        probabilities = jnp.exp(scores - log_block)
        prob_grad = jnp.einsum(
            "qkgd,tkd->kgqt", grad_block, value_heads, preferred_element_type=jnp.float32
        )
        centre = jnp.sum(probabilities * prob_grad, axis=-1, keepdims=True)
        score_grad = (probabilities * (prob_grad - centre)).astype(jnp.bfloat16)
        query_part = jnp.einsum(
            "kgqt,tkd->qkgd", score_grad, key_heads, preferred_element_type=jnp.float32
        ) * HEAD_DIM ** (-0.5)
        key_total = key_total + jnp.einsum(
            "kgqt,qkgd->tkd", score_grad, query_block, preferred_element_type=jnp.float32
        ) * HEAD_DIM ** (-0.5)
        value_total = value_total + jnp.einsum(
            "kgqt,qkgd->tkd",
            probabilities.astype(jnp.bfloat16),
            grad_block,
            preferred_element_type=jnp.float32,
        )
        return ((key_total, value_total), query_part)

    zero_heads = jnp.zeros((seq_length, heads_kv, HEAD_DIM), jnp.float32)
    (key_total, value_total), query_parts = lax.scan(
        attend_back,
        (zero_heads, zero_heads),
        (query_blocks, seg_blocks, block_starts, log_totals, attended_grad_blocks),
    )
    query_grad = query_parts.reshape(seq_length, -1).astype(jnp.bfloat16)
    key_grad = key_total.reshape(seq_length, -1).astype(jnp.bfloat16)
    value_grad = value_total.reshape(seq_length, -1).astype(jnp.bfloat16)
    grad_query = contract_first(whole_one, query_grad)
    grad_key = contract_first(whole_one, key_grad)
    grad_value = contract_first(whole_one, value_grad)
    first_grad = lax.psum_scatter(
        (
            contract_last(query_grad, query_w)
            + contract_last(key_grad, key_w)
            + contract_last(value_grad, value_w)
        ).astype(jnp.bfloat16),
        "tp",
        scatter_dimension=0,
        tiled=True,
    ).astype(jnp.float32)
    back_one, first_gain = norm_backward(resid, scale_one, all_gains[0], first_grad)
    grad_tokens = grad_hidden + back_one
    grad_gains = lax.psum_scatter(
        jnp.stack([first_gain, second_gain]), ("fsdp", "tp"), scatter_dimension=1, tiled=True
    )
    summed = (
        lax.psum_scatter(
            grad_query.astype(jnp.bfloat16), "fsdp", scatter_dimension=0, tiled=True
        ).astype(jnp.float32),
        lax.psum_scatter(
            grad_key.astype(jnp.bfloat16), "fsdp", scatter_dimension=0, tiled=True
        ).astype(jnp.float32),
        lax.psum_scatter(
            grad_value.astype(jnp.bfloat16), "fsdp", scatter_dimension=0, tiled=True
        ).astype(jnp.float32),
        lax.psum_scatter(
            grad_out.astype(jnp.bfloat16), "fsdp", scatter_dimension=0, tiled=True
        ).astype(jnp.float32),
        lax.psum_scatter(
            grad_gate.astype(jnp.bfloat16), "fsdp", scatter_dimension=0, tiled=True
        ).astype(jnp.float32),
        lax.psum_scatter(
            grad_up.astype(jnp.bfloat16), "fsdp", scatter_dimension=0, tiled=True
        ).astype(jnp.float32),
        lax.psum_scatter(
            grad_down.astype(jnp.bfloat16), "fsdp", scatter_dimension=0, tiled=True
        ).astype(jnp.float32),
    )
    return (
        mixed_out,
        grad_tokens,
        grad_gains,
        summed[0],
        summed[1],
        summed[2],
        summed[3],
        summed[4],
        summed[5],
        summed[6],
    )


def solution(mesh):
    in_specs = (
        P(("fsdp", "tp"), None),
        P("fsdp"),
        P("fsdp", "tp", None),
        P("fsdp", "tp", None),
        P(None, ("fsdp", "tp")),
        P("fsdp", "tp"),
        P("fsdp", "tp"),
        P("fsdp", "tp"),
        P("fsdp", "tp"),
        P("fsdp", "tp"),
        P("fsdp", "tp"),
        P("fsdp", "tp"),
        P(("fsdp", "tp"), None),
    )
    out_specs = (
        P(("fsdp", "tp"), None),
        P(("fsdp", "tp"), None),
        P(None, ("fsdp", "tp")),
        P("fsdp", "tp"),
        P("fsdp", "tp"),
        P("fsdp", "tp"),
        P("fsdp", "tp"),
        P("fsdp", "tp"),
        P("fsdp", "tp"),
        P("fsdp", "tp"),
    )
    return jax.shard_map(body, mesh=mesh, in_specs=in_specs, out_specs=out_specs, check_vma=False)
```

profile of v0, /device:TPU:0, one launch (start us, length us, event | category | flops | bytes accessed | tf_op | source)
XLA Modules:
  0.0 1994.7 jit_solution(12489793474758037037)
XLA Ops:
  8.0 70.0 %all-gather = f32[32,32,2]{1,2,0:T(2,128)S(1)} all-gather(f32[1,32,2]{1,2,0:T(2,128)} %bitcast.311), channel_id=1, replica_groups=mesh['fsdp'=16,'tp'=2] {'fsdp','tp'}, dimensions={0}, use_global_device_ids=true | all-gather | bytes 8448 | tf_op jit(solution)/shard_map/all_gather | solution.py:77
  84.2 18.7 all_gather.42
  102.9 21.0 %all_gather.43 = bf16[1024,256]{1,0:T(8,128)(2,1)S(1)} all-gather(bf16[64,256]{1,0:T(8,128)(2,1)S(1)} %copy-done.46), channel_id=1, replica_groups=mesh['fsdp'=16,'tp'=2] {'fsdp'}, dimensions={0}, use_global_device_ids=true | all-gather | bytes 557056 | tf_op jit(solution)/shard_map/all_gather | solution.py:81
  138.6 30.1 %while.27 = (s32[]{:T(128)}, bf16[2,512,4,2,64]{1,4,3,2,0:T(8,128)(2,1)}, f32[2,4,2,512,1]{3,2,1,4,0:T(2,128)}, s32[2]{0:T(128)S(1)}, s32[2,512]{1,0:T(2,128)S(1...) while((s32[]{:T(128)}, ...), condition=%wide.region_4.5_spmd, body=%wide.region_1.4_spmd.sunk | while | flops 1125904896 | bytes 63060164 | solution.py:114
  178.5 49.6 %reduce-scatter.15.cloned.1.call-done = f32[512,1024]{1,0:T(8,128)} async-done(((f32[1024,1024]{1,0:T(8,128)}), f32[512,1024]{1,0:T(8,128)}) %reduce-scatter.15.cloned.1.call-update) | async-done | bytes 2097168 | tf_op jit(solution)/shard_map/reduce_scatter | solution.py:116
  235.7 27.1 %all-gather.25.cloned.1.call-done = bf16[1024,1024]{1,0:T(8,128)(2,1)} async-done(((bf16[512,1024]{1,0:T(8,128)(2,1)}), bf16[1024,1024]{1,0:T(8,128)(2,1)}) %all-gather.25.cloned.1.call-update) | async-done | bytes 2097168 | tf_op jit(solution)/shard_map/all_gather | solution.py:141
  262.7 22.8 %gather_fusion.1 = bf16[4096,1024]{1,0:T(8,128)(2,1)} fusion(bf16[1024,1024]{1,0:T(8,128)(2,1)} %all-gather.25.cloned.1.call-done, s32[4096]{0:T(1024)S(1)} %fusion.70), kind=kCustom, calls=%fused_computation.1.clone | custom fusion | bytes 16793600 | tf_op jit(solution)/shard_map/jit(_take)/gather | solution.py:143
  297.9 22.8 %gather_fusion = bf16[4096,1024]{1,0:T(8,128)(2,1)} fusion(bf16[1024,1024]{1,0:T(8,128)(2,1)} %all-gather.17.cloned.1.call-done, s32[4096]{0:T(1024)S(1)} %fusion.70), kind=kCustom, calls=%fused_computation.clone | custom fusion | bytes 16793600 | tf_op jit(solution)/shard_map/jit(_take)/gather | solution.py:125
  332.5 94.8 %all-gather.19.cloned.1.call-done = bf16[1024,8192]{1,0:T(8,128)(2,1)} async-done(((bf16[64,8192]{1,0:T(8,128)(2,1)}), bf16[1024,8192]{1,0:T(8,128)(2,1)}) %all-gather.19.cloned.1.call-update) | async-done | bytes 16777232 | tf_op jit(solution)/shard_map/all_gather | solution.py:52
  427.3 22.6 %copy.59 = bf16[1024,8192]{0,1:T(8,128)(2,1)} copy(bf16[1024,8192]{1,0:T(8,128)(2,1)} %all-gather.19.cloned.1.call-done) | data formatting | bytes 33554432 | tf_op jit(solution)/shard_map/all_gather | solution.py:52
  449.8 104.9 %all-gather.21.cloned.1.call-done = bf16[1024,8192]{1,0:T(8,128)(2,1)} async-done(((bf16[64,8192]{1,0:T(8,128)(2,1)}), bf16[1024,8192]{1,0:T(8,128)(2,1)}) %all-gather.21.cloned.1.call-update) | async-done | bytes 16777232 | tf_op jit(solution)/shard_map/all_gather | solution.py:53
  554.8 22.6 %copy.61 = bf16[1024,8192]{0,1:T(8,128)(2,1)} copy(bf16[1024,8192]{1,0:T(8,128)(2,1)} %all-gather.21.cloned.1.call-done) | data formatting | bytes 33554432 | tf_op jit(solution)/shard_map/all_gather | solution.py:53
  602.8 79.4 %all-gather.23.cloned.1.call-done = bf16[1024,8192]{1,0:T(8,128)(2,1)} async-done(((bf16[64,8192]{1,0:T(8,128)(2,1)}), bf16[1024,8192]{1,0:T(8,128)(2,1)}) %all-gather.23.cloned.1.call-update) | async-done | bytes 16777232 | tf_op jit(solution)/shard_map/all_gather | solution.py:54
  682.2 22.4 %copy.63 = bf16[1024,8192]{0,1:T(8,128)(2,1)} copy(bf16[1024,8192]{1,0:T(8,128)(2,1)} %all-gather.23.cloned.1.call-done) | data formatting | bytes 33554432 | tf_op jit(solution)/shard_map/all_gather | solution.py:54
  704.6 24.8 %multiply_convert_fusion = (bf16[16,256,512]{2,1,0:T(8,128)(2,1)}, bf16[16,256,512]{2,1,0:T(8,128)(2,1)}, bf16[16,256,512]{2,1,0:T(8,128)(2,1)}) fusion(f32[16,256,512]{2,1,0:T(8,128)} %fusion.74, f32[16,256,512]{2,1,0:T(8,128)} %fusion.75, bf16[1024,16,512]{0,2,1:T(8,128)(2,1)} %bitcast.269, bf16[16,256,1024]{2,1,0:T(8,128)(2,1)} %bitcast.275, ...), kind=kOutput, calls=%fused_computation.72 | convolution fusion | flops 4339007488 | bytes 54542336 | tf_op jit(solution)/shard_map/ecd,def->ecf/dot_general | solution.py:153
  746.8 17.4 convolution_add_fusion
  764.2 38.7 %scatter_custom_fusion.1 = f32[1024,1024]{1,0:T(8,128)} fusion(s32[4096]{0:T(1024)} %bitcast.308, f32[4096,1024]{1,0:T(8,128)} %bitcast.278, f32[]{:T(128)} %constant.48.clone.1), kind=kCustom, calls=%fused_computation.106 | custom fusion | flops 4194304 | bytes 4194816 | tf_op jit(solution)/shard_map/scatter-add | solution.py:173
  803.0 52.6 %reduce-scatter.19.cloned.1.call-done = f32[512,1024]{1,0:T(8,128)} async-done(((f32[1024,1024]{1,0:T(8,128)}), f32[512,1024]{1,0:T(8,128)}) %reduce-scatter.19.cloned.1.call-update) | async-done | bytes 2097168 | tf_op jit(solution)/shard_map/reduce_scatter | solution.py:175
  861.1 33.0 %all-gather.27.cloned.1.call-done = bf16[1024,1024]{1,0:T(8,128)(2,1)} async-done(((bf16[512,1024]{1,0:T(8,128)(2,1)}), bf16[1024,1024]{1,0:T(8,128)(2,1)}) %all-gather.27.cloned.1.call-update) | async-done | bytes 2097168 | tf_op jit(solution)/shard_map/all_gather | solution.py:178
  904.0 88.4 %while.28 = (s32[]{:T(128)}, f32[1024,4,64]{0,2,1:T(8,128)}, f32[1024,4,64]{0,2,1:T(8,128)}, bf16[2,512,4,2,64]{1,4,3,2,0:T(8,128)(2,1)}, bf16[2,512,4,2,64]{1,4...) while((s32[]{:T(128)}, f32[1024,4,64]{0,2,1:T(8,128)}, ...), condition=%wide.region_14.16_spmd.clone, body=%wide.region_12.15_spmd.clone.sunk | while | flops 2725245440 | bytes 192510384 | solution.py:212
  1014.4 17.5 convolution_multiply_fusion.1
  1031.9 38.5 %scatter_custom_fusion = f32[1024,1024]{1,0:T(8,128)} fusion(s32[4096]{0:T(1024)} %bitcast.309, f32[4096,1024]{1,0:T(8,128)} %bitcast.277, f32[]{:T(128)} %constant.48.clone.1), kind=kCustom, calls=%fused_computation.108 | custom fusion | flops 4194304 | bytes 4194816 | tf_op jit(solution)/shard_map/scatter-add | solution.py:136
  1089.2 21.3 %copy.77 = bf16[1024,8192]{1,0:T(8,128)(2,1)} copy(bf16[1024,8192]{0,1:T(8,128)(2,1)} %bitcast.273) | data formatting | bytes 33554432 | tf_op jit(solution)/shard_map/convert_element_type | solution.py:258
  1122.8 21.3 %copy.75 = bf16[1024,8192]{1,0:T(8,128)(2,1)} copy(bf16[1024,8192]{0,1:T(8,128)(2,1)} %bitcast.272) | data formatting | bytes 33554432 | tf_op jit(solution)/shard_map/convert_element_type | solution.py:255
  1156.4 21.4 %copy.73 = bf16[1024,8192]{1,0:T(8,128)(2,1)} copy(bf16[1024,8192]{0,1:T(8,128)(2,1)} %bitcast.271) | data formatting | bytes 33554432 | tf_op jit(solution)/shard_map/convert_element_type | solution.py:252
  1180.7 29.9 %reduce-scatter.29.cloned.1.call-done = bf16[64,512]{1,0:T(8,128)(2,1)} async-done(((bf16[1024,512]{1,0:T(8,128)(2,1)}), bf16[64,512]{1,0:T(8,128)(2,1)}) %reduce-scatter.29.cloned.1.call-update) | async-done | bytes 65552 | tf_op jit(solution)/shard_map/reduce_scatter | solution.py:248
  1212.2 58.9 %reduce-scatter.23.cloned.1.call-done = bf16[64,512]{1,0:T(8,128)(2,1)} async-done(((bf16[1024,512]{1,0:T(8,128)(2,1)}), bf16[64,512]{1,0:T(8,128)(2,1)}) %reduce-scatter.23.cloned.1.call-update) | async-done | bytes 65552 | tf_op jit(solution)/shard_map/reduce_scatter | solution.py:239
  1272.6 32.1 %reduce-scatter.17.cloned.1.call-done = bf16[512,1024]{1,0:T(8,128)(2,1)} async-done(((bf16[1024,1024]{1,0:T(8,128)(2,1)}), bf16[512,1024]{1,0:T(8,128)(2,1)}) %reduce-scatter.17.cloned.1.call-update) | async-done | bytes 1048592 | tf_op jit(solution)/shard_map/reduce_scatter | solution.py:137
  1309.3 132.0 %reduce-scatter.37.cloned.1.call-done = f32[32,2]{1,0:T(8,128)} async-done(((f32[1024,2]{1,0:T(8,128)}), f32[32,2]{1,0:T(8,128)}) %reduce-scatter.37.cloned.1.call-update) | async-done | bytes 272
  1442.7 177.9 %reduce-scatter.35.cloned.1.call-done = bf16[64,8192]{1,0:T(8,128)(2,1)} async-done(((bf16[1024,8192]{1,0:T(8,128)(2,1)}), bf16[64,8192]{1,0:T(8,128)(2,1)}) %reduce-scatter.35.cloned.1.call-update) | async-done | bytes 1048592 | tf_op jit(solution)/shard_map/reduce_scatter | solution.py:257
  1623.2 179.4 %reduce-scatter.33.cloned.1.call-done = bf16[64,8192]{1,0:T(8,128)(2,1)} async-done(((bf16[1024,8192]{1,0:T(8,128)(2,1)}), bf16[64,8192]{1,0:T(8,128)(2,1)}) %reduce-scatter.33.cloned.1.call-update) | async-done | bytes 1048592 | tf_op jit(solution)/shard_map/reduce_scatter | solution.py:254
  1805.3 179.6 %reduce-scatter.31.cloned.1.call-done = bf16[64,8192]{1,0:T(8,128)(2,1)} async-done(((bf16[1024,8192]{1,0:T(8,128)(2,1)}), bf16[64,8192]{1,0:T(8,128)(2,1)}) %reduce-scatter.31.cloned.1.call-update) | async-done | bytes 1048592 | tf_op jit(solution)/shard_map/reduce_scatter | solution.py:251
  (283 shorter events, 323.8 us)
Async XLA Ops:
  7.2 76.9 %copy-start.32 = (s32[1024]{0:T(1024)S(1)}, s32[1024]{0:T(1024)}, u32[]{:S(2)}) copy-start(s32[1024]{0:T(1024)} %param.20) | copy-start | bytes 12292
  7.2 77.0 %copy-start.45 = (bf16[64,256]{1,0:T(8,128)(2,1)S(1)}, bf16[64,256]{1,0:T(8,128)(2,1)}, u32[]{:S(2)}) copy-start(bf16[64,256]{1,0:T(8,128)(2,1)} %param.25) | copy-start | bytes 98308
  7.2 95.7 %copy-start.46 = (bf16[64,256]{1,0:T(8,128)(2,1)S(1)}, bf16[64,256]{1,0:T(8,128)(2,1)}, u32[]{:S(2)}) copy-start(bf16[64,256]{1,0:T(8,128)(2,1)} %param.26) | copy-start | bytes 98308
  7.2 116.7 %all-gather.13.cloned.1.call-start = ((), (), s32[]{:S(2)}) async-start(), calls=%async_computation.13 | async-start | bytes 1114112 | tf_op jit(solution)/shard_map/all_gather | solution.py:79
  7.9 115.9 %all-gather.11.cloned.1.call-start = ((), (), s32[]{:S(2)}) async-start(), calls=%async_computation.12 | async-start | bytes 3145728 | tf_op jit(solution)/shard_map/all_gather | solution.py:90
  83.3 88.8 %all-gather.15.cloned.1.call-start = ((), (), s32[]{:S(2)}) async-start(), calls=%async_computation.14 | async-start | bytes 1114112 | tf_op jit(solution)/shard_map/all_gather | solution.py:82
  84.0 144.1 %reduce-scatter.15.cloned.1.call-start = ((), (), s32[]{:S(2)}) async-start(), calls=%async_computation.15 | async-start | bytes 6291456 | tf_op jit(solution)/shard_map/reduce_scatter | solution.py:116
  177.6 85.2 %all-gather.25.cloned.1.call-start = ((), (), s32[]{:S(2)}) async-start(), calls=%async_computation.21 | async-start | bytes 3145728 | tf_op jit(solution)/shard_map/all_gather | solution.py:141
  178.2 119.8 %all-gather.17.cloned.1.call-start = ((), (), s32[]{:S(2)}) async-start(), calls=%async_computation.16 | async-start | bytes 3145728 | tf_op jit(solution)/shard_map/all_gather | solution.py:121
  232.6 194.6 %all-gather.19.cloned.1.call-start = ((), (), s32[]{:S(2)}) async-start(), calls=%async_computation.17 | async-start | bytes 17825792 | tf_op jit(solution)/shard_map/all_gather | solution.py:52
  233.4 321.4 %all-gather.21.cloned.1.call-start = ((), (), s32[]{:S(2)}) async-start(), calls=%async_computation.18 | async-start | bytes 17825792 | tf_op jit(solution)/shard_map/all_gather | solution.py:53
  234.1 448.1 %all-gather.23.cloned.1.call-start = ((), (), s32[]{:S(2)}) async-start(), calls=%async_computation.19 | async-start | bytes 17825792 | tf_op jit(solution)/shard_map/all_gather | solution.py:54
  234.9 620.7 %reduce-scatter.19.cloned.1.call-start = ((), (), s32[]{:S(2)}) async-start(), calls=%async_computation.22 | async-start | bytes 6291456 | tf_op jit(solution)/shard_map/reduce_scatter | solution.py:175
  235.0 469.6 %copy-start.30 = (f32[16,256]{1,0:T(8,128)}, f32[16,256]{1,0:T(8,128)S(1)}, u32[]{:S(2)}) copy-start(f32[16,256]{1,0:T(8,128)S(1)} %select_bitcast_fusion) | copy-start | bytes 49156
  764.2 91.4 %copy-start.4 = (f32[512,1024]{1,0:T(8,128)S(1)}, f32[512,1024]{1,0:T(8,128)}, u32[]{:S(2)}) copy-start(f32[512,1024]{1,0:T(8,128)} %copy-done.3) | copy-start | bytes 6291460
  764.2 91.4 %copy-start.38 = (f32[1,1024]{1,0:T(1,128)S(1)}, f32[1,1024]{1,0:T(1,128)}, u32[]{:S(2)}) copy-start(f32[1,1024]{1,0:T(1,128)} %get-tuple-element.287) | copy-start | bytes 12292
  764.2 91.4 %copy-start.43 = (f32[512]{0:T(512)S(1)}, f32[512]{0:T(512)}, u32[]{:S(2)}) copy-start(f32[512]{0:T(512)} %copy-done.42) | copy-start | bytes 6148
  803.0 91.1 %all-gather.27.cloned.1.call-start = ((), (), s32[]{:S(2)}) async-start(), calls=%async_computation.23 | async-start | bytes 3145728 | tf_op jit(solution)/shard_map/all_gather | solution.py:178
  860.8 213.6 %reduce-scatter.21.cloned.1.call-start = ((), (), s32[]{:S(2)}) async-start(), calls=%async_computation.24 | async-start | bytes 3145728 | tf_op jit(solution)/shard_map/reduce_scatter | solution.py:223
  999.7 178.1 %reduce-scatter.25.cloned.1.call-start = ((), (), s32[]{:S(2)}) async-start(), calls=%async_computation.26 | async-start | bytes 557056 | tf_op jit(solution)/shard_map/reduce_scatter | solution.py:242
  1002.9 176.4 %reduce-scatter.27.cloned.1.call-start = ((), (), s32[]{:S(2)}) async-start(), calls=%async_computation.27 | async-start | bytes 557056 | tf_op jit(solution)/shard_map/reduce_scatter | solution.py:245
  1006.2 204.4 %reduce-scatter.29.cloned.1.call-start = ((), (), s32[]{:S(2)}) async-start(), calls=%async_computation.28 | async-start | bytes 1114112 | tf_op jit(solution)/shard_map/reduce_scatter | solution.py:248
  1010.2 260.9 %reduce-scatter.23.cloned.1.call-start = ((), (), s32[]{:S(2)}) async-start(), calls=%async_computation.25 | async-start | bytes 1114112 | tf_op jit(solution)/shard_map/reduce_scatter | solution.py:239
  1014.2 290.6 %reduce-scatter.17.cloned.1.call-start = ((), (), s32[]{:S(2)}) async-start(), calls=%async_computation.20 | async-start | bytes 3145728 | tf_op jit(solution)/shard_map/reduce_scatter | solution.py:137
  1074.4 366.9 %reduce-scatter.37.cloned.1.call-start = ((), (), s32[]{:S(2)}) async-start(), calls=%async_computation.32 | async-start | bytes 540672
  1077.7 542.9 %reduce-scatter.35.cloned.1.call-start = ((), (), s32[]{:S(2)}) async-start(), calls=%async_computation.31 | async-start | bytes 17825792 | tf_op jit(solution)/shard_map/reduce_scatter | solution.py:257
  1110.5 692.1 %reduce-scatter.33.cloned.1.call-start = ((), (), s32[]{:S(2)}) async-start(), calls=%async_computation.30 | async-start | bytes 17825792 | tf_op jit(solution)/shard_map/reduce_scatter | solution.py:254
  1144.2 840.8 %reduce-scatter.31.cloned.1.call-start = ((), (), s32[]{:S(2)}) async-start(), calls=%async_computation.29 | async-start | bytes 17825792 | tf_op jit(solution)/shard_map/reduce_scatter | solution.py:251
  1177.7 127.0 %copy-start.5 = (f32[512,1024]{1,0:T(8,128)S(1)}, f32[512,1024]{1,0:T(8,128)}, u32[]{:S(2)}) copy-start(f32[512,1024]{1,0:T(8,128)} %copy-done.3) | copy-start | bytes 6291460
  1177.8 127.0 %copy-start.39 = (f32[1,1024]{1,0:T(1,128)S(1)}, f32[1,1024]{1,0:T(1,128)}, u32[]{:S(2)}) copy-start(f32[1,1024]{1,0:T(1,128)} %get-tuple-element.287) | copy-start | bytes 12292
  1177.8 127.0 %copy-start.44 = (f32[512]{0:T(512)S(1)}, f32[512]{0:T(512)}, u32[]{:S(2)}) copy-start(f32[512]{0:T(512)} %copy-done.42) | copy-start | bytes 6148
  1177.8 127.0 %copy-start.50 = (f32[512]{0:T(512)S(1)}, f32[512]{0:T(512)}, u32[]{:S(2)}) copy-start(f32[512]{0:T(512)} %copy-done.49) | copy-start | bytes 6148
  (53 other events, 401.3 us)
Sparse Core Ops, SparseCore 0:
  10.2 40.5 all-gather.12
  83.4 28.9 all-gather.10
  114.6 37.9 all-gather.14
  177.7 50.4 reduce-scatter.14
  229.6 33.0 all-gather.24
  264.8 33.1 all-gather.16
  300.3 126.8 all-gather.18
  429.6 125.0 all-gather.20
  557.1 125.0 all-gather.22
  803.1 52.4 reduce-scatter.18
  860.9 33.1 all-gather.26
  999.8 31.8 reduce-scatter.20
  1035.6 55.7 reduce-scatter.24
  1094.9 54.8 reduce-scatter.26
  1154.2 56.4 reduce-scatter.28
  1214.7 56.3 reduce-scatter.22
  1273.9 30.8 reduce-scatter.16
  1307.4 133.8 reduce-scatter.36
  1446.0 174.4 reduce-scatter.34
  1625.0 177.5 reduce-scatter.32
  1807.3 177.5 reduce-scatter.30
where the time goes:
time: 2010 us; the launch traced here: 1990 us
  waiting for transfers between devices  1250 us (62%)
  matrix products  253 us (13%)
  local copies, waits for them, and re-layouts  211 us (10%)
  other arithmetic  155 us (8%)
  blocking collectives  110 us (5%)
    reduce_scatter x1, waiting for transfers between devices, body(): lax.psum_scatter(grad_gate.astype(jnp.bfloat16), 'fsdp', scatter_dimensio...  180 us
    reduce_scatter x1, waiting for transfers between devices, body(): lax.psum_scatter(grad_up.astype(jnp.bfloat16), 'fsdp', scatter_dimension=...  179 us
    reduce_scatter x1, waiting for transfers between devices, body(): lax.psum_scatter(grad_down.astype(jnp.bfloat16), 'fsdp', scatter_dimensio...  178 us
    unnamed x22, waiting for transfers between devices  136 us
    all_gather x1, waiting for transfers between devices, expert_matrices(): lax.all_gather(w_up, 'fsdp', axis=0, tiled=True)  105 us
    all_gather x1, waiting for transfers between devices, expert_matrices(): lax.all_gather(w_gate, 'fsdp', axis=0, tiled=True)  94.8 us
    all_gather x1, waiting for transfers between devices, expert_matrices(): lax.all_gather(w_down, 'fsdp', axis=0, tiled=True)  79.4 us
    all_gather x1, blocking collectives, body(): all_gains = lax.all_gather(gains, ('fsdp', 'tp'), axis=1, tiled=True)  70 us
  transfers between devices with their start and end apart: 21, of which 15 were waited for; matrix products, arithmetic and copies ran while one was open for 19% of the time, Pallas kernels for 0%

commit v1 on v0

v1 whole, which is shorter than its diff:
```python
import functools

import jax
import jax.numpy as jnp
from jax import lax
from jax.experimental import pallas as pl
from jax.experimental.pallas import tpu as pltpu
from jax.sharding import PartitionSpec as P

HEAD_DIM = 64
FF = 512
EPS = 1e-06
SUB = 4
TILE = 256
NEG = -1e30
VMEM_BYTES = 56 * 1024 * 1024
BF = jnp.bfloat16
F32 = jnp.float32


def params(*semantics):
    return pltpu.CompilerParams(
        vmem_limit_bytes=VMEM_BYTES, dimension_semantics=semantics or None
    )


def cost(flops, moved, exps=0):
    return pl.CostEstimate(flops=int(flops), bytes_accessed=int(moved), transcendentals=int(exps))


def dot(left, right, left_dim=1, right_dim=0):
    return lax.dot_general(
        left, right, (((left_dim,), (right_dim,)), ((), ())), preferred_element_type=F32
    )


def fill_bias(bias, seg_row, seg_col):
    length = bias.shape[0]

    @pl.when(pl.program_id(0) == 0)
    def _():
        for start in range(0, length, TILE):
            depth = start + TILE
            key_pos = lax.broadcasted_iota(jnp.int32, (depth, TILE), 0)
            query_pos = lax.broadcasted_iota(jnp.int32, (depth, TILE), 1) + start
            allowed = (query_pos >= key_pos) & (
                seg_col[:depth, :] == seg_row[:, start : start + TILE]
            )
            bias[:depth, start : start + TILE] = jnp.where(allowed, 0.0, NEG)


def attend_kernel(group, qkv_ref, seg_row, seg_col, out_ref, log_ref, bias):
    fill_bias(bias, seg_row, seg_col)
    length = bias.shape[0]
    wide = group * HEAD_DIM
    keys = qkv_ref[wide : wide + HEAD_DIM, :].T
    for head in range(group):
        rows = slice(head * HEAD_DIM, (head + 1) * HEAD_DIM)
        for start in range(0, length, TILE):
            depth = start + TILE
            cols = slice(start, depth)
            query = qkv_ref[rows, cols] * jnp.asarray(HEAD_DIM**-0.5, BF)
            scores = dot(keys[:depth], query) + bias[:depth, cols]
            top = jnp.max(scores, axis=0, keepdims=True)
            expo = jnp.exp(scores - top)
            total = jnp.sum(expo, axis=0, keepdims=True)
            mixed = dot(qkv_ref[wide + HEAD_DIM : wide + 2 * HEAD_DIM, :depth], expo.astype(BF))
            out_ref[rows, cols] = (mixed / total).astype(BF)
            log_ref[0, head : head + 1, cols] = top + jnp.log(total)


def attend(qkv, segments, heads_kv, group):
    length = qkv.shape[1]
    wide = (group + 2) * HEAD_DIM
    return pl.pallas_call(
        functools.partial(attend_kernel, group),
        grid=(heads_kv,),
        in_specs=[
            pl.BlockSpec((wide, length), lambda h: (h, 0)),
            pl.BlockSpec((1, length), lambda h: (0, 0)),
            pl.BlockSpec((length, 1), lambda h: (0, 0)),
        ],
        out_specs=[
            pl.BlockSpec((group * HEAD_DIM, length), lambda h: (h, 0)),
            pl.BlockSpec((1, group, length), lambda h: (h, 0, 0)),
        ],
        out_shape=[
            jax.ShapeDtypeStruct((heads_kv * group * HEAD_DIM, length), BF),
            jax.ShapeDtypeStruct((heads_kv, group, length), F32),
        ],
        scratch_shapes=[pltpu.VMEM((length, length), F32)],
        compiler_params=params("arbitrary"),
        cost_estimate=cost(
            heads_kv * group * length * length * HEAD_DIM * 12,
            4 * qkv.size,
            heads_kv * group * length * length,
        ),
        name="attend",
    )(qkv, segments.reshape(1, -1), segments.reshape(-1, 1))


def attend_back_kernel(
    group, qkv_ref, grad_ref, out_ref, log_ref, seg_row, seg_col, back_ref, bias, key_sum, value_sum
):
    fill_bias(bias, seg_row, seg_col)
    length = bias.shape[0]
    wide = group * HEAD_DIM
    scale = HEAD_DIM**-0.5
    keys_t = qkv_ref[wide : wide + HEAD_DIM, :]
    keys = keys_t.T
    values = qkv_ref[wide + HEAD_DIM : wide + 2 * HEAD_DIM, :].T
    key_sum[...] = jnp.zeros_like(key_sum)
    value_sum[...] = jnp.zeros_like(value_sum)
    for head in range(group):
        rows = slice(head * HEAD_DIM, (head + 1) * HEAD_DIM)
        for start in range(0, length, TILE):
            depth = start + TILE
            cols = slice(start, depth)
            query_t = qkv_ref[rows, cols] * jnp.asarray(scale, BF)
            grad_t = grad_ref[rows, cols]
            centre = jnp.sum(
                grad_t.astype(F32) * out_ref[rows, cols].astype(F32), axis=0, keepdims=True
            )
            scores = dot(keys[:depth], query_t) + bias[:depth, cols]
            prob = jnp.exp(scores - log_ref[0, head : head + 1, cols])
            prob_grad = dot(values[:depth], grad_t)
            score_grad = (prob * (prob_grad - centre)).astype(BF)
            back_ref[rows, cols] = (dot(keys_t[:, :depth], score_grad) * scale).astype(BF)
            key_sum[:depth, :] += dot(score_grad, query_t.T)
            value_sum[:depth, :] += dot(prob.astype(BF), grad_t.T)
    back_ref[wide : wide + HEAD_DIM, :] = key_sum[...].T.astype(BF)
    back_ref[wide + HEAD_DIM : wide + 2 * HEAD_DIM, :] = value_sum[...].T.astype(BF)


def attend_back(qkv, grads, attended, logs, segments, heads_kv, group):
    length = qkv.shape[1]
    wide = (group + 2) * HEAD_DIM
    head_block = pl.BlockSpec((group * HEAD_DIM, length), lambda h: (h, 0))
    return pl.pallas_call(
        functools.partial(attend_back_kernel, group),
        grid=(heads_kv,),
        in_specs=[
            pl.BlockSpec((wide, length), lambda h: (h, 0)),
            head_block,
            head_block,
            pl.BlockSpec((1, group, length), lambda h: (h, 0, 0)),
            pl.BlockSpec((1, length), lambda h: (0, 0)),
            pl.BlockSpec((length, 1), lambda h: (0, 0)),
        ],
        out_specs=pl.BlockSpec((wide, length), lambda h: (h, 0)),
        out_shape=jax.ShapeDtypeStruct(qkv.shape, BF),
        scratch_shapes=[
            pltpu.VMEM((length, length), F32),
            pltpu.VMEM((length, HEAD_DIM), F32),
            pltpu.VMEM((length, HEAD_DIM), F32),
        ],
        compiler_params=params("arbitrary"),
        cost_estimate=cost(
            heads_kv * group * length * length * HEAD_DIM * 30,
            8 * qkv.size,
            heads_kv * group * length * length,
        ),
        name="attend_back",
    )(qkv, grads, attended, logs, segments.reshape(1, -1), segments.reshape(-1, 1))


def pick_kernel(index_ref, weight_ref, table_ref, out_ref):
    width = table_ref.shape[0]
    marks = lax.broadcasted_iota(jnp.int32, (index_ref.shape[0], width), 1) == index_ref[...]
    picked = dot(marks.astype(BF), table_ref[...])
    if weight_ref is not None:
        picked = picked * weight_ref[...]
    out_ref[0] = picked.astype(BF)


def pick_plain_kernel(index_ref, table_ref, out_ref):
    pick_kernel(index_ref, None, table_ref, out_ref)


def pick(table, index_col, weight_col, experts):
    cap = index_col.shape[0] // experts
    length, width = table.shape
    column = pl.BlockSpec((cap, 1), lambda e: (e, 0))
    weighted = weight_col is not None
    return pl.pallas_call(
        pick_kernel if weighted else pick_plain_kernel,
        grid=(experts,),
        in_specs=[column] * (2 if weighted else 1)
        + [pl.BlockSpec((length, width), lambda e: (0, 0))],
        out_specs=pl.BlockSpec((1, cap, width), lambda e: (e, 0, 0)),
        out_shape=jax.ShapeDtypeStruct((experts, cap, width), BF),
        compiler_params=params("arbitrary"),
        cost_estimate=cost(
            2 * experts * cap * length * width, 2 * (length + experts * cap) * width
        ),
        name="pick_rows",
    )(*((index_col, weight_col) if weighted else (index_col,)), table)


def put_kernel(experts, index_ref, *refs):
    parts, out_ref = refs[:experts], refs[experts]
    cap = parts[0].shape[1]
    first = pl.program_id(0) * out_ref.shape[0]
    total = None
    for expert in range(experts):
        index = index_ref[:, expert * cap : (expert + 1) * cap]
        marks = lax.broadcasted_iota(jnp.int32, (out_ref.shape[0], cap), 0) + first == index
        part = dot(marks.astype(BF), parts[expert][0])
        total = part if total is None else total + part
    out_ref[...] = total.astype(BF)


def put(parts, index_row, which, length):
    experts = len(parts)
    cap, width = parts[0].shape[1:]
    return pl.pallas_call(
        functools.partial(put_kernel, experts),
        grid=(length // TILE,),
        in_specs=[pl.BlockSpec((1, experts * cap), lambda r: (0, 0))]
        + [pl.BlockSpec((1, cap, width), lambda r: (which, 0, 0))] * experts,
        out_specs=pl.BlockSpec((TILE, width), lambda r: (r, 0)),
        out_shape=jax.ShapeDtypeStruct((length, width), BF),
        compiler_params=params("arbitrary"),
        cost_estimate=cost(
            2 * experts * cap * length * width, 2 * (length + experts * cap) * width
        ),
        name="put_rows",
    )(index_row, *parts)


def expert_kernel(expert, blocks, at_ref, weight_ref, *refs):
    picks, grads, shards = refs[:SUB], refs[SUB : 2 * SUB], refs[2 * SUB : 2 * SUB + blocks]
    refs = refs[2 * SUB + blocks :]
    slot_out, pick_grad, backs = refs[0], refs[1], refs[2 : 2 + blocks]
    picked, slot_grad, gate_w, up_w, down_w, acts, hid_grads, sems = refs[2 + blocks :]
    cap = slot_out.shape[1]
    deep = shards[0].shape[1]
    copies = []
    for k in range(SUB):
        rows = pl.ds(k * cap, cap)
        copies.append(pltpu.make_async_copy(picks[k].at[expert], picked.at[rows], sems.at[2 * k]))
        copies.append(
            pltpu.make_async_copy(grads[k].at[expert], slot_grad.at[rows], sems.at[2 * k + 1])
        )
    for copy in copies:
        copy.start()
    offsets = []
    for r in range(blocks):
        offset = pl.multiple_of(lax.rem(at_ref[0] + r, blocks) * deep, deep)
        offsets.append(offset)
        for held, which in ((gate_w, 0), (up_w, 1), (down_w, 2)):
            held[pl.ds(offset, deep), :] = shards[r][which]
    for copy in copies:
        copy.wait()

    def one(k, carry):
        rows = pl.ds(pl.multiple_of(k * cap, cap), cap)
        weight = weight_ref[rows, :]
        gate_pre = dot(picked[rows, :], gate_w[...])
        up_pre = dot(picked[rows, :], up_w[...])
        sig = 1.0 / (1.0 + jnp.exp(-gate_pre))
        silu = gate_pre * sig
        act = (silu * up_pre).astype(BF)
        acts[rows, :] = act
        slot_out[k] = (dot(act, down_w[...], 1, 1) * weight).astype(BF)
        inner = dot(slot_grad[rows, :], down_w[...])
        gate_grad = (inner * up_pre * sig * (1.0 + gate_pre * (1.0 - sig))).astype(BF)
        up_grad = (inner * silu).astype(BF)
        hid_grads[rows, :FF] = gate_grad
        hid_grads[rows, FF:] = up_grad
        pick_grad[k] = (dot(gate_grad, gate_w[...], 1, 1) + dot(up_grad, up_w[...], 1, 1)).astype(
            BF
        )
        return carry

    lax.fori_loop(0, SUB, one, 0)
    for r in range(blocks):
        cols = pl.ds(offsets[r], deep)
        both = dot(picked[:, cols], hid_grads[...], 0, 0)
        backs[r][0] = both[:, :FF].astype(BF)
        backs[r][1] = both[:, FF:].astype(BF)
        backs[r][2] = dot(slot_grad[:, cols], acts[...], 0, 0).astype(BF)


def run_expert(expert, at, weight_col, picks, grads, shards):
    blocks = len(shards)
    cap, width = picks[0].shape[1:]
    slots = SUB * cap
    whole = pl.BlockSpec(memory_space=pltpu.VMEM)
    return pl.pallas_call(
        functools.partial(expert_kernel, expert, blocks),
        in_specs=[pl.BlockSpec(memory_space=pltpu.SMEM), whole]
        + [pl.BlockSpec(memory_space=pl.ANY)] * (2 * SUB)
        + [whole] * blocks,
        out_specs=[whole] * (2 + blocks),
        out_shape=[jax.ShapeDtypeStruct((SUB, cap, width), BF)] * 2
        + [jax.ShapeDtypeStruct(shards[0].shape, BF)] * blocks,
        scratch_shapes=[
            pltpu.VMEM((slots, width), BF),
            pltpu.VMEM((slots, width), BF),
            pltpu.VMEM((width, FF), BF),
            pltpu.VMEM((width, FF), BF),
            pltpu.VMEM((width, FF), BF),
            pltpu.VMEM((slots, FF), BF),
            pltpu.VMEM((slots, 2 * FF), BF),
            pltpu.SemaphoreType.DMA((2 * SUB,)),
        ],
        compiler_params=params(),
        cost_estimate=cost(18 * slots * width * FF, 8 * slots * width + 12 * width * FF),
        name="expert",
    )(at, weight_col, *picks, *grads, *shards)


def norm_scale(values):
    return lax.rsqrt(jnp.mean(values * values, axis=-1, keepdims=True) + EPS)


def norm_backward(values, rms_scale, gain_row, gradient):
    weighted = gradient * gain_row
    centre = jnp.mean(weighted * values, axis=-1, keepdims=True)
    back_values = rms_scale * weighted - values * rms_scale * rms_scale * rms_scale * centre
    return (back_values, jnp.sum(gradient * values * rms_scale, axis=0))


def layer(
    fsdp,
    tp,
    tokens,
    segments,
    slots,
    gate_values,
    gains,
    w_query,
    w_key,
    w_value,
    w_out,
    w_gate,
    w_up,
    w_down,
    cotangent,
):
    length, width = segments.shape[0], tokens.shape[1]
    half = tokens.shape[0]
    planes = fsdp // SUB
    at_fsdp, at_tp = lax.axis_index("fsdp"), lax.axis_index("tp")
    sub, plane = at_fsdp % SUB, at_fsdp // SUB
    heads_kv = w_key.shape[1] // HEAD_DIM
    group = w_query.shape[1] // w_key.shape[1]
    experts = slots.shape[1] // SUB
    cap = slots.shape[2]

    def swap(values, mask, axis="fsdp"):
        size = fsdp if axis == "fsdp" else tp
        return lax.ppermute(values, axis, [(i, i ^ mask) for i in range(size)])

    def shift(values, planes_on):
        return lax.ppermute(
            values, "fsdp", [(i, (i + planes_on * SUB) % fsdp) for i in range(fsdp)]
        )

    def by_sub(pieces):
        near = [jnp.where((sub & 1) == 1, pieces[k ^ 1], pieces[k]) for k in range(SUB)]
        return [jnp.where((sub & 2) == 2, near[k ^ 2], near[k]) for k in range(SUB)]

    def ordered(mine, other):
        return jnp.where(
            at_tp == 0, jnp.concatenate([mine, other]), jnp.concatenate([other, mine])
        )

    def sequence_gather(mine):
        if tp == 2:
            return ordered(mine, swap(mine, 1, "tp"))
        return lax.all_gather(mine, "tp", axis=0, tiled=True)

    def part_of(values, which):
        return lax.dynamic_slice_in_dim(values, which * half, half, 0)

    def sequence_scatter(values):
        if tp == 2:
            other = swap(part_of(values, 1 - at_tp).astype(BF), 1, "tp")
            return part_of(values, at_tp) + other.astype(F32)
        return lax.psum_scatter(values, "tp", scatter_dimension=0, tiled=True)

    def plane_gather(mine):
        if tp == 2:
            beside, across = swap(mine, 1, "tp"), swap(mine, 2)
            corner = swap(beside, 2)
            first, third = ordered(mine, beside), ordered(across, corner)
        else:
            first = lax.all_gather(mine, "tp", axis=0, tiled=True)
            third = swap(first, 2)
        return [first, swap(first, 1), third, swap(third, 1)]

    def plane_scatter(put_one):
        second, fourth = put_one(1), put_one(3)
        second, fourth = swap(second, 1), swap(fourth, 1)
        third = put_one(2).astype(F32) + fourth.astype(F32)
        if tp == 2:
            corner = swap(part_of(third, 1 - at_tp).astype(BF), 2)
            across = swap(part_of(third, at_tp).astype(BF), 2)
            first = put_one(0).astype(F32) + second.astype(F32)
            beside = part_of(first, 1 - at_tp) + corner.astype(F32)
            beside = swap(beside.astype(BF), 1, "tp")
            return part_of(first, at_tp) + across.astype(F32) + beside.astype(F32)
        first = put_one(0).astype(F32) + second.astype(F32)
        first = first + swap(third.astype(BF), 2).astype(F32)
        return lax.psum_scatter(first, "tp", scatter_dimension=0, tiled=True)

    all_gains = gains
    for axis, size, at in (("tp", tp, at_tp), ("fsdp", fsdp, at_fsdp)):
        mask = 1
        while mask < size:
            other = swap(all_gains, mask, axis)
            all_gains = jnp.where(
                (at & mask) != 0,
                jnp.concatenate([other, all_gains], axis=1),
                jnp.concatenate([all_gains, other], axis=1),
            )
            mask *= 2

    rows = w_query.shape[0]
    packed = jnp.concatenate(
        [
            w_query.reshape(rows, heads_kv, group * HEAD_DIM),
            w_key.reshape(rows, heads_kv, HEAD_DIM),
            w_value.reshape(rows, heads_kv, HEAD_DIM),
        ],
        axis=2,
    ).reshape(rows, -1)
    qkv_cols = packed.shape[1]
    attn_w = lax.all_gather(
        jnp.concatenate([packed, w_out], axis=1), "fsdp", axis=0, tiled=True
    )
    qkv_w, out_w = attn_w[:, :qkv_cols], attn_w[:, qkv_cols:]

    live = slots[0] >= 0
    table = jnp.stack([slots[0].astype(F32), jnp.where(live, gate_values[0], 0.0)])

    def table_for(k):
        return lax.dynamic_slice_in_dim(table, (sub ^ k) * experts, experts, 1)

    tables = [table_for(0)] + [swap(table_for(k), k) for k in range(1, SUB)]
    index = [t[0].astype(jnp.int32) for t in tables]
    index_col = [v.reshape(-1, 1) for v in index]
    index_row = [v.reshape(1, -1) for v in index]
    slot_weight = [t[1] for t in tables]

    def shards_of(expert):
        def piece(k):
            column = ((sub ^ k) * experts + expert) * FF
            return jnp.stack(
                [lax.dynamic_slice_in_dim(w, column, FF, 1) for w in (w_gate, w_up, w_down)]
            )

        pieces = [piece(0)] + [swap(piece(k), k) for k in range(1, SUB)]
        mine = jnp.concatenate(by_sub(pieces), axis=1)
        return [mine] + [shift(mine, -r) for r in range(1, planes)]

    shards = [shards_of(expert) for expert in range(experts)]

    whole_tokens = sequence_gather(tokens).astype(F32)
    first_low = (whole_tokens * norm_scale(whole_tokens) * all_gains[0]).astype(BF)
    qkv = dot(qkv_w, first_low, 0, 1).astype(BF)
    attended, logs = attend(qkv, segments, heads_kv, group)
    resid = tokens.astype(F32)
    hidden = resid + sequence_scatter(dot(attended, out_w, 0, 1))
    scale_two = norm_scale(hidden)
    second_low = (hidden * scale_two * all_gains[1]).astype(BF)

    cots = plane_gather(cotangent)
    slot_grads = [
        pick(cots[k], index_col[k], slot_weight[k].reshape(-1, 1), experts) for k in range(SUB)
    ]
    seconds = plane_gather(second_low)
    picks = [pick(seconds[k], index_col[k], None, experts) for k in range(SUB)]
    at = plane.astype(jnp.int32).reshape(1)
    slot_outs, pick_grads, sums = [], [], []
    for expert in range(experts):
        weight_col = jnp.stack([w[expert] for w in slot_weight]).reshape(-1, 1)
        slot_out, pick_grad, *backs = run_expert(
            expert, at, weight_col, picks, slot_grads, shards[expert]
        )
        slot_outs.append(slot_out)
        pick_grads.append(pick_grad)
        total = backs[0].astype(F32)
        for r in range(1, planes):
            total = total + shift(backs[r], r).astype(F32)
        own_rows = w_gate.shape[0]
        total = total.reshape(3, SUB, own_rows, FF)

        def rows_for(k):
            return lax.dynamic_index_in_dim(total, sub ^ k, 1, keepdims=False)

        pieces = [rows_for(0)] + [
            swap(rows_for(k).astype(BF), k).astype(F32) for k in range(1, SUB)
        ]
        sums.append(by_sub(pieces))
    expert_grads = [
        jnp.concatenate(
            [sums[expert][owner][which] for owner in range(SUB) for expert in range(experts)],
            axis=1,
        )
        for which in range(3)
    ]
    second_grad = plane_scatter(lambda k: put(pick_grads, index_row[k], k, length))
    expert_sum = plane_scatter(lambda k: put(slot_outs, index_row[k], k, length))
    mixed = (hidden + expert_sum).astype(BF)

    back_two, second_gain = norm_backward(hidden, scale_two, all_gains[1], second_grad)
    grad_hidden = cotangent.astype(F32) + back_two
    hidden_low = sequence_gather(grad_hidden.astype(BF))
    grad_out = dot(hidden_low, attended, 0, 1).astype(BF)
    attended_grad = dot(out_w, hidden_low, 0, 1).astype(BF)
    qkv_grad = attend_back(qkv, attended_grad, attended, logs, segments, heads_kv, group)
    grad_qkv = dot(first_low, qkv_grad, 0, 1).astype(BF)
    first_grad = sequence_scatter(dot(qkv_grad, qkv_w, 0, 1))
    back_one, first_gain = norm_backward(resid, norm_scale(resid), all_gains[0], first_grad)
    grad_tokens = grad_hidden + back_one

    grad_gains = jnp.stack([first_gain, second_gain])
    for axis, size, at_axis in (("fsdp", fsdp, at_fsdp), ("tp", tp, at_tp)):
        mask = size // 2
        while mask:
            low, high = jnp.split(grad_gains, 2, axis=1)
            upper = (at_axis & mask) != 0
            kept, sent = jnp.where(upper, high, low), jnp.where(upper, low, high)
            grad_gains = kept + swap(sent, mask, axis)
            mask //= 2

    grad_out = lax.psum_scatter(grad_out, "fsdp", scatter_dimension=0, tiled=True).astype(F32)
    grad_qkv = lax.psum_scatter(grad_qkv, "fsdp", scatter_dimension=0, tiled=True).astype(F32)
    grad_qkv = grad_qkv.reshape(rows, heads_kv, -1)
    cut = group * HEAD_DIM
    return (
        mixed,
        grad_tokens,
        grad_gains,
        grad_qkv[:, :, :cut].reshape(rows, -1),
        grad_qkv[:, :, cut : cut + HEAD_DIM].reshape(rows, -1),
        grad_qkv[:, :, cut + HEAD_DIM :].reshape(rows, -1),
        grad_out,
        *expert_grads,
    )


def solution(mesh):
    both, split = P(("fsdp", "tp"), None), P("fsdp", "tp")
    experts, feature = P("fsdp", "tp", None), P(None, ("fsdp", "tp"))
    return jax.shard_map(
        functools.partial(layer, mesh.shape["fsdp"], mesh.shape["tp"]),
        mesh=mesh,
        in_specs=(both, P("fsdp"), experts, experts, feature) + (split,) * 7 + (both,),
        out_specs=(both, both, feature) + (split,) * 7,
        check_vma=False,
    )
```

time: 2010 us -> 1080 us (0.54)
  waiting for transfers between devices: 1250 us -> 560 us
  matrix products: 253 us -> 25.3 us
  Pallas kernels: 0 us -> 197 us
  local copies, waits for them, and re-layouts: 211 us -> 46.6 us
  starting transfers between devices: 1.79 us -> 161 us
  blocking collectives: 110 us -> 0 us
  other arithmetic: 155 us -> 64 us
    reduce_scatter x11 -> x2, waiting for transfers between devices: 760 us -> 63.4 us  [the longest x1 63.2 us: layer(): lax.psum_scatter(grad_qkv, 'fsdp', scatter_dimension=0, tiled=True)]
    ppermute x0 -> x85, waiting for transfers between devices: none -> 495 us  [the longest x24 300 us: shift(): lax.ppermute(values, 'fsdp', [(i, (i + planes_on * SUB) % fsdp) for i in...]
    all_gather x9 -> x1, waiting for transfers between devices: 352 us -> 2.08 us  [layer(): lax.all_gather(jnp.concatenate([packed, w_out], axis=1), 'fsdp', axis=0,...]
    dot_general x35 -> x6, matrix products: 253 us -> 25.3 us  [dot(): lax.dot_general(left, right, (((left_dim,), (right_dim,)), ((), ())), pre...]
    pallas_call x0 -> x22, Pallas kernels: none -> 197 us  [the longest x4 67.2 us: run_expert(): pl.pallas_call(functools.partial(expert_kernel, expert, blocks), in_specs...]
    ppermute x0 -> x85, starting transfers between devices: none -> 160 us  [the longest x24 94.8 us: shift(): lax.ppermute(values, 'fsdp', [(i, (i + planes_on * SUB) % fsdp) for i in...]
    unnamed x22 -> x3, waiting for transfers between devices: 136 us -> 0.05 us
    all_gather x3 -> x0, blocking collectives: 110 us -> none  [the longest x1 70 us: body(): all_gains = lax.all_gather(gains, ('fsdp', 'tp'), axis=1, tiled=True)]
  transfers between devices with their start and end apart: 21 -> 88, of which waited for: 15 -> 40; matrix products, arithmetic and copies ran while one was open for 19% -> 11% of each run, Pallas kernels for 0% -> 16%
where the time goes in v1:
time: 1080 us; the launch traced here: 1070 us
  waiting for transfers between devices  560 us (52%)
  Pallas kernels  197 us (18%)
  starting transfers between devices  161 us (15%)
  other arithmetic  64 us (6%)
  local copies, waits for them, and re-layouts  46.6 us (4%)
  matrix products  25.3 us (2%)
  between operations  15.2 us (1%)
    ppermute x24, waiting for transfers between devices, shift(): lax.ppermute(values, 'fsdp', [(i, (i + planes_on * SUB) % fsdp) for i in...  300 us
    ppermute x61, waiting for transfers between devices, swap(): return lax.ppermute(values, axis, [(i, i ^ mask) for i in range(size)])  194 us
    ppermute x24, starting transfers between devices, shift(): lax.ppermute(values, 'fsdp', [(i, (i + planes_on * SUB) % fsdp) for i in...  94.8 us
    pallas_call x4, Pallas kernels, run_expert(): pl.pallas_call(functools.partial(expert_kernel, expert, blocks), in_specs...  67.2 us
    ppermute x61, starting transfers between devices, swap(): return lax.ppermute(values, axis, [(i, i ^ mask) for i in range(size)])  65.6 us
    reduce_scatter x1, waiting for transfers between devices, layer(): lax.psum_scatter(grad_qkv, 'fsdp', scatter_dimension=0, tiled=True)  63.2 us
    pallas_call x8, Pallas kernels, pick(): pl.pallas_call(pick_kernel if weighted else pick_plain_kernel, grid=(expe...  48.6 us
    pallas_call x8, Pallas kernels, put(): pl.pallas_call(functools.partial(put_kernel, experts), grid=(length // TI...  42.6 us
  transfers between devices with their start and end apart: 88, of which 40 were waited for; matrix products, arithmetic and copies ran while one was open for 11% of the time, Pallas kernels for 16%

profile of v1, /device:TPU:0, one launch (start us, length us, event | category | flops | bytes accessed | tf_op | source)
XLA Modules:
  0.0 1068.6 jit_solution(13329716407494106891)
XLA Ops:
  29.9 9.2 collective-permute-done.1
  63.5 7.4 convolution_convert_fusion.1.qkv_ref
  70.8 18.2 %attend.1 = (bf16[512,1024]{1,0:T(8,128)(2,1)}, f32[4,2,1024]{2,1,0:T(2,128)}) custom-call(bf16[1024,1024]{1,0:T(8,128)(2,1)} %convolution_convert_fusion.1.qkv_ref, s32[1,1024]{1,0:T(1,128)} %bitcast.577, s32[1024,1]{1,0:T(8,128)} %copy.23.seg_col), custom_call_target="tpu_custom_call" | custom-call | flops 6442450944 | bytes 4194304 | tf_op jit(solution)/shard_map/attend/pallas_call | solution.py:75
  110.9 8.7 collective-permute-done.6
  156.1 41.5 %collective-permute-done.27 = bf16[3,64,512]{2,1,0:T(8,128)(2,1)S(1)} collective-permute-done((bf16[3,64,512]{2,1,0:T(8,128)(2,1)S(1)}, bf16[3,64,512]{2,1,0:T(8,128)(2,1)S(1)}, u32[]{:S(2)}, u32[]{:S(2)}) %collective-permute-start.27) | collective-permute-done | bytes 196640 | tf_op jit(solution)/shard_map/ppermute | solution.py:354
  217.6 6.5 pick_rows.12.refs_4_
  224.1 6.1 pick_rows.14.refs_6_
  231.1 6.2 pick_rows.13.refs_5_
  238.1 6.1 pick_rows.15.refs_7_
  271.6 15.1 %collective-permute-done.42.refs_10_ = bf16[3,256,512]{2,1,0:T(8,128)(2,1)S(1)} collective-permute-done((bf16[3,256,512]{2,1,0:T(8,128)(2,1)S(1)}, bf16[3,256,512]{2,1,0:T(8,128)(2,1)S(1)}, u32[]{:S(2)}, u32[]{:S(2)}) %collective-permute-start.42) | collective-permute-done | bytes 786464 | tf_op jit(solution)/shard_map/ppermute | solution.py:357
  286.7 35.6 %collective-permute-start.30 = (bf16[3,256,512]{2,1,0:T(8,128)(2,1)S(1)}, bf16[3,256,512]{2,1,0:T(8,128)(2,1)}, u32[]{:S(2)}, u32[]{:S(2)}) collective-permute-start(bf16[3,256,512]{2,1,0:T(8,128)(2,1)S(1)} %copy-done.27), channel_id=1, source_target_pairs={{0,16},{2,18},{4,20},{6,22},{8,24},{10,26},{12,28},{14,30},{16,0},... | collective-permute-start | bytes 2359304 | tf_op jit(solution)/shard_map/ppermute | solution.py:357
  322.3 16.8 %expert.7 = (bf16[4,256,1024]{2,1,0:T(8,128)(2,1)}, bf16[4,256,1024]{2,1,0:T(8,128)(2,1)}, bf16[3,256,512]{2,1,0:T(8,128)(2,1)}, bf16[3,256,512]{2,1,0:T(8,128)(...) custom-call(s32[1]{0:T(128)} %bitcast.3.at_ref, f32[1024,1]{1,0:T(8,128)} %bitcast.539, ...), custom_call_target="tpu_custom_call" | custom-call | flops 9663676416 | bytes 14680064 | tf_op jit(solution)/shard_map/expert/pallas_call | solution.py:290
  339.2 48.3 %collective-permute-done.36.refs_10_ = bf16[3,256,512]{2,1,0:T(8,128)(2,1)} collective-permute-done((bf16[3,256,512]{2,1,0:T(8,128)(2,1)S(1)}, bf16[3,256,512]{2,1,0:T(8,128)(2,1)}, u32[]{:S(2)}, u32[]{:S(2)}) %collective-permute-start.36) | collective-permute-done | bytes 786464 | tf_op jit(solution)/shard_map/ppermute | solution.py:357
  389.4 16.8 %expert.6 = (bf16[4,256,1024]{2,1,0:T(8,128)(2,1)}, bf16[4,256,1024]{2,1,0:T(8,128)(2,1)}, bf16[3,256,512]{2,1,0:T(8,128)(2,1)}, bf16[3,256,512]{2,1,0:T(8,128)(...) custom-call(s32[1]{0:T(128)} %bitcast.3.at_ref, f32[1024,1]{1,0:T(8,128)} %bitcast.537, ...), custom_call_target="tpu_custom_call" | custom-call | flops 9663676416 | bytes 14680064 | tf_op jit(solution)/shard_map/expert/pallas_call | solution.py:290
  406.4 48.6 %collective-permute-done.30.refs_10_ = bf16[3,256,512]{2,1,0:T(8,128)(2,1)} collective-permute-done((bf16[3,256,512]{2,1,0:T(8,128)(2,1)S(1)}, bf16[3,256,512]{2,1,0:T(8,128)(2,1)}, u32[]{:S(2)}, u32[]{:S(2)}) %collective-permute-start.30) | collective-permute-done | bytes 786464 | tf_op jit(solution)/shard_map/ppermute | solution.py:357
  455.0 16.9 %expert.5 = (bf16[4,256,1024]{2,1,0:T(8,128)(2,1)}, bf16[4,256,1024]{2,1,0:T(8,128)(2,1)}, bf16[3,256,512]{2,1,0:T(8,128)(2,1)}, bf16[3,256,512]{2,1,0:T(8,128)(...) custom-call(s32[1]{0:T(128)} %bitcast.3.at_ref, f32[1024,1]{1,0:T(8,128)} %bitcast.536, ...), custom_call_target="tpu_custom_call" | custom-call | flops 9663676416 | bytes 14680064 | tf_op jit(solution)/shard_map/expert/pallas_call | solution.py:290
  471.9 16.3 %collective-permute-done.24.refs_10_ = bf16[3,256,512]{2,1,0:T(8,128)(2,1)S(1)} collective-permute-done((bf16[3,256,512]{2,1,0:T(8,128)(2,1)S(1)}, bf16[3,256,512]{2,1,0:T(8,128)(2,1)S(1)}, u32[]{:S(2)}, u32[]{:S(2)}) %collective-permute-start.24) | collective-permute-done | bytes 786464 | tf_op jit(solution)/shard_map/ppermute | solution.py:357
  489.1 16.8 %expert.4 = (bf16[4,256,1024]{2,1,0:T(8,128)(2,1)}, bf16[4,256,1024]{2,1,0:T(8,128)(2,1)}, bf16[3,256,512]{2,1,0:T(8,128)(2,1)}, bf16[3,256,512]{2,1,0:T(8,128)(...) custom-call(s32[1]{0:T(128)} %bitcast.3.at_ref, f32[1024,1]{1,0:T(8,128)} %bitcast.531, ...), custom_call_target="tpu_custom_call" | custom-call | flops 9663676416 | bytes 14680064 | tf_op jit(solution)/shard_map/expert/pallas_call | solution.py:290
  546.6 57.4 %collective-permute-done.80 = bf16[3,256,512]{2,1,0:T(8,128)(2,1)S(1)} collective-permute-done((bf16[3,256,512]{2,1,0:T(8,128)(2,1)}, bf16[3,256,512]{2,1,0:T(8,128)(2,1)S(1)}, u32[]{:S(2)}, u32[]{:S(2)}) %collective-permute-start.80) | collective-permute-done | bytes 786464 | tf_op jit(solution)/shard_map/ppermute | solution.py:357
  603.9 16.7 %collective-permute-start.67 = (bf16[3,256,512]{2,1,0:T(8,128)(2,1)}, bf16[3,256,512]{2,1,0:T(8,128)(2,1)S(1)}, u32[]{:S(2)}, u32[]{:S(2)}) collective-permute-start(bf16[3,256,512]{2,1,0:T(8,128)(2,1)} %get-tuple-element.51), channel_id=1, source_target_pairs={{0,8},{2,10},{4,12},{6,14},{8,16},{10,18},{12,20},{14,22},{16,24},... | collective-permute-start | bytes 2359304 | tf_op jit(solution)/shard_map/ppermute | solution.py:357
  637.4 35.1 %collective-permute-done.74 = bf16[3,256,512]{2,1,0:T(8,128)(2,1)S(1)} collective-permute-done((bf16[3,256,512]{2,1,0:T(8,128)(2,1)}, bf16[3,256,512]{2,1,0:T(8,128)(2,1)S(1)}, u32[]{:S(2)}, u32[]{:S(2)}) %collective-permute-start.74) | collective-permute-done | bytes 786464 | tf_op jit(solution)/shard_map/ppermute | solution.py:357
  672.5 15.7 %collective-permute-start.61 = (bf16[3,256,512]{2,1,0:T(8,128)(2,1)S(1)}, bf16[3,256,512]{2,1,0:T(8,128)(2,1)S(1)}, u32[]{:S(2)}, u32[]{:S(2)}) collective-permute-start(bf16[3,256,512]{2,1,0:T(8,128)(2,1)S(1)} %copy-done.84), channel_id=1, source_target_pairs={{0,8},{2,10},{4,12},{6,14},{8,16},{10,18},{12,20},{14,22},{16,24},... | collective-permute-start | bytes 2359304 | tf_op jit(solution)/shard_map/ppermute | solution.py:357
  692.8 47.1 %collective-permute-done.68 = bf16[3,256,512]{2,1,0:T(8,128)(2,1)S(1)} collective-permute-done((bf16[3,256,512]{2,1,0:T(8,128)(2,1)}, bf16[3,256,512]{2,1,0:T(8,128)(2,1)S(1)}, u32[]{:S(2)}, u32[]{:S(2)}) %collective-permute-start.68) | collective-permute-done | bytes 786464 | tf_op jit(solution)/shard_map/ppermute | solution.py:357
  741.1 32.5 %collective-permute-done.62 = bf16[3,256,512]{2,1,0:T(8,128)(2,1)S(1)} collective-permute-done((bf16[3,256,512]{2,1,0:T(8,128)(2,1)S(1)}, bf16[3,256,512]{2,1,0:T(8,128)(2,1)S(1)}, u32[]{:S(2)}, u32[]{:S(2)}) %collective-permute-start.62) | collective-permute-done | bytes 786464 | tf_op jit(solution)/shard_map/ppermute | solution.py:357
  811.2 20.8 %collective-permute-done.52 = bf16[512,1024]{1,0:T(8,128)(2,1)S(1)} collective-permute-done((bf16[512,1024]{1,0:T(8,128)(2,1)S(1)}, bf16[512,1024]{1,0:T(8,128)(2,1)S(1)}, u32[]{:S(2)}, u32[]{:S(2)}) %collective-permute-start.52) | collective-permute-done | bytes 1048608 | tf_op jit(solution)/shard_map/ppermute | solution.py:354
  837.5 16.6 %collective-permute-done.51 = bf16[512,1024]{1,0:T(8,128)(2,1)S(1)} collective-permute-done((bf16[512,1024]{1,0:T(8,128)(2,1)S(1)}, bf16[512,1024]{1,0:T(8,128)(2,1)S(1)}, u32[]{:S(2)}, u32[]{:S(2)}) %collective-permute-start.51) | collective-permute-done | bytes 1048608 | tf_op jit(solution)/shard_map/ppermute | solution.py:354
  864.0 18.4 %collective-permute-done.54 = bf16[512,1024]{1,0:T(8,128)(2,1)S(1)} collective-permute-done((bf16[512,1024]{1,0:T(8,128)(2,1)S(1)}, bf16[512,1024]{1,0:T(8,128)(2,1)S(1)}, u32[]{:S(2)}, u32[]{:S(2)}) %collective-permute-start.54) | collective-permute-done | bytes 1048608 | tf_op jit(solution)/shard_map/ppermute | solution.py:354
  886.0 20.1 %attend_back.1 = bf16[1024,1024]{1,0:T(8,128)(2,1)} custom-call(bf16[1024,1024]{1,0:T(8,128)(2,1)} %convolution_convert_fusion.1.qkv_ref, bf16[512,1024]{1,0:T(8,128)(2,1)} %convolution_convert_fusion.3.grad_ref, bf16[512,1024]{1,0:T(8,128)(2,1)} %get-tuple-element.36.out_ref, f32[4,2,1024]{2,1,0:T(2,128)} %get-tuple-element.45.log_ref, ...), custom_call_target="tpu_custom_call" | custom-call | flops 16106127360 | bytes 8388608 | tf_op jit(solution)/shard_map/attend_back/pallas_call | solution.py:139
  926.5 10.2 collective-permute-done.55
  938.9 13.7 %collective-permute-start.56 = (f32[2,512]{1,0:T(2,128)S(1)}, f32[2,512]{1,0:T(2,128)S(1)}, u32[]{:S(2)}, u32[]{:S(2)}) collective-permute-start(f32[2,512]{1,0:T(2,128)S(1)} %broadcast_select_fusion.32), channel_id=1, source_target_pairs={{0,16},{2,18},{4,20},{6,22},{8,24},{10,26},{12,28},{14,30},{16,0},... | collective-permute-start | bytes 12296 | tf_op jit(solution)/shard_map/ppermute | solution.py:354
  974.4 14.2 %collective-permute-done.48 = bf16[512,1024]{1,0:T(8,128)(2,1)S(1)} collective-permute-done((bf16[512,1024]{1,0:T(8,128)(2,1)S(1)}, bf16[512,1024]{1,0:T(8,128)(2,1)S(1)}, u32[]{:S(2)}, u32[]{:S(2)}) %collective-permute-start.48) | collective-permute-done | bytes 1048608 | tf_op jit(solution)/shard_map/ppermute | solution.py:354
  995.2 63.2 %reduce-scatter.3.cloned.1.call-done = bf16[64,1024]{1,0:T(8,128)(2,1)} async-done(((bf16[1024,1024]{1,0:T(8,128)(2,1)}), bf16[64,1024]{1,0:T(8,128)(2,1)}) %reduce-scatter.3.cloned.1.call-update) | async-done | bytes 131088 | tf_op jit(solution)/shard_map/reduce_scatter | solution.py:531
  (500 shorter events, 330.6 us)
Async XLA Ops:
  11.7 982.0 %reduce-scatter.5.cloned.1.call-start = ((), (), s32[]{:S(2)}) async-start(), calls=%async_computation.4 | async-start | bytes 1114112 | tf_op jit(solution)/shard_map/reduce_scatter | solution.py:530
  11.8 98.6 %collective-permute-start.15 = (bf16[512,1024]{1,0:T(8,128)(2,1)}, bf16[512,1024]{1,0:T(8,128)(2,1)}, u32[]{:S(2)}, u32[]{:S(2)}) collective-permute-start(bf16[512,1024]{1,0:T(8,128)(2,1)} %param.25), channel_id=1, source_target_pairs={{0,1},{1,0},{2,3},{3,2},{4,5},{5,4},{6,7},{7,6},{8,9},{9,8},{10,11... | collective-permute-start | bytes 3145736 | tf_op jit(solution)/shard_map/ppermute | solution.py:354
  14.8 126.3 %collective-permute-start.17 = (bf16[512,1024]{1,0:T(8,128)(2,1)}, bf16[512,1024]{1,0:T(8,128)(2,1)}, u32[]{:S(2)}, u32[]{:S(2)}) collective-permute-start(bf16[512,1024]{1,0:T(8,128)(2,1)} %param.25), channel_id=1, source_target_pairs={{0,4},{2,6},{4,0},{6,2},{8,12},{10,14},{12,8},{14,10},{16,20},{18,... | collective-permute-start | bytes 3145736 | tf_op jit(solution)/shard_map/ppermute | solution.py:354
  19.4 106.3 %collective-permute-start.38 = (bf16[3,64,512]{2,1,0:T(8,128)(2,1)}, bf16[3,64,512]{2,1,0:T(8,128)(2,1)}, u32[]{:S(2)}, u32[]{:S(2)}) collective-permute-start(bf16[3,64,512]{2,1,0:T(8,128)(2,1)} %pad_maximum_fusion.17), channel_id=1, source_target_pairs={{0,6},{2,4},{4,2},{6,0},{8,14},{10,12},{12,10},{14,8},{16,22},{18,... | collective-permute-start | bytes 589832 | tf_op jit(solution)/shard_map/ppermute | solution.py:354
  141.2 65.3 %collective-permute-start.12 = (bf16[512,1024]{1,0:T(8,128)(2,1)}, bf16[512,1024]{1,0:T(8,128)(2,1)S(1)}, u32[]{:S(2)}, u32[]{:S(2)}) collective-permute-start(bf16[512,1024]{1,0:T(8,128)(2,1)} %multiply_convert_fusion), channel_id=1, source_target_pairs={{0,4},{2,6},{4,0},{6,2},{8,12},{10,14},{12,8},{14,10},{16,20},{18,... | collective-permute-start | bytes 3145736 | tf_op jit(solution)/shard_map/ppermute | solution.py:354
  155.5 74.8 %collective-permute-start.16 = (bf16[1024,1024]{1,0:T(8,128)(2,1)S(1)}, bf16[1024,1024]{1,0:T(8,128)(2,1)}, u32[]{:S(2)}, u32[]{:S(2)}) collective-permute-start(bf16[1024,1024]{1,0:T(8,128)(2,1)S(1)} %maximum_select_fusion.3.table_ref), channel_id=1, source_target_pairs={{0,2},{2,0},{4,6},{6,4},{8,10},{10,8},{12,14},{14,12},{16,18},{18,... | collective-permute-start | bytes 6291464 | tf_op jit(solution)/shard_map/ppermute | solution.py:354
  155.5 81.8 %collective-permute-start.19 = (bf16[1024,1024]{1,0:T(8,128)(2,1)}, bf16[1024,1024]{1,0:T(8,128)(2,1)}, u32[]{:S(2)}, u32[]{:S(2)}) collective-permute-start(bf16[1024,1024]{1,0:T(8,128)(2,1)} %maximum_select_fusion.4.table_ref), channel_id=1, source_target_pairs={{0,2},{2,0},{4,6},{6,4},{8,10},{10,8},{12,14},{14,12},{16,18},{18,... | collective-permute-start | bytes 6291464 | tf_op jit(solution)/shard_map/ppermute | solution.py:354
  256.1 83.0 %collective-permute-start.35 = (bf16[3,256,512]{2,1,0:T(8,128)(2,1)S(1)}, bf16[3,256,512]{2,1,0:T(8,128)(2,1)}, u32[]{:S(2)}, u32[]{:S(2)}) collective-permute-start(bf16[3,256,512]{2,1,0:T(8,128)(2,1)S(1)} %pad_maximum_fusion.2.refs_8_), channel_id=1, source_target_pairs={{0,24},{2,26},{4,28},{6,30},{8,0},{10,2},{12,4},{14,6},{16,8},{18,... | collective-permute-start | bytes 2359304 | tf_op jit(solution)/shard_map/ppermute | solution.py:357
  265.1 122.5 %collective-permute-start.36 = (bf16[3,256,512]{2,1,0:T(8,128)(2,1)S(1)}, bf16[3,256,512]{2,1,0:T(8,128)(2,1)}, u32[]{:S(2)}, u32[]{:S(2)}) collective-permute-start(bf16[3,256,512]{2,1,0:T(8,128)(2,1)S(1)} %pad_maximum_fusion.2.refs_8_), channel_id=1, source_target_pairs={{0,16},{2,18},{4,20},{6,22},{8,24},{10,26},{12,28},{14,30},{16,0},... | collective-permute-start | bytes 2359304 | tf_op jit(solution)/shard_map/ppermute | solution.py:357
  271.3 116.3 %collective-permute-start.37 = (bf16[3,256,512]{2,1,0:T(8,128)(2,1)S(1)}, bf16[3,256,512]{2,1,0:T(8,128)(2,1)}, u32[]{:S(2)}, u32[]{:S(2)}) collective-permute-start(bf16[3,256,512]{2,1,0:T(8,128)(2,1)S(1)} %pad_maximum_fusion.2.refs_8_), channel_id=1, source_target_pairs={{0,8},{2,10},{4,12},{6,14},{8,16},{10,18},{12,20},{14,22},{16,24},... | collective-permute-start | bytes 2359304 | tf_op jit(solution)/shard_map/ppermute | solution.py:357
  286.7 119.4 %collective-permute-start.29 = (bf16[3,256,512]{2,1,0:T(8,128)(2,1)S(1)}, bf16[3,256,512]{2,1,0:T(8,128)(2,1)}, u32[]{:S(2)}, u32[]{:S(2)}) collective-permute-start(bf16[3,256,512]{2,1,0:T(8,128)(2,1)S(1)} %copy-done.27), channel_id=1, source_target_pairs={{0,24},{2,26},{4,28},{6,30},{8,0},{10,2},{12,4},{14,6},{16,8},{18,... | collective-permute-start | bytes 2359304 | tf_op jit(solution)/shard_map/ppermute | solution.py:357
  286.7 168.2 %collective-permute-start.30 = (bf16[3,256,512]{2,1,0:T(8,128)(2,1)S(1)}, bf16[3,256,512]{2,1,0:T(8,128)(2,1)}, u32[]{:S(2)}, u32[]{:S(2)}) collective-permute-start(bf16[3,256,512]{2,1,0:T(8,128)(2,1)S(1)} %copy-done.27), channel_id=1, source_target_pairs={{0,16},{2,18},{4,20},{6,22},{8,24},{10,26},{12,28},{14,30},{16,0},... | collective-permute-start | bytes 2359304 | tf_op jit(solution)/shard_map/ppermute | solution.py:357
  339.2 115.8 %collective-permute-start.31 = (bf16[3,256,512]{2,1,0:T(8,128)(2,1)S(1)}, bf16[3,256,512]{2,1,0:T(8,128)(2,1)}, u32[]{:S(2)}, u32[]{:S(2)}) collective-permute-start(bf16[3,256,512]{2,1,0:T(8,128)(2,1)S(1)} %copy-done.27), channel_id=1, source_target_pairs={{0,8},{2,10},{4,12},{6,14},{8,16},{10,18},{12,20},{14,22},{16,24},... | collective-permute-start | bytes 2359304 | tf_op jit(solution)/shard_map/ppermute | solution.py:357
  387.6 84.3 %collective-permute-start.23 = (bf16[3,256,512]{2,1,0:T(8,128)(2,1)S(1)}, bf16[3,256,512]{2,1,0:T(8,128)(2,1)S(1)}, u32[]{:S(2)}, u32[]{:S(2)}) collective-permute-start(bf16[3,256,512]{2,1,0:T(8,128)(2,1)S(1)} %copy-done.28), channel_id=1, source_target_pairs={{0,24},{2,26},{4,28},{6,30},{8,0},{10,2},{12,4},{14,6},{16,8},{18,... | collective-permute-start | bytes 2359304 | tf_op jit(solution)/shard_map/ppermute | solution.py:357
  387.6 100.6 %collective-permute-start.24 = (bf16[3,256,512]{2,1,0:T(8,128)(2,1)S(1)}, bf16[3,256,512]{2,1,0:T(8,128)(2,1)S(1)}, u32[]{:S(2)}, u32[]{:S(2)}) collective-permute-start(bf16[3,256,512]{2,1,0:T(8,128)(2,1)S(1)} %copy-done.28), channel_id=1, source_target_pairs={{0,16},{2,18},{4,20},{6,22},{8,24},{10,26},{12,28},{14,30},{16,0},... | collective-permute-start | bytes 2359304 | tf_op jit(solution)/shard_map/ppermute | solution.py:357
  406.2 82.0 %collective-permute-start.25 = (bf16[3,256,512]{2,1,0:T(8,128)(2,1)S(1)}, bf16[3,256,512]{2,1,0:T(8,128)(2,1)}, u32[]{:S(2)}, u32[]{:S(2)}) collective-permute-start(bf16[3,256,512]{2,1,0:T(8,128)(2,1)S(1)} %copy-done.28), channel_id=1, source_target_pairs={{0,8},{2,10},{4,12},{6,14},{8,16},{10,18},{12,20},{14,22},{16,24},... | collective-permute-start | bytes 2359304 | tf_op jit(solution)/shard_map/ppermute | solution.py:357
  516.5 87.4 %collective-permute-start.80 = (bf16[3,256,512]{2,1,0:T(8,128)(2,1)}, bf16[3,256,512]{2,1,0:T(8,128)(2,1)S(1)}, u32[]{:S(2)}, u32[]{:S(2)}) collective-permute-start(bf16[3,256,512]{2,1,0:T(8,128)(2,1)} %get-tuple-element.60), channel_id=1, source_target_pairs={{0,16},{2,18},{4,20},{6,22},{8,24},{10,26},{12,28},{14,30},{16,0},... | collective-permute-start | bytes 2359304 | tf_op jit(solution)/shard_map/ppermute | solution.py:357
  518.0 113.4 %collective-permute-start.81 = (bf16[3,256,512]{2,1,0:T(8,128)(2,1)}, bf16[3,256,512]{2,1,0:T(8,128)(2,1)}, u32[]{:S(2)}, u32[]{:S(2)}) collective-permute-start(bf16[3,256,512]{2,1,0:T(8,128)(2,1)} %get-tuple-element.61), channel_id=1, source_target_pairs={{0,24},{2,26},{4,28},{6,30},{8,0},{10,2},{12,4},{14,6},{16,8},{18,... | collective-permute-start | bytes 2359304 | tf_op jit(solution)/shard_map/ppermute | solution.py:357
  520.8 113.9 %collective-permute-start.73 = (bf16[3,256,512]{2,1,0:T(8,128)(2,1)}, bf16[3,256,512]{2,1,0:T(8,128)(2,1)S(1)}, u32[]{:S(2)}, u32[]{:S(2)}) collective-permute-start(bf16[3,256,512]{2,1,0:T(8,128)(2,1)} %get-tuple-element.55), channel_id=1, source_target_pairs={{0,8},{2,10},{4,12},{6,14},{8,16},{10,18},{12,20},{14,22},{16,24},... | collective-permute-start | bytes 2359304 | tf_op jit(solution)/shard_map/ppermute | solution.py:357
  520.9 151.6 %collective-permute-start.74 = (bf16[3,256,512]{2,1,0:T(8,128)(2,1)}, bf16[3,256,512]{2,1,0:T(8,128)(2,1)S(1)}, u32[]{:S(2)}, u32[]{:S(2)}) collective-permute-start(bf16[3,256,512]{2,1,0:T(8,128)(2,1)} %get-tuple-element.56), channel_id=1, source_target_pairs={{0,16},{2,18},{4,20},{6,22},{8,24},{10,26},{12,28},{14,30},{16,0},... | collective-permute-start | bytes 2359304 | tf_op jit(solution)/shard_map/ppermute | solution.py:357
  543.6 144.5 %collective-permute-start.75 = (bf16[3,256,512]{2,1,0:T(8,128)(2,1)}, bf16[3,256,512]{2,1,0:T(8,128)(2,1)S(1)}, u32[]{:S(2)}, u32[]{:S(2)}) collective-permute-start(bf16[3,256,512]{2,1,0:T(8,128)(2,1)} %get-tuple-element.57), channel_id=1, source_target_pairs={{0,24},{2,26},{4,28},{6,30},{8,0},{10,2},{12,4},{14,6},{16,8},{18,... | collective-permute-start | bytes 2359304 | tf_op jit(solution)/shard_map/ppermute | solution.py:357
  603.9 87.5 %collective-permute-start.67 = (bf16[3,256,512]{2,1,0:T(8,128)(2,1)}, bf16[3,256,512]{2,1,0:T(8,128)(2,1)S(1)}, u32[]{:S(2)}, u32[]{:S(2)}) collective-permute-start(bf16[3,256,512]{2,1,0:T(8,128)(2,1)} %get-tuple-element.51), channel_id=1, source_target_pairs={{0,8},{2,10},{4,12},{6,14},{8,16},{10,18},{12,20},{14,22},{16,24},... | collective-permute-start | bytes 2359304 | tf_op jit(solution)/shard_map/ppermute | solution.py:357
  631.3 108.6 %collective-permute-start.68 = (bf16[3,256,512]{2,1,0:T(8,128)(2,1)}, bf16[3,256,512]{2,1,0:T(8,128)(2,1)S(1)}, u32[]{:S(2)}, u32[]{:S(2)}) collective-permute-start(bf16[3,256,512]{2,1,0:T(8,128)(2,1)} %get-tuple-element.52), channel_id=1, source_target_pairs={{0,16},{2,18},{4,20},{6,22},{8,24},{10,26},{12,28},{14,30},{16,0},... | collective-permute-start | bytes 2359304 | tf_op jit(solution)/shard_map/ppermute | solution.py:357
  634.7 105.2 %collective-permute-start.69 = (bf16[3,256,512]{2,1,0:T(8,128)(2,1)}, bf16[3,256,512]{2,1,0:T(8,128)(2,1)S(1)}, u32[]{:S(2)}, u32[]{:S(2)}) collective-permute-start(bf16[3,256,512]{2,1,0:T(8,128)(2,1)} %get-tuple-element.53), channel_id=1, source_target_pairs={{0,24},{2,26},{4,28},{6,30},{8,0},{10,2},{12,4},{14,6},{16,8},{18,... | collective-permute-start | bytes 2359304 | tf_op jit(solution)/shard_map/ppermute | solution.py:357
  672.5 68.3 %collective-permute-start.61 = (bf16[3,256,512]{2,1,0:T(8,128)(2,1)S(1)}, bf16[3,256,512]{2,1,0:T(8,128)(2,1)S(1)}, u32[]{:S(2)}, u32[]{:S(2)}) collective-permute-start(bf16[3,256,512]{2,1,0:T(8,128)(2,1)S(1)} %copy-done.84), channel_id=1, source_target_pairs={{0,8},{2,10},{4,12},{6,14},{8,16},{10,18},{12,20},{14,22},{16,24},... | collective-permute-start | bytes 2359304 | tf_op jit(solution)/shard_map/ppermute | solution.py:357
  688.2 85.5 %collective-permute-start.62 = (bf16[3,256,512]{2,1,0:T(8,128)(2,1)S(1)}, bf16[3,256,512]{2,1,0:T(8,128)(2,1)S(1)}, u32[]{:S(2)}, u32[]{:S(2)}) collective-permute-start(bf16[3,256,512]{2,1,0:T(8,128)(2,1)S(1)} %copy-done.83), channel_id=1, source_target_pairs={{0,16},{2,18},{4,20},{6,22},{8,24},{10,26},{12,28},{14,30},{16,0},... | collective-permute-start | bytes 2359304 | tf_op jit(solution)/shard_map/ppermute | solution.py:357
  691.5 82.7 %collective-permute-start.63 = (bf16[3,256,512]{2,1,0:T(8,128)(2,1)S(1)}, bf16[3,256,512]{2,1,0:T(8,128)(2,1)S(1)}, u32[]{:S(2)}, u32[]{:S(2)}) collective-permute-start(bf16[3,256,512]{2,1,0:T(8,128)(2,1)S(1)} %copy-done.82), channel_id=1, source_target_pairs={{0,24},{2,26},{4,28},{6,30},{8,0},{10,2},{12,4},{14,6},{16,8},{18,... | collective-permute-start | bytes 2359304 | tf_op jit(solution)/shard_map/ppermute | solution.py:357
  739.9 70.4 %collective-permute-start.49 = (bf16[1024,1024]{1,0:T(8,128)(2,1)S(1)}, bf16[1024,1024]{1,0:T(8,128)(2,1)S(1)}, u32[]{:S(2)}, u32[]{:S(2)}) collective-permute-start(bf16[1024,1024]{1,0:T(8,128)(2,1)S(1)} %copy-done.11), channel_id=1, source_target_pairs={{0,2},{2,0},{4,6},{6,4},{8,10},{10,8},{12,14},{14,12},{16,18},{18,... | collective-permute-start | bytes 6291464 | tf_op jit(solution)/shard_map/ppermute | solution.py:354
  740.0 64.9 %collective-permute-start.50 = (bf16[1024,1024]{1,0:T(8,128)(2,1)S(1)}, bf16[1024,1024]{1,0:T(8,128)(2,1)S(1)}, u32[]{:S(2)}, u32[]{:S(2)}) collective-permute-start(bf16[1024,1024]{1,0:T(8,128)(2,1)S(1)} %copy-done.12), channel_id=1, source_target_pairs={{0,2},{2,0},{4,6},{6,4},{8,10},{10,8},{12,14},{14,12},{16,18},{18,... | collective-permute-start | bytes 6291464 | tf_op jit(solution)/shard_map/ppermute | solution.py:354
  798.8 163.2 %collective-permute-start.44 = (bf16[1024,1024]{1,0:T(8,128)(2,1)}, bf16[1024,1024]{1,0:T(8,128)(2,1)}, u32[]{:S(2)}, u32[]{:S(2)}) collective-permute-start(bf16[1024,1024]{1,0:T(8,128)(2,1)} %put_rows.9), channel_id=1, source_target_pairs={{0,2},{2,0},{4,6},{6,4},{8,10},{10,8},{12,14},{14,12},{16,18},{18,... | collective-permute-start | bytes 6291464 | tf_op jit(solution)/shard_map/ppermute | solution.py:354
  804.6 115.2 %collective-permute-start.45 = (bf16[1024,1024]{1,0:T(8,128)(2,1)}, bf16[1024,1024]{1,0:T(8,128)(2,1)}, u32[]{:S(2)}, u32[]{:S(2)}) collective-permute-start(bf16[1024,1024]{1,0:T(8,128)(2,1)} %put_rows.11), channel_id=1, source_target_pairs={{0,2},{2,0},{4,6},{6,4},{8,10},{10,8},{12,14},{14,12},{16,18},{18,... | collective-permute-start | bytes 6291464 | tf_op jit(solution)/shard_map/ppermute | solution.py:354
  919.7 138.7 %reduce-scatter.3.cloned.1.call-start = ((), (), s32[]{:S(2)}) async-start(), calls=%async_computation.3 | async-start | bytes 2228224 | tf_op jit(solution)/shard_map/reduce_scatter | solution.py:531
  (147 other events, 3108.6 us)
Sparse Core Ops, SparseCore 0:
  11.8 51.6 all-gather.1
  919.9 73.8 reduce-scatter.4
  997.9 60.4 reduce-scatter.2

commit v2 on v1

v2 whole, which is shorter than its diff:
```python
import functools

import jax
import jax.numpy as jnp
from jax import lax
from jax.experimental import pallas as pl
from jax.experimental.pallas import tpu as pltpu
from jax.sharding import PartitionSpec as P

HEAD_DIM = 64
FF = 512
EPS = 1e-06
SUB = 4
TILE = 256
NEG = -1e30
CHUNKS = (2, 2)
VMEM_BYTES = 56 * 1024 * 1024
BF = jnp.bfloat16
F32 = jnp.float32


def params(*semantics):
    return pltpu.CompilerParams(
        vmem_limit_bytes=VMEM_BYTES, dimension_semantics=semantics or None
    )


def cost(flops, moved, exps=0):
    return pl.CostEstimate(flops=int(flops), bytes_accessed=int(moved), transcendentals=int(exps))


def dot(left, right, left_dim=1, right_dim=0):
    return lax.dot_general(
        left, right, (((left_dim,), (right_dim,)), ((), ())), preferred_element_type=F32
    )


def tie_kernel(*refs):
    pass


def tie(values, others):
    leaves, tree = jax.tree.flatten(values)
    others = jax.tree.leaves(others)
    anywhere = pl.BlockSpec(memory_space=pl.ANY)
    outs = pl.pallas_call(
        tie_kernel,
        in_specs=[anywhere] * (len(leaves) + len(others)),
        out_specs=[anywhere] * len(leaves),
        out_shape=[jax.ShapeDtypeStruct(leaf.shape, leaf.dtype) for leaf in leaves],
        input_output_aliases={i: i for i in range(len(leaves))},
        compiler_params=params(),
        cost_estimate=cost(0, 0),
        name="tie",
    )(*leaves, *others)
    return jax.tree.unflatten(tree, outs)


def fill_bias(bias, seg_row, seg_col):
    length = bias.shape[0]

    @pl.when(pl.program_id(0) == 0)
    def _():
        for start in range(0, length, TILE):
            depth = start + TILE
            key_pos = lax.broadcasted_iota(jnp.int32, (depth, TILE), 0)
            query_pos = lax.broadcasted_iota(jnp.int32, (depth, TILE), 1) + start
            allowed = (query_pos >= key_pos) & (
                seg_col[:depth, :] == seg_row[:, start : start + TILE]
            )
            bias[:depth, start : start + TILE] = jnp.where(allowed, 0.0, NEG)


def attend_kernel(group, qkv_ref, seg_row, seg_col, out_ref, log_ref, bias):
    fill_bias(bias, seg_row, seg_col)
    length = bias.shape[0]
    wide = group * HEAD_DIM
    keys = qkv_ref[wide : wide + HEAD_DIM, :].T
    for head in range(group):
        rows = slice(head * HEAD_DIM, (head + 1) * HEAD_DIM)
        for start in range(0, length, TILE):
            depth = start + TILE
            cols = slice(start, depth)
            query = qkv_ref[rows, cols] * jnp.asarray(HEAD_DIM**-0.5, BF)
            scores = dot(keys[:depth], query) + bias[:depth, cols]
            top = jnp.max(scores, axis=0, keepdims=True)
            expo = jnp.exp(scores - top)
            total = jnp.sum(expo, axis=0, keepdims=True)
            mixed = dot(qkv_ref[wide + HEAD_DIM : wide + 2 * HEAD_DIM, :depth], expo.astype(BF))
            out_ref[rows, cols] = (mixed / total).astype(BF)
            log_ref[0, head : head + 1, cols] = top + jnp.log(total)


def attend(qkv, segments, heads_kv, group):
    length = qkv.shape[1]
    wide = (group + 2) * HEAD_DIM
    return pl.pallas_call(
        functools.partial(attend_kernel, group),
        grid=(heads_kv,),
        in_specs=[
            pl.BlockSpec((wide, length), lambda h: (h, 0)),
            pl.BlockSpec((1, length), lambda h: (0, 0)),
            pl.BlockSpec((length, 1), lambda h: (0, 0)),
        ],
        out_specs=[
            pl.BlockSpec((group * HEAD_DIM, length), lambda h: (h, 0)),
            pl.BlockSpec((1, group, length), lambda h: (h, 0, 0)),
        ],
        out_shape=[
            jax.ShapeDtypeStruct((heads_kv * group * HEAD_DIM, length), BF),
            jax.ShapeDtypeStruct((heads_kv, group, length), F32),
        ],
        scratch_shapes=[pltpu.VMEM((length, length), F32)],
        compiler_params=params("arbitrary"),
        cost_estimate=cost(
            heads_kv * group * length * length * HEAD_DIM * 12,
            4 * qkv.size,
            heads_kv * group * length * length,
        ),
        name="attend",
    )(qkv, segments.reshape(1, -1), segments.reshape(-1, 1))


def attend_back_kernel(
    group, qkv_ref, grad_ref, out_ref, log_ref, seg_row, seg_col, back_ref, bias, key_sum, value_sum
):
    fill_bias(bias, seg_row, seg_col)
    length = bias.shape[0]
    wide = group * HEAD_DIM
    scale = HEAD_DIM**-0.5
    keys_t = qkv_ref[wide : wide + HEAD_DIM, :]
    keys = keys_t.T
    values = qkv_ref[wide + HEAD_DIM : wide + 2 * HEAD_DIM, :].T
    key_sum[...] = jnp.zeros_like(key_sum)
    value_sum[...] = jnp.zeros_like(value_sum)
    for head in range(group):
        rows = slice(head * HEAD_DIM, (head + 1) * HEAD_DIM)
        for start in range(0, length, TILE):
            depth = start + TILE
            cols = slice(start, depth)
            query_t = qkv_ref[rows, cols] * jnp.asarray(scale, BF)
            grad_t = grad_ref[rows, cols]
            centre = jnp.sum(
                grad_t.astype(F32) * out_ref[rows, cols].astype(F32), axis=0, keepdims=True
            )
            scores = dot(keys[:depth], query_t) + bias[:depth, cols]
            prob = jnp.exp(scores - log_ref[0, head : head + 1, cols])
            prob_grad = dot(values[:depth], grad_t)
            score_grad = (prob * (prob_grad - centre)).astype(BF)
            back_ref[rows, cols] = (dot(keys_t[:, :depth], score_grad) * scale).astype(BF)
            key_sum[:depth, :] += dot(score_grad, query_t.T)
            value_sum[:depth, :] += dot(prob.astype(BF), grad_t.T)
    back_ref[wide : wide + HEAD_DIM, :] = key_sum[...].T.astype(BF)
    back_ref[wide + HEAD_DIM : wide + 2 * HEAD_DIM, :] = value_sum[...].T.astype(BF)


def attend_back(qkv, grads, attended, logs, segments, heads_kv, group):
    length = qkv.shape[1]
    wide = (group + 2) * HEAD_DIM
    head_block = pl.BlockSpec((group * HEAD_DIM, length), lambda h: (h, 0))
    return pl.pallas_call(
        functools.partial(attend_back_kernel, group),
        grid=(heads_kv,),
        in_specs=[
            pl.BlockSpec((wide, length), lambda h: (h, 0)),
            head_block,
            head_block,
            pl.BlockSpec((1, group, length), lambda h: (h, 0, 0)),
            pl.BlockSpec((1, length), lambda h: (0, 0)),
            pl.BlockSpec((length, 1), lambda h: (0, 0)),
        ],
        out_specs=pl.BlockSpec((wide, length), lambda h: (h, 0)),
        out_shape=jax.ShapeDtypeStruct(qkv.shape, BF),
        scratch_shapes=[
            pltpu.VMEM((length, length), F32),
            pltpu.VMEM((length, HEAD_DIM), F32),
            pltpu.VMEM((length, HEAD_DIM), F32),
        ],
        compiler_params=params("arbitrary"),
        cost_estimate=cost(
            heads_kv * group * length * length * HEAD_DIM * 30,
            8 * qkv.size,
            heads_kv * group * length * length,
        ),
        name="attend_back",
    )(qkv, grads, attended, logs, segments.reshape(1, -1), segments.reshape(-1, 1))


def pick_kernel(weighted, parts, index_ref, *refs):
    tables, out_ref = refs[int(weighted) : int(weighted) + parts], refs[-1]
    picked, start = None, 0
    for table in tables:
        count = table.shape[0]
        places = lax.broadcasted_iota(jnp.int32, (index_ref.shape[0], count), 1) + start
        part = dot((places == index_ref[...]).astype(BF), table[...])
        picked = part if picked is None else picked + part
        start += count
    if weighted:
        picked = picked * refs[0][...]
    out_ref[0, 0] = picked.astype(BF)


def pick(tables, index_cols, weight_cols, experts):
    cap = index_cols[0].shape[0] // experts
    width = tables[0][0].shape[1]
    column = pl.BlockSpec((cap, 1), lambda e: (e, 0))
    weighted = weight_cols is not None
    held = None
    for k, parts in enumerate(tables):
        args = [index_cols[k]] + ([weight_cols[k]] if weighted else []) + list(parts)
        specs = [column] * (len(args) - len(parts))
        specs += [pl.BlockSpec(part.shape, lambda e: (0, 0)) for part in parts]
        length = sum(part.shape[0] for part in parts)
        if held is not None:
            args.append(held)
            specs.append(pl.BlockSpec(memory_space=pl.ANY))
        held = pl.pallas_call(
            functools.partial(pick_kernel, weighted, len(parts)),
            grid=(experts,),
            in_specs=specs,
            out_specs=pl.BlockSpec((1, 1, cap, width), lambda e, k=k: (e, k, 0, 0)),
            out_shape=jax.ShapeDtypeStruct((experts, len(tables), cap, width), BF),
            input_output_aliases={} if k == 0 else {len(args) - 1: 0},
            compiler_params=params("arbitrary"),
            cost_estimate=cost(
                2 * experts * cap * length * width, 2 * (length + experts * cap) * width
            ),
            name="pick_rows",
        )(*args)
    return held


def put_kernel(start, added, index_ref, *refs):
    parts, out_ref = refs[: len(refs) - 1 - int(added)], refs[-1]
    cap = parts[0].shape[2]
    first = start + pl.program_id(0) * out_ref.shape[0]
    total, at = (refs[-2][...].astype(F32) if added else None), 0
    for held in parts:
        for expert in range(held.shape[0]):
            index = index_ref[:, at : at + cap]
            marks = lax.broadcasted_iota(jnp.int32, (out_ref.shape[0], cap), 0) + first == index
            part = dot(marks.astype(BF), held[expert, 0])
            total = part if total is None else total + part
            at += cap
    out_ref[...] = total.astype(out_ref.dtype)


def put(parts, index_row, which, start, count, addend=None, kind=BF):
    slots = index_row.shape[1]
    cap, width = parts[0].shape[2:]
    tile = min(TILE, count)
    in_specs = [pl.BlockSpec((1, slots), lambda r: (0, 0))]
    in_specs += [
        pl.BlockSpec((p.shape[0], 1, cap, width), lambda r: (0, which, 0, 0)) for p in parts
    ]
    added = addend is not None
    if added:
        in_specs.append(pl.BlockSpec((tile, width), lambda r: (start // tile + r, 0)))
    return pl.pallas_call(
        functools.partial(put_kernel, start, added),
        grid=(count // tile,),
        in_specs=in_specs,
        out_specs=pl.BlockSpec((tile, width), lambda r: (r, 0)),
        out_shape=jax.ShapeDtypeStruct((count, width), kind),
        compiler_params=params("arbitrary"),
        cost_estimate=cost(2 * slots * count * width, 2 * (count + slots) * width),
        name="put_rows",
    )(index_row, *parts, *([addend] if added else []))


def expert_kernel(
    weight_ref, picked, slot_grad, shards, slot_out, pick_grad, backs, acts, hid_grads
):
    cap, width = picked.shape[2:]
    planes, deep = shards.shape[0], shards.shape[3]

    def weights(which):
        return shards[:, 0, which].reshape(width, FF)

    def one(k, carry):
        rows = pl.ds(pl.multiple_of(k * cap, cap), cap)
        weight = weight_ref[0, rows, :]
        gate_pre = dot(picked[0, k], weights(0))
        up_pre = dot(picked[0, k], weights(1))
        sig = 1.0 / (1.0 + jnp.exp(-gate_pre))
        silu = gate_pre * sig
        act = (silu * up_pre).astype(BF)
        acts[rows, :] = act
        slot_out[0, k] = (dot(act, weights(2), 1, 1) * weight).astype(BF)
        inner = dot(slot_grad[0, k], weights(2))
        gate_grad = (inner * up_pre * sig * (1.0 + gate_pre * (1.0 - sig))).astype(BF)
        up_grad = (inner * silu).astype(BF)
        hid_grads[rows, :FF] = gate_grad
        hid_grads[rows, FF:] = up_grad
        pick_grad[0, k] = (
            dot(gate_grad, weights(0), 1, 1) + dot(up_grad, weights(1), 1, 1)
        ).astype(BF)
        return carry

    lax.fori_loop(0, SUB, one, 0)
    for plane in range(planes):
        cols = slice(plane * deep, (plane + 1) * deep)
        mine = picked[0, :, :, cols].reshape(SUB * cap, deep)
        both = dot(mine, hid_grads[...], 0, 0)
        backs[plane, 0, 0] = both[:, :FF].astype(BF)
        backs[plane, 0, 1] = both[:, FF:].astype(BF)
        mine = slot_grad[0, :, :, cols].reshape(SUB * cap, deep)
        backs[plane, 0, 2] = dot(mine, acts[...], 0, 0).astype(BF)


def run_experts(first, weight_col, picked, slot_grads, shards):
    planes, count, _, deep, _ = shards.shape
    cap, width = picked.shape[2:]
    slots = SUB * cap
    rows = pl.BlockSpec((1, SUB, cap, width), lambda e: (first + e, 0, 0, 0))
    out_rows = pl.BlockSpec((1, SUB, cap, width), lambda e: (e, 0, 0, 0))
    block = pl.BlockSpec((planes, 1, 3, deep, FF), lambda e: (0, e, 0, 0, 0))
    return pl.pallas_call(
        expert_kernel,
        grid=(count,),
        in_specs=[pl.BlockSpec((1, slots, 1), lambda e: (first + e, 0, 0)), rows, rows, block],
        out_specs=[out_rows, out_rows, block],
        out_shape=[jax.ShapeDtypeStruct((count, SUB, cap, width), BF)] * 2
        + [jax.ShapeDtypeStruct(shards.shape, BF)],
        scratch_shapes=[pltpu.VMEM((slots, FF), BF), pltpu.VMEM((slots, 2 * FF), BF)],
        compiler_params=params("arbitrary"),
        cost_estimate=cost(
            18 * count * slots * width * FF, count * (8 * slots * width + 12 * width * FF)
        ),
        name="experts",
    )(weight_col, picked, slot_grads, shards)


def place_kernel(first, experts, at_ref, *refs):
    pieces, outs, held, sems = refs[:SUB], refs[-5:-2], refs[-2], refs[-1]
    count = pieces[0].shape[0]
    copies = []
    for k in range(SUB):
        owner = lax.bitwise_xor(at_ref[0], k)
        for e in range(count):
            column = pl.multiple_of((owner * experts + (first + e)) * FF, FF)
            for which, out in enumerate(outs):
                at = len(copies)
                held[at] = pieces[k][e, which].astype(F32)
                copy = pltpu.make_async_copy(
                    held.at[at], out.at[:, pl.ds(column, FF)], sems.at[at]
                )
                copy.start()
                copies.append(copy)
    for copy in copies:
        copy.wait()


def place(sub, pieces, first, experts, held):
    count, _, rows, _ = pieces[0].shape
    anywhere = pl.BlockSpec(memory_space=pl.ANY)
    in_specs = [pl.BlockSpec(memory_space=pltpu.SMEM)]
    in_specs += [pl.BlockSpec(memory_space=pltpu.VMEM)] * SUB
    held = list(held or ())
    return pl.pallas_call(
        functools.partial(place_kernel, first, experts),
        in_specs=in_specs + [anywhere] * len(held),
        out_specs=[anywhere] * 3,
        out_shape=[jax.ShapeDtypeStruct((rows, SUB * experts * FF), F32)] * 3,
        scratch_shapes=[
            pltpu.VMEM((3 * SUB * count, rows, FF), F32),
            pltpu.SemaphoreType.DMA((3 * SUB * count,)),
        ],
        input_output_aliases={1 + SUB + i: i for i in range(len(held))},
        compiler_params=params(),
        cost_estimate=cost(0, 18 * SUB * count * rows * FF),
        name="place_rows",
    )(sub.astype(jnp.int32).reshape(1), *pieces, *held)


def norm_scale(values):
    return lax.rsqrt(jnp.mean(values * values, axis=-1, keepdims=True) + EPS)


def norm_backward(values, rms_scale, gain_row, gradient):
    weighted = gradient * gain_row
    centre = jnp.mean(weighted * values, axis=-1, keepdims=True)
    back_values = rms_scale * weighted - values * rms_scale * rms_scale * rms_scale * centre
    return (back_values, jnp.sum(gradient * values * rms_scale, axis=0))


def layer(
    fsdp,
    tp,
    tokens,
    segments,
    slots,
    gate_values,
    gains,
    w_query,
    w_key,
    w_value,
    w_out,
    w_gate,
    w_up,
    w_down,
    cotangent,
):
    length, width = segments.shape[0], tokens.shape[1]
    half = tokens.shape[0]
    planes = fsdp // SUB
    at_fsdp, at_tp = lax.axis_index("fsdp"), lax.axis_index("tp")
    sub, plane = at_fsdp % SUB, at_fsdp // SUB
    heads_kv = w_key.shape[1] // HEAD_DIM
    group = w_query.shape[1] // w_key.shape[1]
    experts = slots.shape[1] // SUB
    cap = slots.shape[2]

    def swap(values, mask, axis="fsdp"):
        size = fsdp if axis == "fsdp" else tp
        return lax.ppermute(values, axis, [(i, i ^ mask) for i in range(size)])

    def shift(values, planes_on):
        return lax.ppermute(
            values, "fsdp", [(i, (i + planes_on * SUB) % fsdp) for i in range(fsdp)]
        )

    def by_sub(pieces):
        near = [jnp.where((sub & 1) == 1, pieces[k ^ 1], pieces[k]) for k in range(SUB)]
        return [jnp.where((sub & 2) == 2, near[k ^ 2], near[k]) for k in range(SUB)]

    def ordered(mine, other):
        return jnp.where(
            at_tp == 0, jnp.concatenate([mine, other]), jnp.concatenate([other, mine])
        )

    def sequence_gather(mine):
        if tp == 2:
            return ordered(mine, swap(mine, 1, "tp"))
        return lax.all_gather(mine, "tp", axis=0, tiled=True)

    def part_of(values, which):
        return lax.dynamic_slice_in_dim(values, which * half, half, 0)

    def sequence_scatter(values):
        if tp == 2:
            other = swap(part_of(values, 1 - at_tp).astype(BF), 1, "tp")
            return part_of(values, at_tp) + other.astype(F32)
        return lax.psum_scatter(values, "tp", scatter_dimension=0, tiled=True)

    turn = half * at_tp if tp == 2 else 0

    def plane_start(mine):
        if tp == 2:
            return swap(mine, 1, "tp"), swap(mine, 2)
        return (lax.all_gather(mine, "tp", axis=0, tiled=True),)

    def plane_finish(mine, begun):
        if tp == 2:
            beside, across = begun
            first, third = (mine, beside), (across, swap(beside, 2))
        else:
            first = begun
            third = (swap(first[0], 2),)
        return [first, [swap(p, 1) for p in first], third, [swap(p, 1) for p in third]]

    def plane_scatter(put_one):
        fourth, second = swap(put_one(3, 0, length), 1), swap(put_one(1, 0, length), 1)
        if tp == 2:
            corner = put_one(2, half, half, fourth)
            across = put_one(2, 0, half, fourth)
            other = put_one(0, half, half, second, F32)
            mine = put_one(0, 0, half, second, F32)

            def finish(got):
                corner, across = got
                beside = swap((other + corner.astype(F32)).astype(BF), 1, "tp")
                return mine + across.astype(F32) + beside.astype(F32)

            return (swap(corner, 2), swap(across, 2)), (corner, across), finish
        third = put_one(2, 0, length, fourth)
        first = put_one(0, 0, length, second, F32)

        def finish(got):
            total = first + got.astype(F32)
            return lax.psum_scatter(total, "tp", scatter_dimension=0, tiled=True)

        return swap(third, 2), third, finish

    def weight_scatter(values):
        values = values.reshape(planes, 2, 2, -1, values.shape[1])
        core, line = sub & 1, sub >> 1
        sent = lax.dynamic_index_in_dim(values, 1 - core, 2, keepdims=False)
        kept = lax.dynamic_index_in_dim(values, core, 2, keepdims=False)
        values = kept.astype(F32) + swap(sent.astype(BF), 1).astype(F32)
        sent = lax.dynamic_index_in_dim(values, 1 - line, 1, keepdims=False)
        kept = lax.dynamic_index_in_dim(values, line, 1, keepdims=False)
        values = kept + swap(sent.astype(BF), 2).astype(F32)

        total = lax.dynamic_index_in_dim(values, plane, 0, keepdims=False)
        got = [
            shift(
                lax.dynamic_index_in_dim(
                    values, (plane + r) % planes, 0, keepdims=False
                ).astype(BF),
                r,
            )
            for r in range(1, planes)
        ]
        return values, got, lambda got: sum([total] + [part.astype(F32) for part in got])

    def gain_scatter(values):
        values = values.reshape(2, planes, SUB, tp, -1)

        def block(which, axis):
            return lax.dynamic_index_in_dim(values, which, axis, keepdims=False)

        if tp == 2:
            values = block(at_tp, 3) + swap(block(1 - at_tp, 3), 1, "tp")
        else:
            values = lax.psum_scatter(values, "tp", scatter_dimension=3)
        values = sum([block(sub, 2)] + [swap(block(sub ^ k, 2), k) for k in range(1, SUB)])
        return values, lambda values: sum(
            [lax.dynamic_index_in_dim(values, plane, 1, keepdims=False)]
            + [
                shift(
                    lax.dynamic_index_in_dim(values, (plane + r) % planes, 1, keepdims=False), r
                )
                for r in range(1, planes)
            ]
        )

    if tp == 2:
        near_gains = swap(gains, 1, "tp")
        near_gains = jnp.where(
            at_tp == 0,
            jnp.concatenate([gains, near_gains], axis=1),
            jnp.concatenate([near_gains, gains], axis=1),
        )
    else:
        near_gains = lax.all_gather(gains, "tp", axis=1, tiled=True)
    whole_tokens = sequence_gather(tokens)
    plane_gains = jnp.concatenate(
        by_sub([near_gains] + [swap(near_gains, k) for k in range(1, SUB)]), axis=1
    )
    all_gains = jnp.stack([plane_gains] + [shift(plane_gains, -r) for r in range(1, planes)])
    all_gains = jnp.concatenate([all_gains, all_gains])
    all_gains = lax.dynamic_slice_in_dim(all_gains, planes - plane, planes, 0)
    all_gains = all_gains.transpose(1, 0, 2).reshape(2, -1)

    rows = w_query.shape[0]
    packed = jnp.concatenate(
        [
            w_query.reshape(rows, heads_kv, group * HEAD_DIM),
            w_key.reshape(rows, heads_kv, HEAD_DIM),
            w_value.reshape(rows, heads_kv, HEAD_DIM),
        ],
        axis=2,
    ).reshape(rows, -1)
    qkv_cols = packed.shape[1]
    attn_w = lax.all_gather(
        jnp.concatenate([packed, w_out], axis=1), "fsdp", axis=0, tiled=True
    )
    qkv_w, out_w = attn_w[:, :qkv_cols], attn_w[:, qkv_cols:]

    live = slots[0] >= 0
    table = jnp.stack([slots[0].astype(F32), jnp.where(live, gate_values[0], 0.0)])

    def table_for(k):
        return lax.dynamic_slice_in_dim(table, (sub ^ k) * experts, experts, 1)

    tables = [table_for(0)] + [swap(table_for(k), k) for k in range(1, SUB)]
    index = [t[0].astype(jnp.int32) for t in tables]
    index = [jnp.where(v < 0, -1, (v + (length - turn)) % length) for v in index]
    index_col = [v.reshape(-1, 1) for v in index]
    index_row = [v.reshape(1, -1) for v in index]
    slot_weight = [t[1] for t in tables]

    across = [[j + SUB * p for p in range(planes)] for j in range(SUB)]
    chunks, taken = [], 0
    for count in CHUNKS:
        count = min(count, experts - taken)
        if count:
            chunks.append((taken, count))
            taken += count

    def pieces_of(first, count, others):
        def piece(k):
            column = ((sub ^ k) * experts + first) * FF
            cut = [
                lax.dynamic_slice_in_dim(w, column, count * FF, 1).reshape(-1, count, FF)
                for w in (w_gate, w_up, w_down)
            ]
            return jnp.stack(cut).transpose(2, 0, 1, 3)

        sends = tie([piece(k) for k in range(1, SUB)], others)
        return [piece(0)] + [swap(sent, k + 1) for k, sent in enumerate(sends)]

    def shards_of(pieces, others=None):
        if others is not None:
            pieces = [pieces[0]] + tie(pieces[1:], others)
        mine = jnp.concatenate(by_sub(pieces), axis=2)
        return lax.all_gather(mine, "fsdp", axis_index_groups=across), mine

    held, mine_first = shards_of(
        pieces_of(*chunks[0], (plane_gains, tables)), (all_gains, whole_tokens)
    )
    shards = [held]

    whole_resid = whole_tokens.astype(F32)
    first_low = (whole_resid * norm_scale(whole_resid) * all_gains[0]).astype(BF)
    begun = plane_start(tie(cotangent, mine_first))
    qkv = dot(qkv_w, first_low, 0, 1).astype(BF)
    later = [pieces_of(*chunk, qkv) for chunk in chunks[1:]]
    attended, logs = attend(qkv, segments, heads_kv, group)
    begun, later = tie((begun, later), attended)
    shards += [shards_of(pieces)[0] for pieces in later]
    cots = plane_finish(cotangent, begun)
    resid = tokens.astype(F32)
    hidden = resid + sequence_scatter(dot(attended, out_w, 0, 1))
    scale_two = norm_scale(hidden)
    second_low = (hidden * scale_two * all_gains[1]).astype(BF)

    slot_grads = pick(
        cots, index_col, [w.reshape(-1, 1) for w in slot_weight], experts
    )
    picked = pick(
        plane_finish(second_low, plane_start(second_low)), index_col, None, experts
    )
    weight_col = jnp.stack(slot_weight, axis=1).reshape(experts, -1, 1)
    slot_outs, pick_grads, sums = [], [], []
    for (first, count), held in zip(chunks, shards):
        slot_out, pick_grad, backs = run_experts(first, weight_col, picked, slot_grads, held)
        slot_outs.append(slot_out)
        pick_grads.append(pick_grad)
        sums.append(
            lax.psum_scatter(backs, "fsdp", scatter_dimension=0, axis_index_groups=across)
        )
    got, sent, finish = plane_scatter(lambda k, *more: put(pick_grads, index_row[k], k, *more))
    second_grad = finish(got)
    index_row = tie(index_row, sent)
    got_out, _, finish_out_sum = plane_scatter(
        lambda k, *more: put(slot_outs, index_row[k], k, *more)
    )

    back_two, second_gain = norm_backward(hidden, scale_two, all_gains[1], second_grad)
    grad_hidden = cotangent.astype(F32) + back_two
    own_low = grad_hidden.astype(BF)

    def rows_out(part):
        part = part.reshape(-1, 3, SUB, rows, FF)
        return [
            lax.dynamic_index_in_dim(part, sub ^ k, 2, keepdims=False) for k in range(SUB)
        ]

    early = []
    for part in sums[:-1]:
        own, *sends = rows_out(part)
        early.append((own, tie(sends, own_low)))
    if tp == 2:
        other_low = tie(swap(own_low, 1, "tp"), early)
        hidden_low = ordered(own_low, other_low)
    else:
        hidden_low = lax.all_gather(own_low, "tp", axis=0, tiled=True)
    early = [[own] + [swap(sent, k + 1) for k, sent in enumerate(sends)] for own, sends in early]
    _, got_grad_out, finish_out = weight_scatter(dot(hidden_low, attended, 0, 1))
    attended_grad = dot(out_w, hidden_low, 0, 1).astype(BF)
    qkv_grad = attend_back(qkv, attended_grad, attended, logs, segments, heads_kv, group)
    grad_qkv = dot(first_low, qkv_grad, 0, 1)
    first_part = dot(qkv_grad, qkv_w, 0, 1)
    if tp == 2:
        got = swap(part_of(first_part, 1 - at_tp).astype(BF), 1, "tp")
        got, early, got_out = tie((got, early, got_out), ())
        first_grad = part_of(first_part, at_tp) + got.astype(F32)
    else:
        first_grad = sequence_scatter(first_part)
    mixed = (hidden + finish_out_sum(got_out)).astype(BF)
    expert_grads = None
    for number, pieces in enumerate(early):
        expert_grads = place(sub, pieces, chunks[number][0], experts, expert_grads)
    back_one, first_gain = norm_backward(resid, norm_scale(resid), all_gains[0], first_grad)
    grad_tokens = grad_hidden + back_one
    grad_gains, finish_gains = gain_scatter(jnp.stack([first_gain, second_gain]))
    grad_qkv, got_qkv, finish_qkv = weight_scatter(grad_qkv)
    grad_out = finish_out(tie(got_grad_out, grad_qkv))

    own, *sends = rows_out(tie(sums[-1], (grad_qkv, grad_gains)))
    late = [own] + [swap(sent, k + 1) for k, sent in enumerate(sends)]
    expert_grads = place(sub, late, chunks[-1][0], experts, expert_grads)
    grad_gains = finish_gains(grad_gains)
    grad_qkv = finish_qkv(got_qkv).reshape(rows, heads_kv, -1)
    cut = group * HEAD_DIM
    return (
        mixed,
        grad_tokens,
        grad_gains,
        grad_qkv[:, :, :cut].reshape(rows, -1),
        grad_qkv[:, :, cut : cut + HEAD_DIM].reshape(rows, -1),
        grad_qkv[:, :, cut + HEAD_DIM :].reshape(rows, -1),
        grad_out,
        *expert_grads,
    )


def solution(mesh):
    both, split = P(("fsdp", "tp"), None), P("fsdp", "tp")
    experts, feature = P("fsdp", "tp", None), P(None, ("fsdp", "tp"))
    return jax.shard_map(
        functools.partial(layer, mesh.shape["fsdp"], mesh.shape["tp"]),
        mesh=mesh,
        in_specs=(both, P("fsdp"), experts, experts, feature) + (split,) * 7 + (both,),
        out_specs=(both, both, feature) + (split,) * 7,
        check_vma=False,
    )
```

time: 1080 us -> 598 us (0.55)
  waiting for transfers between devices: 560 us -> 172 us
  starting transfers between devices: 161 us -> 61.5 us
    ppermute x24 -> x12, waiting for transfers between devices: 300 us -> 17.6 us  [shift(): lax.ppermute(values, 'fsdp', [(i, (i + planes_on * SUB) % fsdp) for i in...]
    ppermute x24 -> x12, starting transfers between devices: 94.8 us -> 20.6 us  [shift(): lax.ppermute(values, 'fsdp', [(i, (i + planes_on * SUB) % fsdp) for i in...]
    reduce_scatter x2, waiting for transfers between devices: 63.4 us -> 0.01 us  [layer(): lax.psum_scatter(backs, 'fsdp', scatter_dimension=0, axis_index_groups=ac...]
    ppermute x61 -> x55, waiting for transfers between devices: 194 us -> 154 us  [swap(): return lax.ppermute(values, axis, [(i, i ^ mask) for i in range(size)])]
    ppermute x61 -> x55, starting transfers between devices: 65.6 us -> 40.2 us  [swap(): return lax.ppermute(values, axis, [(i, i ^ mask) for i in range(size)])]
    another operation x12 -> x1, other arithmetic: 12 us -> 0.01 us  [layer(): weight_col = jnp.stack(slot_weight, axis=1).reshape(experts, -1, 1)]
    pallas_call x20 -> x35, Pallas kernels: 158 us -> 167 us  [the longest x2 57.7 us: run_experts(): pl.pallas_call(expert_kernel, grid=(count,), in_specs=[pl.BlockSpec((1, s...]
    unnamed x223 -> x206, local copies, waits for them, and re-layouts: 31.5 us -> 24 us
  transfers between devices with their start and end apart: 88 -> 72, of which waited for: 40 -> 25; matrix products, arithmetic and copies ran while one was open for 11% -> 20% of each run, Pallas kernels for 16% -> 34%
where the time goes in v2:
time: 598 us; the launch traced here: 592 us
  Pallas kernels  205 us (34%)
  waiting for transfers between devices  172 us (29%)
  starting transfers between devices  61.5 us (10%)
  other arithmetic  60.4 us (10%)
  local copies, waits for them, and re-layouts  54.5 us (9%)
  matrix products  22.9 us (4%)
  between operations  15.6 us (3%)
    ppermute x55, waiting for transfers between devices, swap(): return lax.ppermute(values, axis, [(i, i ^ mask) for i in range(size)])  154 us
    pallas_call x2, Pallas kernels, run_experts(): pl.pallas_call(expert_kernel, grid=(count,), in_specs=[pl.BlockSpec((1, s...  57.7 us
    pallas_call x12, Pallas kernels, put(): pl.pallas_call(functools.partial(put_kernel, start, added), grid=(count /...  54.5 us
    pallas_call x8, Pallas kernels, pick(): pl.pallas_call(functools.partial(pick_kernel, weighted, len(parts)), grid...  48.3 us
    ppermute x55, starting transfers between devices, swap(): return lax.ppermute(values, axis, [(i, i ^ mask) for i in range(size)])  40.2 us
    unnamed x206, local copies, waits for them, and re-layouts  24 us
    dot_general x6, matrix products, dot(): lax.dot_general(left, right, (((left_dim,), (right_dim,)), ((), ())), pre...  22.9 us
    ppermute x12, starting transfers between devices, shift(): lax.ppermute(values, 'fsdp', [(i, (i + planes_on * SUB) % fsdp) for i in...  20.6 us
  transfers between devices with their start and end apart: 72, of which 25 were waited for; matrix products, arithmetic and copies ran while one was open for 20% of the time, Pallas kernels for 34%

profile of v2, /device:TPU:0, one launch (start us, length us, event | category | flops | bytes accessed | tf_op | source)
XLA Modules:
  0.0 591.8 jit_solution(5560486297447428582)
XLA Ops:
  49.7 5.5 collective-permute-done
  59.6 8.1 %collective-permute-done.21.refs_2_ = bf16[2,3,64,512]{3,2,1,0:T(8,128)(2,1)S(1)} collective-permute-done((bf16[2,3,64,512]{3,2,1,0:T(8,128)(2,1)}, bf16[2,3,64,512]{3,2,1,0:T(8,128)(2,1)S(1)}, u32[]{:S(2)}, u32[]{:S(2)}) %collective-permute-start.21) | collective-permute-done | bytes 393248 | tf_op jit(solution)/shard_map/ppermute | solution.py:416
  84.0 5.5 convolution_convert_fusion.qkv_ref.refs_3_
  91.3 18.0 %attend.1 = (bf16[512,1024]{1,0:T(8,128)(2,1)}, f32[4,2,1024]{2,1,0:T(2,128)}) custom-call(bf16[1024,1024]{1,0:T(8,128)(2,1)} %convolution_convert_fusion.qkv_ref.refs_3_, s32[1,1024]{1,0:T(1,128)} %bitcast.291, s32[1024,1]{1,0:T(8,128)} %copy.196.seg_col), custom_call_target="tpu_custom_call" | custom-call | flops 6442450944 | bytes 4194304 | tf_op jit(solution)/shard_map/attend/pallas_call | solution.py:97
  109.4 7.2 %collective-permute-done.25.refs_4_ = bf16[2,3,64,512]{3,2,1,0:T(8,128)(2,1)S(1)} collective-permute-done((bf16[2,3,64,512]{3,2,1,0:T(8,128)(2,1)}, bf16[2,3,64,512]{3,2,1,0:T(8,128)(2,1)S(1)}, u32[]{:S(2)}, u32[]{:S(2)}) %collective-permute-start.25) | collective-permute-done | bytes 393248 | tf_op jit(solution)/shard_map/ppermute | solution.py:416
  116.6 6.8 %collective-permute-done.26.refs_5_ = bf16[2,3,64,512]{3,2,1,0:T(8,128)(2,1)S(1)} collective-permute-done((bf16[2,3,64,512]{3,2,1,0:T(8,128)(2,1)}, bf16[2,3,64,512]{3,2,1,0:T(8,128)(2,1)S(1)}, u32[]{:S(2)}, u32[]{:S(2)}) %collective-permute-start.26) | collective-permute-done | bytes 393248 | tf_op jit(solution)/shard_map/ppermute | solution.py:416
  139.2 19.7 %collective-permute-done.8 = bf16[512,1024]{1,0:T(8,128)(2,1)} collective-permute-done((bf16[512,1024]{1,0:T(8,128)(2,1)S(1)}, bf16[512,1024]{1,0:T(8,128)(2,1)}, u32[]{:S(2)}, u32[]{:S(2)}) %collective-permute-start.8) | collective-permute-done | bytes 1048608 | tf_op jit(solution)/shard_map/ppermute | solution.py:416
  167.6 19.1 %collective-permute-done.14.refs_1_ = bf16[512,1024]{1,0:T(8,128)(2,1)} collective-permute-done((bf16[512,1024]{1,0:T(8,128)(2,1)S(1)}, bf16[512,1024]{1,0:T(8,128)(2,1)}, u32[]{:S(2)}, u32[]{:S(2)}) %collective-permute-start.14) | collective-permute-done | bytes 1048608 | tf_op jit(solution)/shard_map/ppermute | solution.py:416
  199.7 6.5 %pick_rows.12.refs_3_ = bf16[4,4,256,1024]{3,2,1,0:T(8,128)(2,1)} custom-call(s32[1024,1]{1,0:T(8,128)} %fusion.29.index_ref, f32[1024,1]{1,0:T(8,128)} %bitcast.246, bf16[512,1024]{1,0:T(8,128)(2,1)} %refs_1_.1, bf16[512,1024]{1,0:T(8,128)(2,1)} %get-tuple-element.67.refs_2_), custom_call_target="tpu_custom_call" | custom-call | flops 2147483648 | bytes 4194304 | tf_op jit(solution)/shard_map/pick_rows/pallas_call | solution.py:217
  206.2 7.6 %collective-permute-done.12.refs_0_ = bf16[512,1024]{1,0:T(8,128)(2,1)} collective-permute-done((bf16[512,1024]{1,0:T(8,128)(2,1)S(1)}, bf16[512,1024]{1,0:T(8,128)(2,1)}, u32[]{:S(2)}, u32[]{:S(2)}) %collective-permute-start.12) | collective-permute-done | bytes 1048608 | tf_op jit(solution)/shard_map/ppermute | solution.py:416
  213.8 20.3 %collective-permute-done.15.refs_1_ = bf16[512,1024]{1,0:T(8,128)(2,1)} collective-permute-done((bf16[512,1024]{1,0:T(8,128)(2,1)}, bf16[512,1024]{1,0:T(8,128)(2,1)}, u32[]{:S(2)}, u32[]{:S(2)}) %collective-permute-start.15) | collective-permute-done | bytes 1048608 | tf_op jit(solution)/shard_map/ppermute | solution.py:416
  234.2 6.1 %pick_rows.13.refs_3_ = bf16[4,4,256,1024]{3,2,1,0:T(8,128)(2,1)} custom-call(s32[1024,1]{1,0:T(8,128)} %fusion.27.index_ref, f32[1024,1]{1,0:T(8,128)} %bitcast.249, bf16[512,1024]{1,0:T(8,128)(2,1)} %collective-permute-done.30.refs_1_, bf16[512,1024]{1,0:T(8,128)(2,1)} %collective-permute-done.31.refs_2_, ...), custom_call_target="tpu_custom_call", output_to_operand_aliasing={{}: (4, {})} | custom-call | flops 2147483648 | bytes 4194304 | tf_op jit(solution)/shard_map/pick_rows/pallas_call | solution.py:217
  240.3 6.1 %pick_rows.14.refs_3_ = bf16[4,4,256,1024]{3,2,1,0:T(8,128)(2,1)} custom-call(s32[1024,1]{1,0:T(8,128)} %fusion.25.index_ref, f32[1024,1]{1,0:T(8,128)} %bitcast.248, bf16[512,1024]{1,0:T(8,128)(2,1)} %get-tuple-element.66.refs_1_, bf16[512,1024]{1,0:T(8,128)(2,1)} %collective-permute-done.28.refs_2_, ...), custom_call_target="tpu_custom_call", output_to_operand_aliasing={{}: (4, {})} | custom-call | flops 2147483648 | bytes 4194304 | tf_op jit(solution)/shard_map/pick_rows/pallas_call | solution.py:217
  246.4 5.9 pick_rows.8.refs_2_
  252.3 6.1 %pick_rows.15.slot_grad = bf16[4,4,256,1024]{3,2,1,0:T(8,128)(2,1)} custom-call(s32[1024,1]{1,0:T(8,128)} %fusion.23.index_ref, f32[1024,1]{1,0:T(8,128)} %bitcast.247, bf16[512,1024]{1,0:T(8,128)(2,1)} %collective-permute-done.27.refs_1_, bf16[512,1024]{1,0:T(8,128)(2,1)} %collective-permute-done.29.refs_2_, ...), custom_call_target="tpu_custom_call", output_to_operand_aliasing={{}: (4, {})} | custom-call | flops 2147483648 | bytes 4194304 | tf_op jit(solution)/shard_map/pick_rows/pallas_call | solution.py:217
  258.4 5.9 pick_rows.9.refs_2_
  264.3 5.9 pick_rows.10.refs_2_
  272.1 5.8 pick_rows.11.picked
  278.0 28.8 %experts.2 = (bf16[2,4,256,1024]{3,2,1,0:T(8,128)(2,1)}, bf16[2,4,256,1024]{3,2,1,0:T(8,128)(2,1)}, bf16[4,2,3,256,512]{4,3,2,1,0:T(8,128)(2,1)}) custom-call(f32[4,1024,1]{2,1,0:T(8,128)} %copy.241.weight_ref, bf16[4,4,256,1024]{3,2,1,0:T(8,128)(2,1)} %pick_rows.11.picked, bf16[4,4,256,1024]{3,2,1,0:T(8,128)(2,1)} %pick_rows.15.slot_grad, ...), custom_call_target="tpu_custom_call" | custom-call | flops 19327352832 | bytes 29360128 | tf_op jit(solution)/shard_map/experts/pallas_call | solution.py:318
  307.4 28.9 %experts.3 = (bf16[2,4,256,1024]{3,2,1,0:T(8,128)(2,1)}, bf16[2,4,256,1024]{3,2,1,0:T(8,128)(2,1)}, bf16[4,2,3,256,512]{4,3,2,1,0:T(8,128)(2,1)}) custom-call(f32[4,1024,1]{2,1,0:T(8,128)} %copy.241.weight_ref, bf16[4,4,256,1024]{3,2,1,0:T(8,128)(2,1)} %pick_rows.11.picked, bf16[4,4,256,1024]{3,2,1,0:T(8,128)(2,1)} %pick_rows.15.slot_grad, ...), custom_call_target="tpu_custom_call" | custom-call | flops 19327352832 | bytes 29360128 | tf_op jit(solution)/shard_map/experts/pallas_call | solution.py:318
  336.4 5.3 put_rows.12
  342.8 5.3 put_rows.17
  364.3 15.4 %collective-permute-done.36 = bf16[512,1024]{1,0:T(8,128)(2,1)} collective-permute-done((bf16[512,1024]{1,0:T(8,128)(2,1)}, bf16[512,1024]{1,0:T(8,128)(2,1)}, u32[]{:S(2)}, u32[]{:S(2)}) %collective-permute-start.36) | collective-permute-done | bytes 1048608 | tf_op jit(solution)/shard_map/ppermute | solution.py:416
  387.1 5.5 put_rows.20
  392.6 9.1 %collective-permute-done.35 = bf16[512,1024]{1,0:T(8,128)(2,1)S(1)} collective-permute-done((bf16[512,1024]{1,0:T(8,128)(2,1)}, bf16[512,1024]{1,0:T(8,128)(2,1)S(1)}, u32[]{:S(2)}, u32[]{:S(2)}) %collective-permute-start.35) | collective-permute-done | bytes 1048608 | tf_op jit(solution)/shard_map/ppermute | solution.py:416
  412.1 5.3 put_rows.15
  441.9 19.9 %attend_back.1 = bf16[1024,1024]{1,0:T(8,128)(2,1)} custom-call(bf16[1024,1024]{1,0:T(8,128)(2,1)} %convolution_convert_fusion.qkv_ref.refs_3_, bf16[512,1024]{1,0:T(8,128)(2,1)} %convolution_convert_fusion.1.grad_ref, bf16[512,1024]{1,0:T(8,128)(2,1)} %get-tuple-element.56.refs_6_.out_ref, f32[4,2,1024]{2,1,0:T(2,128)} %get-tuple-element.82.log_ref, ...), custom_call_target="tpu_custom_call" | custom-call | flops 16106127360 | bytes 8388608 | tf_op jit(solution)/shard_map/attend_back/pallas_call | solution.py:161
  500.2 7.3 %collective-permute-done.42.refs_4_ = bf16[2,3,64,512]{3,2,1,0:T(8,128)(2,1)S(1)} collective-permute-done((bf16[2,3,64,512]{3,2,1,0:T(8,128)(2,1)S(1)}, bf16[2,3,64,512]{3,2,1,0:T(8,128)(2,1)S(1)}, u32[]{:S(2)}, u32[]{:S(2)}) %collective-permute-start.42) | collective-permute-done | bytes 393248 | tf_op jit(solution)/shard_map/ppermute | solution.py:416
  511.9 4.8 fusion.8
  546.1 5.7 collective-permute-done.57
  565.6 6.6 %collective-permute-done.66.refs_3_ = bf16[2,3,64,512]{3,2,1,0:T(8,128)(2,1)S(1)} collective-permute-done((bf16[2,3,64,512]{3,2,1,0:T(8,128)(2,1)S(1)}, bf16[2,3,64,512]{3,2,1,0:T(8,128)(2,1)S(1)}, u32[]{:S(2)}, u32[]{:S(2)}) %collective-permute-start.66) | collective-permute-done | bytes 393248 | tf_op jit(solution)/shard_map/ppermute | solution.py:416
  572.2 8.5 %collective-permute-done.65.refs_2_ = bf16[2,3,64,512]{3,2,1,0:T(8,128)(2,1)S(1)} collective-permute-done((bf16[2,3,64,512]{3,2,1,0:T(8,128)(2,1)S(1)}, bf16[2,3,64,512]{3,2,1,0:T(8,128)(2,1)S(1)}, u32[]{:S(2)}, u32[]{:S(2)}) %collective-permute-start.65) | collective-permute-done | bytes 393248 | tf_op jit(solution)/shard_map/ppermute | solution.py:416
  (505 shorter events, 253.8 us)
Async XLA Ops:
  7.2 76.8 %all-gather.6.cloned.1.call-start = ((), (), s32[]{:S(2)}) async-start(), calls=%async_computation.2 | async-start | bytes 3342336 | tf_op jit(solution)/shard_map/all_gather | solution.py:556
  11.8 266.2 %all-gather.8.cloned.1.call-start = ((), (), s32[]{:S(2)}) async-start(), calls=%async_computation.5 | async-start | bytes 7864320 | tf_op jit(solution)/shard_map/all_gather | solution.py:598
  16.9 29.6 %collective-permute-start.11 = (f32[2,4,256]{2,1,0:T(4,128)}, f32[2,4,256]{2,1,0:T(4,128)S(1)}, u32[]{:S(2)}, u32[]{:S(2)}) collective-permute-start(f32[2,4,256]{2,1,0:T(4,128)} %get-tuple-element.165), channel_id=1, source_target_pairs={{0,6},{2,4},{4,2},{6,0},{8,14},{10,12},{12,10},{14,8},{16,22},{18,... | collective-permute-start | bytes 24584 | tf_op jit(solution)/shard_map/ppermute | solution.py:416
  17.6 29.0 %collective-permute-start.9 = (f32[2,4,256]{2,1,0:T(4,128)}, f32[2,4,256]{2,1,0:T(4,128)S(1)}, u32[]{:S(2)}, u32[]{:S(2)}) collective-permute-start(f32[2,4,256]{2,1,0:T(4,128)} %get-tuple-element.167), channel_id=1, source_target_pairs={{0,2},{2,0},{4,6},{6,4},{8,10},{10,8},{12,14},{14,12},{16,18},{18,... | collective-permute-start | bytes 24584 | tf_op jit(solution)/shard_map/ppermute | solution.py:416
  71.2 236.2 %all-gather.10.cloned.1.call-start = ((), (), s32[]{:S(2)}) async-start(), calls=%async_computation.6 | async-start | bytes 7864320 | tf_op jit(solution)/shard_map/all_gather | solution.py:598
  81.9 27.5 %collective-permute-start.23 = (bf16[512,1024]{1,0:T(8,128)(2,1)}, bf16[512,1024]{1,0:T(8,128)(2,1)}, u32[]{:S(2)}, u32[]{:S(2)}) collective-permute-start(bf16[512,1024]{1,0:T(8,128)(2,1)} %tie.13), channel_id=1, source_target_pairs={{0,4},{2,6},{4,0},{6,2},{8,12},{10,14},{12,8},{14,10},{16,20},{18,... | collective-permute-start | bytes 3145736 | tf_op jit(solution)/shard_map/ppermute | solution.py:416
  82.1 27.3 %collective-permute-start.22 = (bf16[512,1024]{1,0:T(8,128)(2,1)}, bf16[512,1024]{1,0:T(8,128)(2,1)}, u32[]{:S(2)}, u32[]{:S(2)}) collective-permute-start(bf16[512,1024]{1,0:T(8,128)(2,1)} %tie.13), channel_id=1, source_target_pairs={{0,1},{1,0},{2,3},{3,2},{4,5},{5,4},{6,7},{7,6},{8,9},{9,8},{10,11... | collective-permute-start | bytes 3145736 | tf_op jit(solution)/shard_map/ppermute | solution.py:416
  89.5 27.1 %collective-permute-start.25 = (bf16[2,3,64,512]{3,2,1,0:T(8,128)(2,1)}, bf16[2,3,64,512]{3,2,1,0:T(8,128)(2,1)S(1)}, u32[]{:S(2)}, u32[]{:S(2)}) collective-permute-start(bf16[2,3,64,512]{3,2,1,0:T(8,128)(2,1)} %get-tuple-element.64), channel_id=1, source_target_pairs={{0,4},{2,6},{4,0},{6,2},{8,12},{10,14},{12,8},{14,10},{16,20},{18,... | collective-permute-start | bytes 1179656 | tf_op jit(solution)/shard_map/ppermute | solution.py:416
  91.0 32.3 %collective-permute-start.26 = (bf16[2,3,64,512]{3,2,1,0:T(8,128)(2,1)}, bf16[2,3,64,512]{3,2,1,0:T(8,128)(2,1)S(1)}, u32[]{:S(2)}, u32[]{:S(2)}) collective-permute-start(bf16[2,3,64,512]{3,2,1,0:T(8,128)(2,1)} %get-tuple-element.65), channel_id=1, source_target_pairs={{0,6},{2,4},{4,2},{6,0},{8,14},{10,12},{12,10},{14,8},{16,22},{18,... | collective-permute-start | bytes 1179656 | tf_op jit(solution)/shard_map/ppermute | solution.py:416
  127.0 300.7 %reduce-scatter.3.cloned.1.call-start = ((), (), s32[]{:S(2)}) async-start(), calls=%async_computation.3 | async-start | bytes 7864320 | tf_op jit(solution)/shard_map/reduce_scatter | solution.py:632
  127.3 38.7 %collective-permute-start.30 = (bf16[512,1024]{1,0:T(8,128)(2,1)}, bf16[512,1024]{1,0:T(8,128)(2,1)}, u32[]{:S(2)}, u32[]{:S(2)}) collective-permute-start(bf16[512,1024]{1,0:T(8,128)(2,1)} %refs_1_.1), channel_id=1, source_target_pairs={{0,2},{2,0},{4,6},{6,4},{8,10},{10,8},{12,14},{14,12},{16,18},{18,... | collective-permute-start | bytes 3145736 | tf_op jit(solution)/shard_map/ppermute | solution.py:416
  164.9 29.0 %collective-permute-start.28 = (bf16[512,1024]{1,0:T(8,128)(2,1)}, bf16[512,1024]{1,0:T(8,128)(2,1)}, u32[]{:S(2)}, u32[]{:S(2)}) collective-permute-start(bf16[512,1024]{1,0:T(8,128)(2,1)} %get-tuple-element.67.refs_2_), channel_id=1, source_target_pairs={{0,4},{2,6},{4,0},{6,2},{8,12},{10,14},{12,8},{14,10},{16,20},{18,... | collective-permute-start | bytes 3145736 | tf_op jit(solution)/shard_map/ppermute | solution.py:416
  165.5 29.0 %collective-permute-start.31 = (bf16[512,1024]{1,0:T(8,128)(2,1)}, bf16[512,1024]{1,0:T(8,128)(2,1)}, u32[]{:S(2)}, u32[]{:S(2)}) collective-permute-start(bf16[512,1024]{1,0:T(8,128)(2,1)} %get-tuple-element.67.refs_2_), channel_id=1, source_target_pairs={{0,2},{2,0},{4,6},{6,4},{8,10},{10,8},{12,14},{14,12},{16,18},{18,... | collective-permute-start | bytes 3145736 | tf_op jit(solution)/shard_map/ppermute | solution.py:416
  165.5 28.5 %collective-permute-start.27 = (bf16[512,1024]{1,0:T(8,128)(2,1)}, bf16[512,1024]{1,0:T(8,128)(2,1)}, u32[]{:S(2)}, u32[]{:S(2)}) collective-permute-start(bf16[512,1024]{1,0:T(8,128)(2,1)} %get-tuple-element.66.refs_1_), channel_id=1, source_target_pairs={{0,2},{2,0},{4,6},{6,4},{8,10},{10,8},{12,14},{14,12},{16,18},{18,... | collective-permute-start | bytes 3145736 | tf_op jit(solution)/shard_map/ppermute | solution.py:416
  166.0 47.8 %collective-permute-start.12 = (bf16[512,1024]{1,0:T(8,128)(2,1)S(1)}, bf16[512,1024]{1,0:T(8,128)(2,1)}, u32[]{:S(2)}, u32[]{:S(2)}) collective-permute-start(bf16[512,1024]{1,0:T(8,128)(2,1)S(1)} %multiply_convert_fusion.refs_0_), channel_id=1, source_target_pairs={{0,4},{2,6},{4,0},{6,2},{8,12},{10,14},{12,8},{14,10},{16,20},{18,... | collective-permute-start | bytes 3145736 | tf_op jit(solution)/shard_map/ppermute | solution.py:416
  186.7 47.5 %collective-permute-start.15 = (bf16[512,1024]{1,0:T(8,128)(2,1)}, bf16[512,1024]{1,0:T(8,128)(2,1)}, u32[]{:S(2)}, u32[]{:S(2)}) collective-permute-start(bf16[512,1024]{1,0:T(8,128)(2,1)} %collective-permute-done.14.refs_1_), channel_id=1, source_target_pairs={{0,4},{2,6},{4,0},{6,2},{8,12},{10,14},{12,8},{14,10},{16,20},{18,... | collective-permute-start | bytes 3145736 | tf_op jit(solution)/shard_map/ppermute | solution.py:416
  193.9 58.3 %collective-permute-start.29 = (bf16[512,1024]{1,0:T(8,128)(2,1)}, bf16[512,1024]{1,0:T(8,128)(2,1)}, u32[]{:S(2)}, u32[]{:S(2)}) collective-permute-start(bf16[512,1024]{1,0:T(8,128)(2,1)} %collective-permute-done.28.refs_2_), channel_id=1, source_target_pairs={{0,2},{2,0},{4,6},{6,4},{8,10},{10,8},{12,14},{14,12},{16,18},{18,... | collective-permute-start | bytes 3145736 | tf_op jit(solution)/shard_map/ppermute | solution.py:416
  194.0 64.4 %collective-permute-start.17 = (bf16[512,1024]{1,0:T(8,128)(2,1)S(1)}, bf16[512,1024]{1,0:T(8,128)(2,1)}, u32[]{:S(2)}, u32[]{:S(2)}) collective-permute-start(bf16[512,1024]{1,0:T(8,128)(2,1)S(1)} %multiply_convert_fusion.refs_0_), channel_id=1, source_target_pairs={{0,2},{2,0},{4,6},{6,4},{8,10},{10,8},{12,14},{14,12},{16,18},{18,... | collective-permute-start | bytes 3145736 | tf_op jit(solution)/shard_map/ppermute | solution.py:416
  194.5 63.9 %collective-permute-start.18 = (bf16[512,1024]{1,0:T(8,128)(2,1)}, bf16[512,1024]{1,0:T(8,128)(2,1)}, u32[]{:S(2)}, u32[]{:S(2)}) collective-permute-start(bf16[512,1024]{1,0:T(8,128)(2,1)} %collective-permute-done.14.refs_1_), channel_id=1, source_target_pairs={{0,2},{2,0},{4,6},{6,4},{8,10},{10,8},{12,14},{14,12},{16,18},{18,... | collective-permute-start | bytes 3145736 | tf_op jit(solution)/shard_map/ppermute | solution.py:416
  213.8 56.3 %collective-permute-start.13 = (bf16[512,1024]{1,0:T(8,128)(2,1)}, bf16[512,1024]{1,0:T(8,128)(2,1)S(1)}, u32[]{:S(2)}, u32[]{:S(2)}) collective-permute-start(bf16[512,1024]{1,0:T(8,128)(2,1)} %collective-permute-done.12.refs_0_), channel_id=1, source_target_pairs={{0,2},{2,0},{4,6},{6,4},{8,10},{10,8},{12,14},{14,12},{16,18},{18,... | collective-permute-start | bytes 3145736 | tf_op jit(solution)/shard_map/ppermute | solution.py:416
  234.2 36.0 %collective-permute-start.16 = (bf16[512,1024]{1,0:T(8,128)(2,1)}, bf16[512,1024]{1,0:T(8,128)(2,1)S(1)}, u32[]{:S(2)}, u32[]{:S(2)}) collective-permute-start(bf16[512,1024]{1,0:T(8,128)(2,1)} %collective-permute-done.15.refs_1_), channel_id=1, source_target_pairs={{0,2},{2,0},{4,6},{6,4},{8,10},{10,8},{12,14},{14,12},{16,18},{18,... | collective-permute-start | bytes 3145736 | tf_op jit(solution)/shard_map/ppermute | solution.py:416
  306.8 251.7 %reduce-scatter.5.cloned.1.call-start = ((), (), s32[]{:S(2)}) async-start(), calls=%async_computation.4 | async-start | bytes 7864320 | tf_op jit(solution)/shard_map/reduce_scatter | solution.py:632
  353.4 26.3 %collective-permute-start.36 = (bf16[512,1024]{1,0:T(8,128)(2,1)}, bf16[512,1024]{1,0:T(8,128)(2,1)}, u32[]{:S(2)}, u32[]{:S(2)}) collective-permute-start(bf16[512,1024]{1,0:T(8,128)(2,1)} %put_rows.13.refs_4_), channel_id=1, source_target_pairs={{0,4},{2,6},{4,0},{6,2},{8,12},{10,14},{12,8},{14,10},{16,20},{18,... | collective-permute-start | bytes 3145736 | tf_op jit(solution)/shard_map/ppermute | solution.py:416
  358.7 42.9 %collective-permute-start.35 = (bf16[512,1024]{1,0:T(8,128)(2,1)}, bf16[512,1024]{1,0:T(8,128)(2,1)S(1)}, u32[]{:S(2)}, u32[]{:S(2)}) collective-permute-start(bf16[512,1024]{1,0:T(8,128)(2,1)} %put_rows.14.refs_5_), channel_id=1, source_target_pairs={{0,4},{2,6},{4,0},{6,2},{8,12},{10,14},{12,8},{14,10},{16,20},{18,... | collective-permute-start | bytes 3145736 | tf_op jit(solution)/shard_map/ppermute | solution.py:416
  417.4 58.2 %collective-permute-start.33 = (bf16[1024,1024]{1,0:T(8,128)(2,1)}, bf16[1024,1024]{1,0:T(8,128)(2,1)}, u32[]{:S(2)}, u32[]{:S(2)}) collective-permute-start(bf16[1024,1024]{1,0:T(8,128)(2,1)} %put_rows.15), channel_id=1, source_target_pairs={{0,2},{2,0},{4,6},{6,4},{8,10},{10,8},{12,14},{14,12},{16,18},{18,... | collective-permute-start | bytes 6291464 | tf_op jit(solution)/shard_map/ppermute | solution.py:416
  421.6 66.4 %collective-permute-start.44 = (bf16[512,1024]{1,0:T(8,128)(2,1)}, bf16[512,1024]{1,0:T(8,128)(2,1)}, u32[]{:S(2)}, u32[]{:S(2)}) collective-permute-start(bf16[512,1024]{1,0:T(8,128)(2,1)} %put_rows.21), channel_id=1, source_target_pairs={{0,4},{2,6},{4,0},{6,2},{8,12},{10,14},{12,8},{14,10},{16,20},{18,... | collective-permute-start | bytes 3145736 | tf_op jit(solution)/shard_map/ppermute | solution.py:416
  426.3 66.6 %collective-permute-start.45 = (bf16[512,1024]{1,0:T(8,128)(2,1)}, bf16[512,1024]{1,0:T(8,128)(2,1)}, u32[]{:S(2)}, u32[]{:S(2)}) collective-permute-start(bf16[512,1024]{1,0:T(8,128)(2,1)} %put_rows.22), channel_id=1, source_target_pairs={{0,4},{2,6},{4,0},{6,2},{8,12},{10,14},{12,8},{14,10},{16,20},{18,... | collective-permute-start | bytes 3145736 | tf_op jit(solution)/shard_map/ppermute | solution.py:416
  437.6 36.3 %collective-permute-start.59 = (bf16[4,2,64,512]{3,2,0,1:T(8,128)(2,1)S(1)}, bf16[4,2,64,512]{3,2,0,1:T(8,128)(2,1)S(1)}, u32[]{:S(2)}, u32[]{:S(2)}) collective-permute-start(bf16[4,2,64,512]{3,2,0,1:T(8,128)(2,1)S(1)} %fusion.31), channel_id=1, source_target_pairs={{0,2},{2,0},{4,6},{6,4},{8,10},{10,8},{12,14},{14,12},{16,18},{18,... | collective-permute-start | bytes 1572872 | tf_op jit(solution)/shard_map/ppermute | solution.py:416
  467.8 40.5 %collective-permute-start.39 = (bf16[512,1024]{1,0:T(8,128)(2,1)}, bf16[512,1024]{1,0:T(8,128)(2,1)}, u32[]{:S(2)}, u32[]{:S(2)}) collective-permute-start(bf16[512,1024]{1,0:T(8,128)(2,1)} %dynamic-slice_convert_fusion), channel_id=1, source_target_pairs={{0,1},{1,0},{2,3},{3,2},{4,5},{5,4},{6,7},{7,6},{8,9},{9,8},{10,11... | collective-permute-start | bytes 3145736 | tf_op jit(solution)/shard_map/ppermute | solution.py:416
  493.4 44.4 %collective-permute-start.63 = (bf16[64,512]{1,0:T(8,128)(2,1)}, bf16[64,512]{1,0:T(8,128)(2,1)}, u32[]{:S(2)}, u32[]{:S(2)}) collective-permute-start(bf16[64,512]{1,0:T(8,128)(2,1)} %get-tuple-element.158), channel_id=1, source_target_pairs={{0,24},{2,26},{4,28},{6,30},{8,0},{10,2},{12,4},{14,6},{16,8},{18,... | collective-permute-start | bytes 196616 | tf_op jit(solution)/shard_map/ppermute | solution.py:419
  497.0 39.4 %collective-permute-start.55 = (bf16[4,64,1024]{2,1,0:T(8,128)(2,1)}, bf16[4,64,1024]{2,1,0:T(8,128)(2,1)}, u32[]{:S(2)}, u32[]{:S(2)}) collective-permute-start(bf16[4,64,1024]{2,1,0:T(8,128)(2,1)} %fusion.30), channel_id=1, source_target_pairs={{0,4},{2,6},{4,0},{6,2},{8,12},{10,14},{12,8},{14,10},{16,20},{18,... | collective-permute-start | bytes 1572872 | tf_op jit(solution)/shard_map/ppermute | solution.py:416
  534.9 27.8 %collective-permute-start.46 = (bf16[512,1024]{1,0:T(8,128)(2,1)}, bf16[512,1024]{1,0:T(8,128)(2,1)S(1)}, u32[]{:S(2)}, u32[]{:S(2)}) collective-permute-start(bf16[512,1024]{1,0:T(8,128)(2,1)} %add_convert_fusion.1), channel_id=1, source_target_pairs={{0,1},{1,0},{2,3},{3,2},{4,5},{5,4},{6,7},{7,6},{8,9},{9,8},{10,11... | collective-permute-start | bytes 3145736 | tf_op jit(solution)/shard_map/ppermute | solution.py:416
  (124 other events, 1030.0 us)
Sparse Core Ops, SparseCore 0:
  11.9 50.6 all-gather.5
  71.3 115.3 all-gather.7
  188.3 113.5 all-gather.9
  306.9 110.4 reduce-scatter.2
  419.6 112.6 reduce-scatter.4

commit v3 on v2

--- a/solution.py
+++ b/solution.py
@@ -13,7 +13,8 @@
 SUB = 4
 TILE = 256
 NEG = -1e30
-CHUNKS = (2, 2)
+LANES = 128
+CHUNKS = (3, 1)
 VMEM_BYTES = 56 * 1024 * 1024
 BF = jnp.bfloat16
 F32 = jnp.float32
@@ -54,6 +55,33 @@
         name="tie",
     )(*leaves, *others)
     return jax.tree.unflatten(tree, outs)
+
+
+def move_kernel(plan, sources, at_ref, *refs):
+    outs, sems = refs[sources:-1], refs[-1]
+    copies = [
+        pltpu.make_async_copy(refs[i].at[taken], out.at[put_at], sems.at[number])
+        for number, (i, taken, out, put_at) in enumerate(plan(at_ref, outs))
+    ]
+    for copy in copies:
+        copy.start()
+    for copy in copies:
+        copy.wait()
+
+
+def move(at, sources, shapes, steps, plan, others=()):
+    anywhere = pl.BlockSpec(memory_space=pl.ANY)
+    operands = [*sources, *jax.tree.leaves(others)]
+    return pl.pallas_call(
+        functools.partial(move_kernel, plan, len(operands)),
+        in_specs=[pl.BlockSpec(memory_space=pltpu.SMEM)] + [anywhere] * len(operands),
+        out_specs=[pl.BlockSpec(memory_space=pltpu.VMEM)] * len(shapes),
+        out_shape=[jax.ShapeDtypeStruct(shape, BF) for shape in shapes],
+        scratch_shapes=[pltpu.SemaphoreType.DMA((steps,))],
+        compiler_params=params(),
+        cost_estimate=cost(0, 4 * sum(source.size for source in sources)),
+        name="move",
+    )(at, *operands)
 
 
 def fill_bias(bias, seg_row, seg_col):
@@ -186,29 +214,38 @@
     )(qkv, grads, attended, logs, segments.reshape(1, -1), segments.reshape(-1, 1))
 
 
-def pick_kernel(weighted, parts, index_ref, *refs):
-    tables, out_ref = refs[int(weighted) : int(weighted) + parts], refs[-1]
+def pick_kernel(weighted, parts, slot_ref, *refs):
+    tables, out_ref = refs[:parts], refs[-1]
+    cap = out_ref.shape[2]
+    expert = pl.program_id(0)
+
+    def column(which):
+        row = slot_ref[which, pl.ds(expert, 1), :]
+        return jnp.broadcast_to(row, (LANES, cap)).T
+
+    index = column(0)
+    lane = lax.broadcasted_iota(jnp.int32, (cap, LANES), 1).astype(F32)
     picked, start = None, 0
     for table in tables:
-        count = table.shape[0]
-        places = lax.broadcasted_iota(jnp.int32, (index_ref.shape[0], count), 1) + start
-        part = dot((places == index_ref[...]).astype(BF), table[...])
+        marks = [
+            (lane + float(start + at) == index).astype(BF)
+            for at in range(0, table.shape[0], LANES)
+        ]
+        part = dot(jnp.concatenate(marks, axis=1), table[...])
         picked = part if picked is None else picked + part
-        start += count
+        start += table.shape[0]
     if weighted:
-        picked = picked * refs[0][...]
+        picked = picked * column(1)[:, :1]
     out_ref[0, 0] = picked.astype(BF)
 
 
-def pick(tables, index_cols, weight_cols, experts):
-    cap = index_cols[0].shape[0] // experts
+def pick(tables, slots, weighted):
+    _, experts, cap = slots[0].shape
     width = tables[0][0].shape[1]
-    column = pl.BlockSpec((cap, 1), lambda e: (e, 0))
-    weighted = weight_cols is not None
     held = None
     for k, parts in enumerate(tables):
-        args = [index_cols[k]] + ([weight_cols[k]] if weighted else []) + list(parts)
-        specs = [column] * (len(args) - len(parts))
+        args = [slots[k], *parts]
+        specs = [pl.BlockSpec(slots[k].shape, lambda e: (0, 0, 0))]
         specs += [pl.BlockSpec(part.shape, lambda e: (0, 0)) for part in parts]
         length = sum(part.shape[0] for part in parts)
         if held is not None:
@@ -230,46 +267,50 @@
     return held
 
 
-def put_kernel(start, added, index_ref, *refs):
+def put_kernel(start, weighted, added, slot_ref, *refs):
     parts, out_ref = refs[: len(refs) - 1 - int(added)], refs[-1]
     cap = parts[0].shape[2]
     first = start + pl.program_id(0) * out_ref.shape[0]
-    total, at = (refs[-2][...].astype(F32) if added else None), 0
+    place = (lax.broadcasted_iota(jnp.int32, (out_ref.shape[0], cap), 0) + first).astype(F32)
+    total, at = None, 0
     for held in parts:
         for expert in range(held.shape[0]):
-            index = index_ref[:, at : at + cap]
-            marks = lax.broadcasted_iota(jnp.int32, (out_ref.shape[0], cap), 0) + first == index
-            part = dot(marks.astype(BF), held[expert, 0])
+            match = place == slot_ref[0, at : at + 1, :]
+            if weighted:
+                marks = jnp.where(match, slot_ref[1, at : at + 1, :], 0.0).astype(BF)
+            else:
+                marks = match.astype(BF)
+            part = dot(marks, held[expert, 0])
             total = part if total is None else total + part
-            at += cap
+            at += 1
+    if added:
+        total = total + refs[-2][...].astype(F32)
     out_ref[...] = total.astype(out_ref.dtype)
 
 
-def put(parts, index_row, which, start, count, addend=None, kind=BF):
-    slots = index_row.shape[1]
+def put(parts, slots, weighted, which, start, count, addends=(), kind=BF):
     cap, width = parts[0].shape[2:]
     tile = min(TILE, count)
-    in_specs = [pl.BlockSpec((1, slots), lambda r: (0, 0))]
+    in_specs = [pl.BlockSpec(slots.shape, lambda r: (0, 0, 0))]
     in_specs += [
         pl.BlockSpec((p.shape[0], 1, cap, width), lambda r: (0, which, 0, 0)) for p in parts
     ]
-    added = addend is not None
-    if added:
-        in_specs.append(pl.BlockSpec((tile, width), lambda r: (start // tile + r, 0)))
+    in_specs += [pl.BlockSpec((tile, width), lambda r: (start // tile + r, 0))] * len(addends)
+    moved = slots.shape[1] * cap
     return pl.pallas_call(
-        functools.partial(put_kernel, start, added),
+        functools.partial(put_kernel, start, weighted, bool(addends)),
         grid=(count // tile,),
         in_specs=in_specs,
         out_specs=pl.BlockSpec((tile, width), lambda r: (r, 0)),
         out_shape=jax.ShapeDtypeStruct((count, width), kind),
         compiler_params=params("arbitrary"),
-        cost_estimate=cost(2 * slots * count * width, 2 * (count + slots) * width),
+        cost_estimate=cost(2 * moved * count * width, 2 * (count + moved) * width),
         name="put_rows",
-    )(index_row, *parts, *([addend] if added else []))
+    )(slots, *parts, *addends)
 
 
 def expert_kernel(
-    weight_ref, picked, slot_grad, shards, slot_out, pick_grad, backs, acts, hid_grads
+    picked, slot_grad, shards, slot_out, pick_grad, backs, acts, hid_grads
 ):
     cap, width = picked.shape[2:]
     planes, deep = shards.shape[0], shards.shape[3]
@@ -279,14 +320,13 @@
 
     def one(k, carry):
         rows = pl.ds(pl.multiple_of(k * cap, cap), cap)
-        weight = weight_ref[0, rows, :]
         gate_pre = dot(picked[0, k], weights(0))
         up_pre = dot(picked[0, k], weights(1))
         sig = 1.0 / (1.0 + jnp.exp(-gate_pre))
         silu = gate_pre * sig
         act = (silu * up_pre).astype(BF)
         acts[rows, :] = act
-        slot_out[0, k] = (dot(act, weights(2), 1, 1) * weight).astype(BF)
+        slot_out[0, k] = dot(act, weights(2), 1, 1).astype(BF)
         inner = dot(slot_grad[0, k], weights(2))
         gate_grad = (inner * up_pre * sig * (1.0 + gate_pre * (1.0 - sig))).astype(BF)
         up_grad = (inner * silu).astype(BF)
@@ -308,7 +348,7 @@
         backs[plane, 0, 2] = dot(mine, acts[...], 0, 0).astype(BF)
 
 
-def run_experts(first, weight_col, picked, slot_grads, shards):
+def run_experts(first, picked, slot_grads, shards):
     planes, count, _, deep, _ = shards.shape
     cap, width = picked.shape[2:]
     slots = SUB * cap
@@ -318,7 +358,7 @@
     return pl.pallas_call(
         expert_kernel,
         grid=(count,),
-        in_specs=[pl.BlockSpec((1, slots, 1), lambda e: (first + e, 0, 0)), rows, rows, block],
+        in_specs=[rows, rows, block],
         out_specs=[out_rows, out_rows, block],
         out_shape=[jax.ShapeDtypeStruct((count, SUB, cap, width), BF)] * 2
         + [jax.ShapeDtypeStruct(shards.shape, BF)],
@@ -328,7 +368,7 @@
             18 * count * slots * width * FF, count * (8 * slots * width + 12 * width * FF)
         ),
         name="experts",
-    )(weight_col, picked, slot_grads, shards)
+    )(picked, slot_grads, shards)
 
 
 def place_kernel(first, experts, at_ref, *refs):
@@ -351,7 +391,7 @@
         copy.wait()
 
 
-def place(sub, pieces, first, experts, held):
+def place(at, pieces, first, experts, held):
     count, _, rows, _ = pieces[0].shape
     anywhere = pl.BlockSpec(memory_space=pl.ANY)
     in_specs = [pl.BlockSpec(memory_space=pltpu.SMEM)]
@@ -370,7 +410,7 @@
         compiler_params=params(),
         cost_estimate=cost(0, 18 * SUB * count * rows * FF),
         name="place_rows",
-    )(sub.astype(jnp.int32).reshape(1), *pieces, *held)
+    )(at, *pieces, *held)
 
 
 def norm_scale(values):
@@ -406,6 +446,7 @@
     planes = fsdp // SUB
     at_fsdp, at_tp = lax.axis_index("fsdp"), lax.axis_index("tp")
     sub, plane = at_fsdp % SUB, at_fsdp // SUB
+    at = jnp.stack([sub, plane]).astype(jnp.int32)
     heads_kv = w_key.shape[1] // HEAD_DIM
     group = w_query.shape[1] // w_key.shape[1]
     experts = slots.shape[1] // SUB
@@ -453,7 +494,9 @@
     def plane_finish(mine, begun):
         if tp == 2:
             beside, across = begun
-            first, third = (mine, beside), (across, swap(beside, 2))
+            cut = half // 2
+            corner = (swap(beside[:cut], 2), swap(across[cut:], 1, "tp"))
+            first, third = (mine, beside), (across, *corner)
         else:
             first = begun
             third = (swap(first[0], 2),)
@@ -462,19 +505,26 @@
     def plane_scatter(put_one):
         fourth, second = swap(put_one(3, 0, length), 1), swap(put_one(1, 0, length), 1)
         if tp == 2:
-            corner = put_one(2, half, half, fourth)
-            across = put_one(2, 0, half, fourth)
-            other = put_one(0, half, half, second, F32)
-            mine = put_one(0, 0, half, second, F32)
+            cut = half // 2
+            upper = swap(put_one(2, half, cut, (fourth,)), 2)
+            lower = swap(put_one(2, half + cut, cut, (fourth,)), 1, "tp")
+            across = swap(put_one(2, 0, cut, (fourth,)), 2)
+            beside = swap(put_one(0, half + cut, cut, (second,)), 1, "tp")
+            across_on = put_one(2, cut, cut, (fourth,), F32)
+            beside_on = put_one(0, half, cut, (second,), F32)
+            mine = put_one(0, 0, half, (second,), F32)
 
             def finish(got):
-                corner, across = got
-                beside = swap((other + corner.astype(F32)).astype(BF), 1, "tp")
-                return mine + across.astype(F32) + beside.astype(F32)
-
-            return (swap(corner, 2), swap(across, 2)), (corner, across), finish
-        third = put_one(2, 0, length, fourth)
-        first = put_one(0, 0, length, second, F32)
+                upper, lower, across, beside = got
+                beside_up = swap((beside_on + upper.astype(F32)).astype(BF), 1, "tp")
+                across_low = swap((across_on + lower.astype(F32)).astype(BF), 2)
+                over_y = jnp.concatenate([across, across_low]).astype(F32)
+                over_tp = jnp.concatenate([beside_up, beside]).astype(F32)
+                return mine + over_y + over_tp
+
+            return (upper, lower, across, beside), mine, finish
+        third = put_one(2, 0, length, (fourth,))
+        first = put_one(0, 0, length, (second,), F32)
 
         def finish(got):
             total = first + got.astype(F32)
@@ -487,7 +537,7 @@
         core, line = sub & 1, sub >> 1
         sent = lax.dynamic_index_in_dim(values, 1 - core, 2, keepdims=False)
         kept = lax.dynamic_index_in_dim(values, core, 2, keepdims=False)
-        values = kept.astype(F32) + swap(sent.astype(BF), 1).astype(F32)
+        values = halved = kept.astype(F32) + swap(sent.astype(BF), 1).astype(F32)
         sent = lax.dynamic_index_in_dim(values, 1 - line, 1, keepdims=False)
         kept = lax.dynamic_index_in_dim(values, line, 1, keepdims=False)
         values = kept + swap(sent.astype(BF), 2).astype(F32)
@@ -502,7 +552,7 @@
             )
             for r in range(1, planes)
         ]
-        return values, got, lambda got: sum([total] + [part.astype(F32) for part in got])
+        return halved, values, got, lambda got: sum([total] + [part.astype(F32) for part in got])
 
     def gain_scatter(values):
         values = values.reshape(2, planes, SUB, tp, -1)
@@ -515,15 +565,41 @@
         else:
             values = lax.psum_scatter(values, "tp", scatter_dimension=3)
         values = sum([block(sub, 2)] + [swap(block(sub ^ k, 2), k) for k in range(1, SUB)])
-        return values, lambda values: sum(
-            [lax.dynamic_index_in_dim(values, plane, 1, keepdims=False)]
-            + [
-                shift(
-                    lax.dynamic_index_in_dim(values, (plane + r) % planes, 1, keepdims=False), r
-                )
-                for r in range(1, planes)
-            ]
-        )
+        total = lax.dynamic_index_in_dim(values, plane, 1, keepdims=False)
+        got = [
+            shift(lax.dynamic_index_in_dim(values, (plane + r) % planes, 1, keepdims=False), r)
+            for r in range(1, planes)
+        ]
+        return values, got, lambda got: sum(got, total)
+
+    across = [[j + SUB * p for p in range(planes)] for j in range(SUB)]
+    chunks, taken = [], 0
+    for count in CHUNKS:
+        count = min(count, experts - taken)
+        if count:
+            chunks.append((taken, count))
+            taken += count
+
+    own_rows = w_gate.shape[0]
+    shapes = [(count, 3, own_rows, FF) for _, count in chunks for _ in range(SUB)]
+
+    def cut_plan(at, outs):
+        for number, (first, count) in enumerate(chunks):
+            for k in (3, 2, 1, 0):
+                for e in range(count):
+                    column = lax.bitwise_xor(at[0], k) * experts + (first + e)
+                    column = pl.multiple_of(column * FF, FF)
+                    for which in range(3):
+                        out = outs[number * SUB + k]
+                        yield which, (slice(None), pl.ds(column, FF)), out, (e, which)
+
+    sends = move(at, (w_gate, w_up, w_down), shapes, 3 * SUB * experts, cut_plan)
+    sends = [sends[i : i + SUB] for i in range(0, len(sends), SUB)]
+
+    def swap_all(pieces):
+        return [pieces[0]] + [swap(pieces[k], k) for k in range(1, SUB)]
+
+    first_pieces = swap_all(sends[0])
 
     if tp == 2:
         near_gains = swap(gains, 1, "tp")
@@ -535,6 +611,7 @@
     else:
         near_gains = lax.all_gather(gains, "tp", axis=1, tiled=True)
     whole_tokens = sequence_gather(tokens)
+    near_gains = tie(near_gains, sends[0][1:])
     plane_gains = jnp.concatenate(
         by_sub([near_gains] + [swap(near_gains, k) for k in range(1, SUB)]), axis=1
     )
@@ -559,130 +636,116 @@
     qkv_w, out_w = attn_w[:, :qkv_cols], attn_w[:, qkv_cols:]
 
     live = slots[0] >= 0
-    table = jnp.stack([slots[0].astype(F32), jnp.where(live, gate_values[0], 0.0)])
+    turned = jnp.where(live, (slots[0] + (length - turn)) % length, -1)
+    table = jnp.stack([turned.astype(F32), jnp.where(live, gate_values[0], 0.0)])
+    table = tie(table, plane_gains)
 
     def table_for(k):
         return lax.dynamic_slice_in_dim(table, (sub ^ k) * experts, experts, 1)
 
     tables = [table_for(0)] + [swap(table_for(k), k) for k in range(1, SUB)]
-    index = [t[0].astype(jnp.int32) for t in tables]
-    index = [jnp.where(v < 0, -1, (v + (length - turn)) % length) for v in index]
-    index_col = [v.reshape(-1, 1) for v in index]
-    index_row = [v.reshape(1, -1) for v in index]
-    slot_weight = [t[1] for t in tables]
-
-    across = [[j + SUB * p for p in range(planes)] for j in range(SUB)]
-    chunks, taken = [], 0
-    for count in CHUNKS:
-        count = min(count, experts - taken)
-        if count:
-            chunks.append((taken, count))
-            taken += count
-
-    def pieces_of(first, count, others):
-        def piece(k):
-            column = ((sub ^ k) * experts + first) * FF
-            cut = [
-                lax.dynamic_slice_in_dim(w, column, count * FF, 1).reshape(-1, count, FF)
-                for w in (w_gate, w_up, w_down)
-            ]
-            return jnp.stack(cut).transpose(2, 0, 1, 3)
-
-        sends = tie([piece(k) for k in range(1, SUB)], others)
-        return [piece(0)] + [swap(sent, k + 1) for k, sent in enumerate(sends)]
-
-    def shards_of(pieces, others=None):
-        if others is not None:
-            pieces = [pieces[0]] + tie(pieces[1:], others)
-        mine = jnp.concatenate(by_sub(pieces), axis=2)
+
+    def shards_of(pieces, others=()):
+        count = pieces[0].shape[0]
+
+        def plan(at, outs):
+            for k in range(SUB):
+                row = pl.multiple_of(lax.bitwise_xor(at[0], k) * own_rows, own_rows)
+                taken = (slice(None), slice(None), pl.ds(row, own_rows))
+                yield k, (slice(None),), outs[0], taken
+
+        (mine,) = move(at, pieces, [(count, 3, SUB * own_rows, FF)], SUB, plan, others)
         return lax.all_gather(mine, "fsdp", axis_index_groups=across), mine
 
-    held, mine_first = shards_of(
-        pieces_of(*chunks[0], (plane_gains, tables)), (all_gains, whole_tokens)
-    )
+    held, mine_first = shards_of(first_pieces, (all_gains, whole_tokens))
     shards = [held]
 
     whole_resid = whole_tokens.astype(F32)
     first_low = (whole_resid * norm_scale(whole_resid) * all_gains[0]).astype(BF)
     begun = plane_start(tie(cotangent, mine_first))
+    first_low = tie(first_low, tables)
     qkv = dot(qkv_w, first_low, 0, 1).astype(BF)
-    later = [pieces_of(*chunk, qkv) for chunk in chunks[1:]]
     attended, logs = attend(qkv, segments, heads_kv, group)
-    begun, later = tie((begun, later), attended)
-    shards += [shards_of(pieces)[0] for pieces in later]
+    attended = tie(attended, begun)
     cots = plane_finish(cotangent, begun)
     resid = tokens.astype(F32)
-    hidden = resid + sequence_scatter(dot(attended, out_w, 0, 1))
+    attn_part = dot(attended, out_w, 0, 1)
+    later = [swap_all(tie(sent, attended)) for sent in sends[1:]]
+    if tp == 2:
+        got = swap(part_of(attn_part, 1 - at_tp).astype(BF), 1, "tp")
+        got = tie(got, cots[2])
+        hidden = resid + (part_of(attn_part, at_tp) + got.astype(F32))
+    else:
+        hidden = resid + sequence_scatter(attn_part)
     scale_two = norm_scale(hidden)
     second_low = (hidden * scale_two * all_gains[1]).astype(BF)
 
-    slot_grads = pick(
-        cots, index_col, [w.reshape(-1, 1) for w in slot_weight], experts
-    )
-    picked = pick(
-        plane_finish(second_low, plane_start(second_low)), index_col, None, experts
-    )
-    weight_col = jnp.stack(slot_weight, axis=1).reshape(experts, -1, 1)
-    slot_outs, pick_grads, sums = [], [], []
-    for (first, count), held in zip(chunks, shards):
-        slot_out, pick_grad, backs = run_experts(first, weight_col, picked, slot_grads, held)
+    slot_grads = pick(cots, tables, True)
+    begun, later = tie((plane_start(second_low), later), slot_grads)
+    shards += [shards_of(pieces)[0] for pieces in later]
+    picked = pick(plane_finish(second_low, begun), tables, False)
+
+    sums, slot_outs, pick_grads = [], [], []
+    for number, ((first, count), held) in enumerate(zip(chunks, shards)):
+        slot_out, pick_grad, backs = run_experts(first, picked, slot_grads, held)
         slot_outs.append(slot_out)
         pick_grads.append(pick_grad)
         sums.append(
             lax.psum_scatter(backs, "fsdp", scatter_dimension=0, axis_index_groups=across)
         )
-    got, sent, finish = plane_scatter(lambda k, *more: put(pick_grads, index_row[k], k, *more))
+
+    got, sent, finish = plane_scatter(
+        lambda k, *more: put(pick_grads, tables[k], False, k, *more)
+    )
     second_grad = finish(got)
-    index_row = tie(index_row, sent)
+    late_tables = tie(tables, sent)
     got_out, _, finish_out_sum = plane_scatter(
-        lambda k, *more: put(slot_outs, index_row[k], k, *more)
+        lambda k, *more: put(slot_outs, late_tables[k], True, k, *more)
     )
 
     back_two, second_gain = norm_backward(hidden, scale_two, all_gains[1], second_grad)
     grad_hidden = cotangent.astype(F32) + back_two
     own_low = grad_hidden.astype(BF)
 
-    def rows_out(part):
-        part = part.reshape(-1, 3, SUB, rows, FF)
-        return [
-            lax.dynamic_index_in_dim(part, sub ^ k, 2, keepdims=False) for k in range(SUB)
-        ]
-
-    early = []
-    for part in sums[:-1]:
-        own, *sends = rows_out(part)
-        early.append((own, tie(sends, own_low)))
-    if tp == 2:
-        other_low = tie(swap(own_low, 1, "tp"), early)
-        hidden_low = ordered(own_low, other_low)
-    else:
-        hidden_low = lax.all_gather(own_low, "tp", axis=0, tiled=True)
-    early = [[own] + [swap(sent, k + 1) for k, sent in enumerate(sends)] for own, sends in early]
-    _, got_grad_out, finish_out = weight_scatter(dot(hidden_low, attended, 0, 1))
+    def rows_out(part, others=()):
+        part = part.reshape(-1, 3, SUB * rows, FF)
+
+        def plan(at, outs):
+            for k in (3, 2, 1, 0):
+                row = pl.multiple_of(lax.bitwise_xor(at[0], k) * rows, rows)
+                taken = (slice(None), slice(None), pl.ds(row, rows))
+                yield 0, taken, outs[k], (slice(None),)
+
+        shapes = [(part.shape[0], 3, rows, FF)] * SUB
+        return move(at, (part,), shapes, SUB, plan, others)
+
+    hidden_low = sequence_gather(own_low)
+    _, _, got_grad_out, finish_out = weight_scatter(dot(hidden_low, attended, 0, 1))
     attended_grad = dot(out_w, hidden_low, 0, 1).astype(BF)
     qkv_grad = attend_back(qkv, attended_grad, attended, logs, segments, heads_kv, group)
     grad_qkv = dot(first_low, qkv_grad, 0, 1)
     first_part = dot(qkv_grad, qkv_w, 0, 1)
     if tp == 2:
         got = swap(part_of(first_part, 1 - at_tp).astype(BF), 1, "tp")
-        got, early, got_out = tie((got, early, got_out), ())
         first_grad = part_of(first_part, at_tp) + got.astype(F32)
     else:
         first_grad = sequence_scatter(first_part)
-    mixed = (hidden + finish_out_sum(got_out)).astype(BF)
+    back_one, first_gain = norm_backward(resid, norm_scale(resid), all_gains[0], first_grad)
+    grad_tokens = grad_hidden + back_one
+    mixed = (hidden + finish_out_sum(tie(got_out, first_gain))).astype(BF)
+    grad_gains, got_gains, finish_gains = gain_scatter(jnp.stack([first_gain, second_gain]))
+    halved, grad_qkv, got_qkv, finish_qkv = weight_scatter(grad_qkv)
+
+    early = [swap_all(rows_out(part, halved)) for part in sums[:-1]]
+    late = rows_out(sums[-1], (grad_qkv, grad_gains, early))
+    got_grad_out, got_qkv, got_gains = tie((got_grad_out, got_qkv, got_gains), late[1:])
+    late = swap_all(late)
     expert_grads = None
     for number, pieces in enumerate(early):
-        expert_grads = place(sub, pieces, chunks[number][0], experts, expert_grads)
-    back_one, first_gain = norm_backward(resid, norm_scale(resid), all_gains[0], first_grad)
-    grad_tokens = grad_hidden + back_one
-    grad_gains, finish_gains = gain_scatter(jnp.stack([first_gain, second_gain]))
-    grad_qkv, got_qkv, finish_qkv = weight_scatter(grad_qkv)
-    grad_out = finish_out(tie(got_grad_out, grad_qkv))
-
-    own, *sends = rows_out(tie(sums[-1], (grad_qkv, grad_gains)))
-    late = [own] + [swap(sent, k + 1) for k, sent in enumerate(sends)]
-    expert_grads = place(sub, late, chunks[-1][0], experts, expert_grads)
-    grad_gains = finish_gains(grad_gains)
+        expert_grads = place(at, pieces, chunks[number][0], experts, expert_grads)
+    expert_grads = place(at, late, chunks[-1][0], experts, expert_grads)
+    grad_out = finish_out(got_grad_out)
+    grad_gains = finish_gains(got_gains)
     grad_qkv = finish_qkv(got_qkv).reshape(rows, heads_kv, -1)
     cut = group * HEAD_DIM
     return (

time: 598 us -> 575 us (0.962)
  Pallas kernels: 205 us -> 234 us
  other arithmetic: 60.4 us -> 36.7 us
  waiting for transfers between devices: 172 us -> 154 us
  local copies, waits for them, and re-layouts: 54.5 us -> 39.8 us
    ppermute x55 -> x65, waiting for transfers between devices: 154 us -> 108 us  [swap(): return lax.ppermute(values, axis, [(i, i ^ mask) for i in range(size)])]
    pallas_call x14 -> x25, Pallas kernels: 112 us -> 146 us  [the longest x18 69.6 us: put(): pl.pallas_call(functools.partial(put_kernel, start, weighted, bool(addend...]
    all_gather x2, waiting for transfers between devices: 0.01 us -> 26.8 us  [shards_of(): return (lax.all_gather(mine, 'fsdp', axis_index_groups=across), mine)]
    ppermute x55 -> x65, starting transfers between devices: 40.2 us -> 50.8 us  [swap(): return lax.ppermute(values, axis, [(i, i ^ mask) for i in range(size)])]
    select_n x7 -> x0, other arithmetic: 8.15 us -> none  [layer(): jnp.where(v < 0, -1, (v + (length - turn)) % length)]
    ppermute x12, starting transfers between devices: 20.6 us -> 13 us  [shift(): lax.ppermute(values, 'fsdp', [(i, (i + planes_on * SUB) % fsdp) for i in...]
    another operation x48 -> x0, local copies, waits for them, and re-layouts: 6.78 us -> none  [piece(): return jnp.stack(cut).transpose(2, 0, 1, 3)]
    transpose x7 -> x0, other arithmetic: 6.71 us -> none  [piece(): return jnp.stack(cut).transpose(2, 0, 1, 3)]
  transfers between devices with their start and end apart: 72 -> 82, of which waited for: 25 -> 24; matrix products, arithmetic and copies ran while one was open for 20% -> 14% of each run, Pallas kernels for 34% -> 41%
where the time goes in v3:
time: 575 us; the launch traced here: 568 us
  Pallas kernels  234 us (41%)
  waiting for transfers between devices  154 us (27%)
  starting transfers between devices  64 us (11%)
  local copies, waits for them, and re-layouts  39.8 us (7%)
  other arithmetic  36.7 us (6%)
  matrix products  23.8 us (4%)
  between operations  15.3 us (3%)
    ppermute x65, waiting for transfers between devices, swap(): return lax.ppermute(values, axis, [(i, i ^ mask) for i in range(size)])  108 us
    pallas_call x18, Pallas kernels, put(): pl.pallas_call(functools.partial(put_kernel, start, weighted, bool(addend...  69.6 us
    pallas_call x2, Pallas kernels, run_experts(): pl.pallas_call(expert_kernel, grid=(count,), in_specs=[rows, rows, block]...  57.4 us
    ppermute x65, starting transfers between devices, swap(): return lax.ppermute(values, axis, [(i, i ^ mask) for i in range(size)])  50.8 us
    pallas_call x8, Pallas kernels, pick(): pl.pallas_call(functools.partial(pick_kernel, weighted, len(parts)), grid...  44.2 us
    all_gather x2, waiting for transfers between devices, shards_of(): return (lax.all_gather(mine, 'fsdp', axis_index_groups=across), mine)  26.8 us
    dot_general x6, matrix products, dot(): lax.dot_general(left, right, (((left_dim,), (right_dim,)), ((), ())), pre...  23.8 us
    pallas_call x1, Pallas kernels, attend_back(): pl.pallas_call(functools.partial(attend_back_kernel, group), grid=(heads_...  19.9 us
  transfers between devices with their start and end apart: 82, of which 24 were waited for; matrix products, arithmetic and copies ran while one was open for 14% of the time, Pallas kernels for 41%

profile of v3, /device:TPU:0, one launch (start us, length us, event | category | flops | bytes accessed | tf_op | source)
XLA Modules:
  0.0 568.0 jit_solution(13323728246189634295)
XLA Ops:
  15.1 4.8 move.5
  42.3 14.3 %collective-permute-done = bf16[512,1024]{1,0:T(8,128)(2,1)S(1)} collective-permute-done((bf16[512,1024]{1,0:T(8,128)(2,1)S(1)}, bf16[512,1024]{1,0:T(8,128)(2,1)S(1)}, u32[]{:S(2)}, u32[]{:S(2)}) %collective-permute-start) | collective-permute-done | bytes 1048608 | tf_op jit(solution)/shard_map/ppermute | solution.py:457
  58.4 7.7 %collective-permute-done.13.refs_3_ = bf16[3,3,64,512]{3,2,1,0:T(8,128)(2,1)} collective-permute-done((bf16[3,3,64,512]{3,2,1,0:T(8,128)(2,1)}, bf16[3,3,64,512]{3,2,1,0:T(8,128)(2,1)}, u32[]{:S(2)}, u32[]{:S(2)}) %collective-permute-start.13) | collective-permute-done | bytes 589856 | tf_op jit(solution)/shard_map/ppermute | solution.py:457
  82.3 6.1 %convolution_convert_fusion.qkv_ref = bf16[1024,1024]{1,0:T(8,128)(2,1)} fusion(bf16[1024,1024]{1,0:T(8,128)(2,1)} %tie.13, bf16[1024,1536]{1,0:T(8,128)(2,1)} %all-gather.6.cloned.1.call-done), kind=kOutput, calls=%fused_computation.33 | convolution fusion | flops 2148532224 | bytes 6291456 | tf_op jit(solution)/shard_map/dot_general | solution.py:34
  88.4 18.2 %attend.1 = (bf16[512,1024]{1,0:T(8,128)(2,1)}, f32[4,2,1024]{2,1,0:T(2,128)}) custom-call(bf16[1024,1024]{1,0:T(8,128)(2,1)} %convolution_convert_fusion.qkv_ref, s32[1,1024]{1,0:T(1,128)} %bitcast.118, s32[1024,1]{1,0:T(8,128)} %copy.80.seg_col), custom_call_target="tpu_custom_call" | custom-call | flops 6442450944 | bytes 4194304 | tf_op jit(solution)/shard_map/attend/pallas_call | solution.py:125
  118.2 9.8 %collective-permute-done.17.refs_2_.refs_1_ = bf16[256,1024]{1,0:T(8,128)(2,1)S(1)} collective-permute-done((bf16[256,1024]{1,0:T(8,128)(2,1)}, bf16[256,1024]{1,0:T(8,128)(2,1)S(1)}, u32[]{:S(2)}, u32[]{:S(2)}) %collective-permute-start.17) | collective-permute-done | bytes 524320 | tf_op jit(solution)/shard_map/ppermute | solution.py:457
  128.0 19.9 %collective-permute-done.18.refs_3_.refs_2_ = bf16[256,1024]{1,0:T(8,128)(2,1)S(1)} collective-permute-done((bf16[256,1024]{1,0:T(8,128)(2,1)}, bf16[256,1024]{1,0:T(8,128)(2,1)S(1)}, u32[]{:S(2)}, u32[]{:S(2)}) %collective-permute-start.18) | collective-permute-done | bytes 524320 | tf_op jit(solution)/shard_map/ppermute | solution.py:457
  154.5 5.5 pick_rows.8.refs_2_
  160.0 5.5 pick_rows.9.refs_3_
  165.6 5.5 pick_rows.10.refs_3_
  172.9 5.5 pick_rows.11.refs_6_.slot_grad
  193.9 10.5 %collective-permute-done.30.refs_1_ = bf16[256,1024]{1,0:T(8,128)(2,1)S(1)} collective-permute-done((bf16[256,1024]{1,0:T(8,128)(2,1)S(1)}, bf16[256,1024]{1,0:T(8,128)(2,1)S(1)}, u32[]{:S(2)}, u32[]{:S(2)}) %collective-permute-start.30) | collective-permute-done | bytes 524320 | tf_op jit(solution)/shard_map/ppermute | solution.py:457
  206.3 5.7 %pick_rows.12.refs_2_ = bf16[4,4,256,1024]{3,2,1,0:T(8,128)(2,1)} custom-call(f32[2,4,256]{2,1,0:T(4,128)} %get-tuple-element.151.refs_1_.slot_ref.refs_0_, bf16[512,1024]{1,0:T(8,128)(2,1)} %copy-done.16, bf16[512,1024]{1,0:T(8,128)(2,1)} %get-tuple-element.81.refs_1_), custom_call_target="tpu_custom_call" | custom-call | flops 2147483648 | bytes 4194304 | tf_op jit(solution)/shard_map/pick_rows/pallas_call | solution.py:254
  214.0 5.5 pick_rows.13.refs_3_
  219.5 5.5 pick_rows.14.refs_3_
  226.1 5.5 pick_rows.15.picked
  235.6 40.5 %experts.2 = (bf16[3,4,256,1024]{3,2,1,0:T(8,128)(2,1)}, bf16[3,4,256,1024]{3,2,1,0:T(8,128)(2,1)}, bf16[4,3,3,256,512]{4,3,2,1,0:T(8,128)(2,1)}) custom-call(bf16[4,4,256,1024]{3,2,1,0:T(8,128)(2,1)} %pick_rows.15.picked, bf16[4,4,256,1024]{3,2,1,0:T(8,128)(2,1)} %pick_rows.11.refs_6_.slot_grad, bf16[4,3,3,256,512]{4,3,2,1,0:T(8,128)(2,1)} %bitcast.129), custom_call_target="tpu_custom_call" | custom-call | flops 28991029248 | bytes 44040192 | tf_op jit(solution)/shard_map/experts/pallas_call | solution.py:358
  276.1 22.8 %all-gather.10.cloned.1.call-done = bf16[4,3,256,512]{3,2,1,0:T(8,128)(2,1)} async-done(((bf16[1,3,256,512]{3,2,1,0:T(8,128)(2,1)}), bf16[4,3,256,512]{3,2,1,0:T(8,128)(2,1)}) %all-gather.10.cloned.1.call-update) | async-done | bytes 3145744 | tf_op jit(solution)/shard_map/all_gather | solution.py:658
  298.9 16.9 %experts.3 = (bf16[1,4,256,1024]{3,2,1,0:T(8,128)(2,1)}, bf16[1,4,256,1024]{3,2,1,0:T(8,128)(2,1)}, bf16[4,1,3,256,512]{4,3,2,1,0:T(8,128)(2,1)}) custom-call(bf16[4,4,256,1024]{3,2,1,0:T(8,128)(2,1)} %pick_rows.15.picked, bf16[4,4,256,1024]{3,2,1,0:T(8,128)(2,1)} %pick_rows.11.refs_6_.slot_grad, bf16[4,1,3,256,512]{4,3,2,1,0:T(8,128)(2,1)} %bitcast.130), custom_call_target="tpu_custom_call" | custom-call | flops 9663676416 | bytes 14680064 | tf_op jit(solution)/shard_map/experts/pallas_call | solution.py:358
  315.8 5.3 put_rows.27
  321.2 5.4 put_rows.18
  364.5 5.3 put_rows.22
  369.8 5.7 put_rows.20
  401.9 5.0 collective-permute-done.50
  410.0 4.8 convolution_convert_fusion.1.grad_ref
  414.8 19.9 %attend_back.1 = bf16[1024,1024]{1,0:T(8,128)(2,1)} custom-call(bf16[1024,1024]{1,0:T(8,128)(2,1)} %convolution_convert_fusion.qkv_ref, bf16[512,1024]{1,0:T(8,128)(2,1)} %convolution_convert_fusion.1.grad_ref, bf16[512,1024]{1,0:T(8,128)(2,1)} %tie.15.refs_4_.out_ref, f32[4,2,1024]{2,1,0:T(2,128)} %get-tuple-element.94.log_ref, s32[1,1024]{1,0:T(1,128)} %bitcast.119, ...), custom_call_target="tpu_custom_call" | custom-call | flops 16106127360 | bytes 8388608 | tf_op jit(solution)/shard_map/attend_back/pallas_call | solution.py:189
  434.7 4.7 fusion.12
  460.4 5.6 collective-permute-done.51
  498.6 7.2 %collective-permute-done.61.refs_1_ = bf16[64,512]{1,0:T(8,128)(2,1)S(1)} collective-permute-done((bf16[64,512]{1,0:T(8,128)(2,1)S(1)}, bf16[64,512]{1,0:T(8,128)(2,1)S(1)}, u32[]{:S(2)}, u32[]{:S(2)}) %collective-permute-start.61) | collective-permute-done | bytes 65568 | tf_op jit(solution)/shard_map/ppermute | solution.py:460
  514.8 5.7 %fusion.10 = (f32[512,1024]{1,0:T(8,128)}, bf16[512,1024]{1,0:T(8,128)(2,1)}) fusion(bf16[512,1024]{1,0:T(8,128)(2,1)S(1)} %copy-done.7, f32[512]{0:T(512)S(1)} %copy-done.75, f32[1024]{0:T(1024)S(1)} %bitcast.112, f32[512]{0:T(512)S(1)} %copy-done.70, bf16[512,1024]{1,0:T(8,128)(2,1)} %collective-permute-done.51, f32[1024,1024]{1,0:T(8,128)} %copy-done.13, ...), kind=kLoop, calls=%fused_computation.17 | loop fusion | flops 16777216 | bytes 16793604 | tf_op jit(solution)/shard_map/add | solution.py:734
  520.5 9.9 %collective-permute-done.72.refs_5_.refs_2_ = bf16[3,3,64,512]{3,2,1,0:T(8,128)(2,1)} collective-permute-done((bf16[3,3,64,512]{3,2,1,0:T(8,128)(2,1)S(1)}, bf16[3,3,64,512]{3,2,1,0:T(8,128)(2,1)}, u32[]{:S(2)}, u32[]{:S(2)}) %collective-permute-start.72) | collective-permute-done | bytes 589856 | tf_op jit(solution)/shard_map/ppermute | solution.py:457
  531.9 7.8 %collective-permute-done.73.refs_6_.refs_3_ = bf16[3,3,64,512]{3,2,1,0:T(8,128)(2,1)} collective-permute-done((bf16[3,3,64,512]{3,2,1,0:T(8,128)(2,1)S(1)}, bf16[3,3,64,512]{3,2,1,0:T(8,128)(2,1)}, u32[]{:S(2)}, u32[]{:S(2)}) %collective-permute-start.73) | collective-permute-done | bytes 589856 | tf_op jit(solution)/shard_map/ppermute | solution.py:457
  (445 shorter events, 244.9 us)
Async XLA Ops:
  7.2 75.1 %all-gather.6.cloned.1.call-start = ((), (), s32[]{:S(2)}) async-start(), calls=%async_computation.2 | async-start | bytes 3342336 | tf_op jit(solution)/shard_map/all_gather | solution.py:633
  11.5 224.1 %all-gather.8.cloned.1.call-start = ((), (), s32[]{:S(2)}) async-start(), calls=%async_computation.5 | async-start | bytes 11796480 | tf_op jit(solution)/shard_map/all_gather | solution.py:658
  29.4 29.0 %collective-permute-start.11 = (bf16[3,3,64,512]{3,2,1,0:T(8,128)(2,1)}, bf16[3,3,64,512]{3,2,1,0:T(8,128)(2,1)S(1)}, u32[]{:S(2)}, u32[]{:S(2)}) collective-permute-start(bf16[3,3,64,512]{3,2,1,0:T(8,128)(2,1)} %get-tuple-element.67.refs_1_), channel_id=1, source_target_pairs={{0,2},{2,0},{4,6},{6,4},{8,10},{10,8},{12,14},{14,12},{16,18},{18,... | collective-permute-start | bytes 1769480 | tf_op jit(solution)/shard_map/ppermute | solution.py:457
  29.4 29.0 %collective-permute-start.12 = (bf16[3,3,64,512]{3,2,1,0:T(8,128)(2,1)}, bf16[3,3,64,512]{3,2,1,0:T(8,128)(2,1)}, u32[]{:S(2)}, u32[]{:S(2)}) collective-permute-start(bf16[3,3,64,512]{3,2,1,0:T(8,128)(2,1)} %get-tuple-element.68.refs_2_), channel_id=1, source_target_pairs={{0,4},{2,6},{4,0},{6,2},{8,12},{10,14},{12,8},{14,10},{16,20},{18,... | collective-permute-start | bytes 1769480 | tf_op jit(solution)/shard_map/ppermute | solution.py:457
  30.3 35.9 %collective-permute-start.13 = (bf16[3,3,64,512]{3,2,1,0:T(8,128)(2,1)}, bf16[3,3,64,512]{3,2,1,0:T(8,128)(2,1)}, u32[]{:S(2)}, u32[]{:S(2)}) collective-permute-start(bf16[3,3,64,512]{3,2,1,0:T(8,128)(2,1)} %get-tuple-element.69.refs_3_), channel_id=1, source_target_pairs={{0,6},{2,4},{4,2},{6,0},{8,14},{10,12},{12,10},{14,8},{16,22},{18,... | collective-permute-start | bytes 1769480 | tf_op jit(solution)/shard_map/ppermute | solution.py:457
  31.3 25.3 %collective-permute-start = (bf16[512,1024]{1,0:T(8,128)(2,1)S(1)}, bf16[512,1024]{1,0:T(8,128)(2,1)S(1)}, u32[]{:S(2)}, u32[]{:S(2)}) collective-permute-start(bf16[512,1024]{1,0:T(8,128)(2,1)S(1)} %copy-done.6), channel_id=1, source_target_pairs={{0,1},{1,0},{2,3},{3,2},{4,5},{5,4},{6,7},{7,6},{8,9},{9,8},{10,11... | collective-permute-start | bytes 3145736 | tf_op jit(solution)/shard_map/ppermute | solution.py:457
  70.1 228.8 %all-gather.10.cloned.1.call-start = ((), (), s32[]{:S(2)}) async-start(), calls=%async_computation.6 | async-start | bytes 3932160 | tf_op jit(solution)/shard_map/all_gather | solution.py:658
  78.0 28.6 %collective-permute-start.14 = (bf16[512,1024]{1,0:T(8,128)(2,1)}, bf16[512,1024]{1,0:T(8,128)(2,1)}, u32[]{:S(2)}, u32[]{:S(2)}) collective-permute-start(bf16[512,1024]{1,0:T(8,128)(2,1)} %tie.14), channel_id=1, source_target_pairs={{0,1},{1,0},{2,3},{3,2},{4,5},{5,4},{6,7},{7,6},{8,9},{9,8},{10,11... | collective-permute-start | bytes 3145736 | tf_op jit(solution)/shard_map/ppermute | solution.py:457
  78.6 28.0 %collective-permute-start.15 = (bf16[512,1024]{1,0:T(8,128)(2,1)}, bf16[512,1024]{1,0:T(8,128)(2,1)}, u32[]{:S(2)}, u32[]{:S(2)}) collective-permute-start(bf16[512,1024]{1,0:T(8,128)(2,1)} %tie.14), channel_id=1, source_target_pairs={{0,4},{2,6},{4,0},{6,2},{8,12},{10,14},{12,8},{14,10},{16,20},{18,... | collective-permute-start | bytes 3145736 | tf_op jit(solution)/shard_map/ppermute | solution.py:457
  110.8 37.1 %collective-permute-start.16 = (bf16[512,1024]{1,0:T(8,128)(2,1)}, bf16[512,1024]{1,0:T(8,128)(2,1)S(1)}, u32[]{:S(2)}, u32[]{:S(2)}) collective-permute-start(bf16[512,1024]{1,0:T(8,128)(2,1)} %dynamic-slice_convert_fusion.1), channel_id=1, source_target_pairs={{0,1},{1,0},{2,3},{3,2},{4,5},{5,4},{6,7},{7,6},{8,9},{9,8},{10,11... | collective-permute-start | bytes 3145736 | tf_op jit(solution)/shard_map/ppermute | solution.py:457
  117.1 30.8 %collective-permute-start.18 = (bf16[256,1024]{1,0:T(8,128)(2,1)}, bf16[256,1024]{1,0:T(8,128)(2,1)S(1)}, u32[]{:S(2)}, u32[]{:S(2)}) collective-permute-start(bf16[256,1024]{1,0:T(8,128)(2,1)} %slice.52), channel_id=1, source_target_pairs={{0,1},{1,0},{2,3},{3,2},{4,5},{5,4},{6,7},{7,6},{8,9},{9,8},{10,11... | collective-permute-start | bytes 1572872 | tf_op jit(solution)/shard_map/ppermute | solution.py:457
  117.7 36.3 %collective-permute-start.27 = (bf16[512,1024]{1,0:T(8,128)(2,1)}, bf16[512,1024]{1,0:T(8,128)(2,1)}, u32[]{:S(2)}, u32[]{:S(2)}) collective-permute-start(bf16[512,1024]{1,0:T(8,128)(2,1)} %refs_0_.4), channel_id=1, source_target_pairs={{0,2},{2,0},{4,6},{6,4},{8,10},{10,8},{12,14},{14,12},{16,18},{18,... | collective-permute-start | bytes 3145736 | tf_op jit(solution)/shard_map/ppermute | solution.py:457
  117.7 53.3 %collective-permute-start.24 = (bf16[512,1024]{1,0:T(8,128)(2,1)}, bf16[512,1024]{1,0:T(8,128)(2,1)}, u32[]{:S(2)}, u32[]{:S(2)}) collective-permute-start(bf16[512,1024]{1,0:T(8,128)(2,1)} %collective-permute-done.15.refs_2_.refs_1_.refs_0_), channel_id=1, source_target_pairs={{0,2},{2,0},{4,6},{6,4},{8,10},{10,8},{12,14},{14,12},{16,18},{18,... | collective-permute-start | bytes 3145736 | tf_op jit(solution)/shard_map/ppermute | solution.py:457
  128.0 26.0 %collective-permute-start.28 = (bf16[512,1024]{1,0:T(8,128)(2,1)}, bf16[512,1024]{1,0:T(8,128)(2,1)}, u32[]{:S(2)}, u32[]{:S(2)}) collective-permute-start(bf16[512,1024]{1,0:T(8,128)(2,1)} %collective-permute-done.14.refs_1_), channel_id=1, source_target_pairs={{0,2},{2,0},{4,6},{6,4},{8,10},{10,8},{12,14},{14,12},{16,18},{18,... | collective-permute-start | bytes 3145736 | tf_op jit(solution)/shard_map/ppermute | solution.py:457
  151.8 32.4 %collective-permute-start.19 = (bf16[512,1024]{1,0:T(8,128)(2,1)S(1)}, bf16[512,1024]{1,0:T(8,128)(2,1)S(1)}, u32[]{:S(2)}, u32[]{:S(2)}) collective-permute-start(bf16[512,1024]{1,0:T(8,128)(2,1)S(1)} %multiply_convert_fusion.refs_0_), channel_id=1, source_target_pairs={{0,1},{1,0},{2,3},{3,2},{4,5},{5,4},{6,7},{7,6},{8,9},{9,8},{10,11... | collective-permute-start | bytes 3145736 | tf_op jit(solution)/shard_map/ppermute | solution.py:457
  152.8 31.5 %collective-permute-start.20 = (bf16[512,1024]{1,0:T(8,128)(2,1)S(1)}, bf16[512,1024]{1,0:T(8,128)(2,1)}, u32[]{:S(2)}, u32[]{:S(2)}) collective-permute-start(bf16[512,1024]{1,0:T(8,128)(2,1)S(1)} %multiply_convert_fusion.refs_0_), channel_id=1, source_target_pairs={{0,4},{2,6},{4,0},{6,2},{8,12},{10,14},{12,8},{14,10},{16,20},{18,... | collective-permute-start | bytes 3145736 | tf_op jit(solution)/shard_map/ppermute | solution.py:457
  188.3 299.4 %reduce-scatter.5.cloned.1.call-start = ((), (), s32[]{:S(2)}) async-start(), calls=%async_computation.4 | async-start | bytes 11796480 | tf_op jit(solution)/shard_map/reduce_scatter | solution.py:694
  193.9 31.1 %collective-permute-start.29 = (bf16[512,1024]{1,0:T(8,128)(2,1)}, bf16[512,1024]{1,0:T(8,128)(2,1)S(1)}, u32[]{:S(2)}, u32[]{:S(2)}) collective-permute-start(bf16[512,1024]{1,0:T(8,128)(2,1)} %get-tuple-element.80.refs_0_), channel_id=1, source_target_pairs={{0,2},{2,0},{4,6},{6,4},{8,10},{10,8},{12,14},{14,12},{16,18},{18,... | collective-permute-start | bytes 3145736 | tf_op jit(solution)/shard_map/ppermute | solution.py:457
  276.1 265.1 %reduce-scatter.3.cloned.1.call-start = ((), (), s32[]{:S(2)}) async-start(), calls=%async_computation.3 | async-start | bytes 3932160 | tf_op jit(solution)/shard_map/reduce_scatter | solution.py:694
  331.6 26.1 %collective-permute-start.47 = (bf16[256,1024]{1,0:T(8,128)(2,1)}, bf16[256,1024]{1,0:T(8,128)(2,1)S(1)}, u32[]{:S(2)}, u32[]{:S(2)}) collective-permute-start(bf16[256,1024]{1,0:T(8,128)(2,1)} %put_rows.32), channel_id=1, source_target_pairs={{0,4},{2,6},{4,0},{6,2},{8,12},{10,14},{12,8},{14,10},{16,20},{18,... | collective-permute-start | bytes 1572872 | tf_op jit(solution)/shard_map/ppermute | solution.py:457
  337.7 37.7 %collective-permute-start.49 = (bf16[256,1024]{1,0:T(8,128)(2,1)}, bf16[256,1024]{1,0:T(8,128)(2,1)S(1)}, u32[]{:S(2)}, u32[]{:S(2)}) collective-permute-start(bf16[256,1024]{1,0:T(8,128)(2,1)} %put_rows.33), channel_id=1, source_target_pairs={{0,1},{1,0},{2,3},{3,2},{4,5},{5,4},{6,7},{7,6},{8,9},{9,8},{10,11... | collective-permute-start | bytes 1572872 | tf_op jit(solution)/shard_map/ppermute | solution.py:457
  346.2 29.8 %collective-permute-start.44 = (bf16[256,1024]{1,0:T(8,128)(2,1)}, bf16[256,1024]{1,0:T(8,128)(2,1)S(1)}, u32[]{:S(2)}, u32[]{:S(2)}) collective-permute-start(bf16[256,1024]{1,0:T(8,128)(2,1)} %put_rows.28), channel_id=1, source_target_pairs={{0,4},{2,6},{4,0},{6,2},{8,12},{10,14},{12,8},{14,10},{16,20},{18,... | collective-permute-start | bytes 1572872 | tf_op jit(solution)/shard_map/ppermute | solution.py:457
  380.7 26.2 %collective-permute-start.50 = (bf16[512,1024]{1,0:T(8,128)(2,1)S(1)}, bf16[512,1024]{1,0:T(8,128)(2,1)}, u32[]{:S(2)}, u32[]{:S(2)}) collective-permute-start(bf16[512,1024]{1,0:T(8,128)(2,1)S(1)} %fusion.38), channel_id=1, source_target_pairs={{0,1},{1,0},{2,3},{3,2},{4,5},{5,4},{6,7},{7,6},{8,9},{9,8},{10,11... | collective-permute-start | bytes 3145736 | tf_op jit(solution)/shard_map/ppermute | solution.py:457
  385.7 87.8 %collective-permute-start.39 = (bf16[256,1024]{1,0:T(8,128)(2,1)}, bf16[256,1024]{1,0:T(8,128)(2,1)}, u32[]{:S(2)}, u32[]{:S(2)}) collective-permute-start(bf16[256,1024]{1,0:T(8,128)(2,1)} %put_rows.23), channel_id=1, source_target_pairs={{0,4},{2,6},{4,0},{6,2},{8,12},{10,14},{12,8},{14,10},{16,20},{18,... | collective-permute-start | bytes 1572872 | tf_op jit(solution)/shard_map/ppermute | solution.py:457
  390.5 84.7 %collective-permute-start.40 = (bf16[256,1024]{1,0:T(8,128)(2,1)}, bf16[256,1024]{1,0:T(8,128)(2,1)}, u32[]{:S(2)}, u32[]{:S(2)}) collective-permute-start(bf16[256,1024]{1,0:T(8,128)(2,1)} %put_rows.24), channel_id=1, source_target_pairs={{0,1},{1,0},{2,3},{3,2},{4,5},{5,4},{6,7},{7,6},{8,9},{9,8},{10,11... | collective-permute-start | bytes 1572872 | tf_op jit(solution)/shard_map/ppermute | solution.py:457
  409.9 32.3 %collective-permute-start.58 = (bf16[4,2,64,512]{3,2,0,1:T(8,128)(2,1)S(1)}, bf16[4,2,64,512]{3,2,0,1:T(8,128)(2,1)}, u32[]{:S(2)}, u32[]{:S(2)}) collective-permute-start(bf16[4,2,64,512]{3,2,0,1:T(8,128)(2,1)S(1)} %fusion.20), channel_id=1, source_target_pairs={{0,2},{2,0},{4,6},{6,4},{8,10},{10,8},{12,14},{14,12},{16,18},{18,... | collective-permute-start | bytes 1572872 | tf_op jit(solution)/shard_map/ppermute | solution.py:457
  440.6 25.4 %collective-permute-start.51 = (bf16[512,1024]{1,0:T(8,128)(2,1)}, bf16[512,1024]{1,0:T(8,128)(2,1)}, u32[]{:S(2)}, u32[]{:S(2)}) collective-permute-start(bf16[512,1024]{1,0:T(8,128)(2,1)} %dynamic-slice_convert_fusion), channel_id=1, source_target_pairs={{0,1},{1,0},{2,3},{3,2},{4,5},{5,4},{6,7},{7,6},{8,9},{9,8},{10,11... | collective-permute-start | bytes 3145736 | tf_op jit(solution)/shard_map/ppermute | solution.py:457
  469.9 28.3 %collective-permute-start.60 = (bf16[64,512]{1,0:T(8,128)(2,1)S(1)}, bf16[64,512]{1,0:T(8,128)(2,1)S(1)}, u32[]{:S(2)}, u32[]{:S(2)}) collective-permute-start(bf16[64,512]{1,0:T(8,128)(2,1)S(1)} %get-tuple-element.143), channel_id=1, source_target_pairs={{0,8},{2,10},{4,12},{6,14},{8,16},{10,18},{12,20},{14,22},{16,24},... | collective-permute-start | bytes 196616 | tf_op jit(solution)/shard_map/ppermute | solution.py:460
  509.6 34.5 %collective-permute-start.65 = (bf16[64,1024]{1,0:T(8,128)(2,1)}, bf16[64,1024]{1,0:T(8,128)(2,1)S(1)}, u32[]{:S(2)}, u32[]{:S(2)}) collective-permute-start(bf16[64,1024]{1,0:T(8,128)(2,1)} %get-tuple-element.139), channel_id=1, source_target_pairs={{0,8},{2,10},{4,12},{6,14},{8,16},{10,18},{12,20},{14,22},{16,24},... | collective-permute-start | bytes 393224 | tf_op jit(solution)/shard_map/ppermute | solution.py:460
  511.4 32.7 %collective-permute-start.66 = (bf16[64,1024]{1,0:T(8,128)(2,1)}, bf16[64,1024]{1,0:T(8,128)(2,1)S(1)}, u32[]{:S(2)}, u32[]{:S(2)}) collective-permute-start(bf16[64,1024]{1,0:T(8,128)(2,1)} %get-tuple-element.138), channel_id=1, source_target_pairs={{0,16},{2,18},{4,20},{6,22},{8,24},{10,26},{12,28},{14,30},{16,0},... | collective-permute-start | bytes 393224 | tf_op jit(solution)/shard_map/ppermute | solution.py:460
  511.9 32.2 %collective-permute-start.67 = (bf16[64,1024]{1,0:T(8,128)(2,1)}, bf16[64,1024]{1,0:T(8,128)(2,1)S(1)}, u32[]{:S(2)}, u32[]{:S(2)}) collective-permute-start(bf16[64,1024]{1,0:T(8,128)(2,1)} %get-tuple-element.137), channel_id=1, source_target_pairs={{0,24},{2,26},{4,28},{6,30},{8,0},{10,2},{12,4},{14,6},{16,8},{18,... | collective-permute-start | bytes 393224 | tf_op jit(solution)/shard_map/ppermute | solution.py:460
  514.5 25.2 %collective-permute-start.73 = (bf16[3,3,64,512]{3,2,1,0:T(8,128)(2,1)S(1)}, bf16[3,3,64,512]{3,2,1,0:T(8,128)(2,1)}, u32[]{:S(2)}, u32[]{:S(2)}) collective-permute-start(bf16[3,3,64,512]{3,2,1,0:T(8,128)(2,1)S(1)} %copy-done.85), channel_id=1, source_target_pairs={{0,6},{2,4},{4,2},{6,0},{8,14},{10,12},{12,10},{14,8},{16,22},{18,... | collective-permute-start | bytes 1769480 | tf_op jit(solution)/shard_map/ppermute | solution.py:457
  (138 other events, 1347.8 us)
Sparse Core Ops, SparseCore 0:
  11.6 56.6 all-gather.5
  70.2 165.3 all-gather.7
  237.2 61.6 all-gather.9
  301.1 159.9 reduce-scatter.4
  463.3 73.2 reduce-scatter.2

commit v4 on v3

--- a/solution.py
+++ b/solution.py
@@ -573,6 +573,19 @@
         return values, got, lambda got: sum(got, total)
 
     across = [[j + SUB * p for p in range(planes)] for j in range(SUB)]
+    rows = w_query.shape[0]
+    packed = jnp.concatenate(
+        [
+            w_query.reshape(rows, heads_kv, group * HEAD_DIM),
+            w_key.reshape(rows, heads_kv, HEAD_DIM),
+            w_value.reshape(rows, heads_kv, HEAD_DIM),
+        ],
+        axis=2,
+    ).reshape(rows, -1)
+    qkv_cols = packed.shape[1]
+    mine_attn = jnp.concatenate([packed, w_out], axis=1)
+    line = lax.all_gather(mine_attn, "fsdp", axis_index_groups=across)
+
     chunks, taken = [], 0
     for count in CHUNKS:
         count = min(count, experts - taken)
@@ -611,7 +624,6 @@
     else:
         near_gains = lax.all_gather(gains, "tp", axis=1, tiled=True)
     whole_tokens = sequence_gather(tokens)
-    near_gains = tie(near_gains, sends[0][1:])
     plane_gains = jnp.concatenate(
         by_sub([near_gains] + [swap(near_gains, k) for k in range(1, SUB)]), axis=1
     )
@@ -620,30 +632,29 @@
     all_gains = lax.dynamic_slice_in_dim(all_gains, planes - plane, planes, 0)
     all_gains = all_gains.transpose(1, 0, 2).reshape(2, -1)
 
-    rows = w_query.shape[0]
-    packed = jnp.concatenate(
-        [
-            w_query.reshape(rows, heads_kv, group * HEAD_DIM),
-            w_key.reshape(rows, heads_kv, HEAD_DIM),
-            w_value.reshape(rows, heads_kv, HEAD_DIM),
-        ],
-        axis=2,
-    ).reshape(rows, -1)
-    qkv_cols = packed.shape[1]
-    attn_w = lax.all_gather(
-        jnp.concatenate([packed, w_out], axis=1), "fsdp", axis=0, tiled=True
-    )
-    qkv_w, out_w = attn_w[:, :qkv_cols], attn_w[:, qkv_cols:]
-
     live = slots[0] >= 0
     turned = jnp.where(live, (slots[0] + (length - turn)) % length, -1)
     table = jnp.stack([turned.astype(F32), jnp.where(live, gate_values[0], 0.0)])
-    table = tie(table, plane_gains)
 
     def table_for(k):
         return lax.dynamic_slice_in_dim(table, (sub ^ k) * experts, experts, 1)
 
     tables = [table_for(0)] + [swap(table_for(k), k) for k in range(1, SUB)]
+
+    lines_y = swap(tie(line, plane_gains), 2)
+    lines = [line, swap(line, 1), lines_y, swap(lines_y, 1)]
+    whole_resid = whole_tokens.astype(F32)
+    first_low = (whole_resid * norm_scale(whole_resid) * all_gains[0]).astype(BF)
+
+    def attn_plan(at, outs):
+        for k in range(SUB):
+            for line in range(planes):
+                row = (line * SUB + lax.bitwise_xor(at[0], k)) * rows
+                row = pl.multiple_of(row, rows)
+                yield k, line, outs[0], (pl.ds(row, rows), slice(None))
+
+    (attn_w,) = move(at, lines, [(fsdp * rows, mine_attn.shape[1])], SUB * planes, attn_plan, first_low)
+    qkv_w, out_w = attn_w[:, :qkv_cols], attn_w[:, qkv_cols:]
 
     def shards_of(pieces, others=()):
         count = pieces[0].shape[0]
@@ -657,11 +668,11 @@
         (mine,) = move(at, pieces, [(count, 3, SUB * own_rows, FF)], SUB, plan, others)
         return lax.all_gather(mine, "fsdp", axis_index_groups=across), mine
 
-    held, mine_first = shards_of(first_pieces, (all_gains, whole_tokens))
+    held, mine_first = shards_of(
+        first_pieces, (line, near_gains, tables, whole_tokens)
+    )
     shards = [held]
 
-    whole_resid = whole_tokens.astype(F32)
-    first_low = (whole_resid * norm_scale(whole_resid) * all_gains[0]).astype(BF)
     begun = plane_start(tie(cotangent, mine_first))
     first_low = tie(first_low, tables)
     qkv = dot(qkv_w, first_low, 0, 1).astype(BF)

time: 575 us -> 564 us (0.981)
  waiting for transfers between devices: 154 us -> 114 us
  blocking collectives: 0 us -> 20.4 us
    all_gather x2, waiting for transfers between devices: 26.8 us -> 0.02 us  [shards_of(): return (lax.all_gather(mine, 'fsdp', axis_index_groups=across), mine)]
    all_gather x0 -> x1, blocking collectives: none -> 20.4 us  [layer(): line = lax.all_gather(mine_attn, 'fsdp', axis_index_groups=across)]
    unnamed x186 -> x209, local copies, waits for them, and re-layouts: 19.7 us -> 29.8 us
    ppermute x12, starting transfers between devices: 13 us -> 21.1 us  [shift(): lax.ppermute(values, 'fsdp', [(i, (i + planes_on * SUB) % fsdp) for i in...]
    ppermute x65 -> x68, waiting for transfers between devices: 108 us -> 101 us  [swap(): return lax.ppermute(values, axis, [(i, i ^ mask) for i in range(size)])]
    ppermute x12, waiting for transfers between devices: 19 us -> 12.9 us  [shift(): lax.ppermute(values, 'fsdp', [(i, (i + planes_on * SUB) % fsdp) for i in...]
    ppermute x65 -> x68, starting transfers between devices: 50.8 us -> 45.9 us  [swap(): return lax.ppermute(values, axis, [(i, i ^ mask) for i in range(size)])]
    pallas_call x5 -> x6, Pallas kernels: 18.6 us -> 23 us  [move(): pl.pallas_call(functools.partial(move_kernel, plan, len(operands)), in_sp...]
  transfers between devices with their start and end apart: 82 -> 84, of which waited for: 24 -> 24; matrix products, arithmetic and copies ran while one was open for 14% -> 14% of each run, Pallas kernels for 41% -> 42%
where the time goes in v4:
time: 564 us; the launch traced here: 557 us
  Pallas kernels  239 us (42%)
  waiting for transfers between devices  114 us (20%)
  starting transfers between devices  67.1 us (12%)
  local copies, waits for them, and re-layouts  45.4 us (8%)
  other arithmetic  33.4 us (6%)
  matrix products  22.2 us (4%)
  blocking collectives  20.4 us (4%)
  between operations  15.3 us (3%)
    ppermute x68, waiting for transfers between devices, swap(): return lax.ppermute(values, axis, [(i, i ^ mask) for i in range(size)])  101 us
    pallas_call x18, Pallas kernels, put(): pl.pallas_call(functools.partial(put_kernel, start, weighted, bool(addend...  69.5 us
    pallas_call x2, Pallas kernels, run_experts(): pl.pallas_call(expert_kernel, grid=(count,), in_specs=[rows, rows, block]...  57.3 us
    ppermute x68, starting transfers between devices, swap(): return lax.ppermute(values, axis, [(i, i ^ mask) for i in range(size)])  45.9 us
    pallas_call x8, Pallas kernels, pick(): pl.pallas_call(functools.partial(pick_kernel, weighted, len(parts)), grid...  44.3 us
    unnamed x209, local copies, waits for them, and re-layouts  29.8 us
    pallas_call x6, Pallas kernels, move(): pl.pallas_call(functools.partial(move_kernel, plan, len(operands)), in_sp...  23 us
    dot_general x6, matrix products, dot(): lax.dot_general(left, right, (((left_dim,), (right_dim,)), ((), ())), pre...  22.2 us
  transfers between devices with their start and end apart: 84, of which 24 were waited for; matrix products, arithmetic and copies ran while one was open for 14% of the time, Pallas kernels for 42%

profile of v4, /device:TPU:0, one launch (start us, length us, event | category | flops | bytes accessed | tf_op | source)
XLA Modules:
  0.0 557.0 jit_solution(17402648558598725018)
XLA Ops:
  11.0 4.8 move.7
  18.4 20.4 %all-gather = bf16[256,1536]{1,0:T(8,128)(2,1)} all-gather(bf16[64,1536]{1,0:T(8,128)(2,1)S(1)} %pad_maximum_fusion), channel_id=2, replica_groups={{0,8,16,24},{2,10,18,26},{4,12,20,28},{6,14,22,30},{1,9,17,25},{3,11,19..., dimensions={0}, use_global_device_ids=true | all-gather | bytes 983040 | tf_op jit(solution)/shard_map/all_gather | solution.py:587
  66.0 6.0 %collective-permute-done.9 = f32[2,256]{1,0:T(2,128)S(1)} collective-permute-done((f32[2,256]{1,0:T(2,128)S(1)}, f32[2,256]{1,0:T(2,128)S(1)}, u32[]{:S(2)}, u32[]{:S(2)}) %collective-permute-start.9) | collective-permute-done | bytes 2080 | tf_op jit(solution)/shard_map/ppermute | solution.py:460
  72.7 12.4 %collective-permute-done.5.refs_2_ = bf16[4,64,1536]{2,1,0:T(8,128)(2,1)S(1)} collective-permute-done((bf16[4,64,1536]{2,1,0:T(8,128)(2,1)}, bf16[4,64,1536]{2,1,0:T(8,128)(2,1)S(1)}, u32[]{:S(2)}, u32[]{:S(2)}) %collective-permute-start.5) | collective-permute-done | bytes 786464 | tf_op jit(solution)/shard_map/ppermute | solution.py:457
  90.7 4.5 move.6
  97.1 5.3 convolution_convert_fusion.qkv_ref
  102.4 18.2 %attend.1 = (bf16[512,1024]{1,0:T(8,128)(2,1)}, f32[4,2,1024]{2,1,0:T(2,128)}) custom-call(bf16[1024,1024]{1,0:T(8,128)(2,1)} %convolution_convert_fusion.qkv_ref, s32[1,1024]{1,0:T(1,128)} %bitcast.116, s32[1024,1]{1,0:T(8,128)} %copy.79.seg_col), custom_call_target="tpu_custom_call" | custom-call | flops 6442450944 | bytes 4194304 | tf_op jit(solution)/shard_map/attend/pallas_call | solution.py:125
  132.2 8.6 %collective-permute-done.20.refs_2_.refs_1_ = bf16[256,1024]{1,0:T(8,128)(2,1)S(1)} collective-permute-done((bf16[256,1024]{1,0:T(8,128)(2,1)}, bf16[256,1024]{1,0:T(8,128)(2,1)S(1)}, u32[]{:S(2)}, u32[]{:S(2)}) %collective-permute-start.20) | collective-permute-done | bytes 524320 | tf_op jit(solution)/shard_map/ppermute | solution.py:457
  140.8 19.4 %collective-permute-done.21.refs_3_.refs_2_ = bf16[256,1024]{1,0:T(8,128)(2,1)S(1)} collective-permute-done((bf16[256,1024]{1,0:T(8,128)(2,1)}, bf16[256,1024]{1,0:T(8,128)(2,1)S(1)}, u32[]{:S(2)}, u32[]{:S(2)}) %collective-permute-start.21) | collective-permute-done | bytes 524320 | tf_op jit(solution)/shard_map/ppermute | solution.py:457
  166.7 5.5 pick_rows.8.refs_2_
  172.2 5.5 pick_rows.9.refs_3_
  177.7 5.5 pick_rows.10.refs_3_
  185.8 5.5 pick_rows.11.refs_6_.slot_grad
  191.3 4.7 collective-permute-done.25.refs_4_
  205.0 12.3 %collective-permute-done.33.refs_1_ = bf16[256,1024]{1,0:T(8,128)(2,1)S(1)} collective-permute-done((bf16[256,1024]{1,0:T(8,128)(2,1)S(1)}, bf16[256,1024]{1,0:T(8,128)(2,1)S(1)}, u32[]{:S(2)}, u32[]{:S(2)}) %collective-permute-start.33) | collective-permute-done | bytes 524320 | tf_op jit(solution)/shard_map/ppermute | solution.py:457
  218.4 5.7 %pick_rows.12.refs_2_ = bf16[4,4,256,1024]{3,2,1,0:T(8,128)(2,1)} custom-call(f32[2,4,256]{2,1,0:T(4,128)} %get-tuple-element.149.refs_1_.refs_6_.slot_ref.refs_0_, bf16[512,1024]{1,0:T(8,128)(2,1)} %copy-done.16, bf16[512,1024]{1,0:T(8,128)(2,1)} %get-tuple-element.81.refs_1_), custom_call_target="tpu_custom_call" | custom-call | flops 2147483648 | bytes 4194304 | tf_op jit(solution)/shard_map/pick_rows/pallas_call | solution.py:254
  226.1 5.7 %pick_rows.13.refs_3_ = bf16[4,4,256,1024]{3,2,1,0:T(8,128)(2,1)} custom-call(f32[2,4,256]{2,1,0:T(4,128)} %copy-done.53, bf16[512,1024]{1,0:T(8,128)(2,1)} %copy-done.36, bf16[512,1024]{1,0:T(8,128)(2,1)} %copy-done.38, bf16[4,4,256,1024]{3,2,1,0:T(8,128)(2,1)} %pick_rows.12.refs_2_), custom_call_target="tpu_custom_call", output_to_operand_aliasing={{}: (3, {})} | custom-call | flops 2147483648 | bytes 4194304 | tf_op jit(solution)/shard_map/pick_rows/pallas_call | solution.py:254
  231.7 5.5 pick_rows.14.refs_3_
  239.0 5.5 pick_rows.15.picked
  244.5 40.5 %experts.2 = (bf16[3,4,256,1024]{3,2,1,0:T(8,128)(2,1)}, bf16[3,4,256,1024]{3,2,1,0:T(8,128)(2,1)}, bf16[4,3,3,256,512]{4,3,2,1,0:T(8,128)(2,1)}) custom-call(bf16[4,4,256,1024]{3,2,1,0:T(8,128)(2,1)} %pick_rows.15.picked, bf16[4,4,256,1024]{3,2,1,0:T(8,128)(2,1)} %pick_rows.11.refs_6_.slot_grad, bf16[4,3,3,256,512]{4,3,2,1,0:T(8,128)(2,1)} %bitcast.127), custom_call_target="tpu_custom_call" | custom-call | flops 28991029248 | bytes 44040192 | tf_op jit(solution)/shard_map/experts/pallas_call | solution.py:358
  285.0 16.9 %experts.3 = (bf16[1,4,256,1024]{3,2,1,0:T(8,128)(2,1)}, bf16[1,4,256,1024]{3,2,1,0:T(8,128)(2,1)}, bf16[4,1,3,256,512]{4,3,2,1,0:T(8,128)(2,1)}) custom-call(bf16[4,4,256,1024]{3,2,1,0:T(8,128)(2,1)} %pick_rows.15.picked, bf16[4,4,256,1024]{3,2,1,0:T(8,128)(2,1)} %pick_rows.11.refs_6_.slot_grad, bf16[4,1,3,256,512]{4,3,2,1,0:T(8,128)(2,1)} %bitcast.128), custom_call_target="tpu_custom_call" | custom-call | flops 9663676416 | bytes 14680064 | tf_op jit(solution)/shard_map/experts/pallas_call | solution.py:358
  301.9 5.3 put_rows.27
  307.7 5.3 put_rows.18
  350.6 5.5 put_rows.22
  356.1 5.6 %put_rows.20 = bf16[1024,1024]{1,0:T(8,128)(2,1)} custom-call(f32[2,4,256]{2,1,0:T(4,128)} %get-tuple-element.91.slot_ref, bf16[3,4,256,1024]{3,2,1,0:T(8,128)(2,1)} %get-tuple-element.89.refs_0_, bf16[1,4,256,1024]{3,2,1,0:T(8,128)(2,1)} %get-tuple-element.90.refs_1_), custom_call_target="tpu_custom_call" | custom-call | flops 2147483648 | bytes 4194304 | tf_op jit(solution)/shard_map/put_rows/pallas_call | solution.py:300
  387.3 5.5 collective-permute-done.53
  401.6 19.9 %attend_back.1 = bf16[1024,1024]{1,0:T(8,128)(2,1)} custom-call(bf16[1024,1024]{1,0:T(8,128)(2,1)} %convolution_convert_fusion.qkv_ref, bf16[512,1024]{1,0:T(8,128)(2,1)} %convolution_convert_fusion.1.grad_ref, bf16[512,1024]{1,0:T(8,128)(2,1)} %tie.13.refs_4_.out_ref, f32[4,2,1024]{2,1,0:T(2,128)} %get-tuple-element.94.log_ref, s32[1,1024]{1,0:T(1,128)} %bitcast.117, ...), custom_call_target="tpu_custom_call" | custom-call | flops 16106127360 | bytes 8388608 | tf_op jit(solution)/shard_map/attend_back/pallas_call | solution.py:189
  421.5 4.7 fusion.12
  447.4 5.9 %collective-permute-done.54 = bf16[512,1024]{1,0:T(8,128)(2,1)} collective-permute-done((bf16[512,1024]{1,0:T(8,128)(2,1)}, bf16[512,1024]{1,0:T(8,128)(2,1)}, u32[]{:S(2)}, u32[]{:S(2)}) %collective-permute-start.54) | collective-permute-done | bytes 1048608 | tf_op jit(solution)/shard_map/ppermute | solution.py:457
  504.7 5.7 %fusion.10 = (f32[512,1024]{1,0:T(8,128)}, bf16[512,1024]{1,0:T(8,128)(2,1)}) fusion(bf16[512,1024]{1,0:T(8,128)(2,1)S(1)} %copy-done.8, f32[512]{0:T(512)S(1)} %copy-done.86, f32[1024]{0:T(1024)S(1)} %bitcast.111, f32[512]{0:T(512)S(1)} %copy-done.80, bf16[512,1024]{1,0:T(8,128)(2,1)} %collective-permute-done.54, f32[1024,1024]{1,0:T(8,128)} %copy-done.13, ...), kind=kLoop, calls=%fused_computation.17 | loop fusion | flops 16777216 | bytes 16793604 | tf_op jit(solution)/shard_map/add | solution.py:745
  510.5 9.0 %collective-permute-done.75.refs_5_.refs_2_ = bf16[3,3,64,512]{3,2,1,0:T(8,128)(2,1)} collective-permute-done((bf16[3,3,64,512]{3,2,1,0:T(8,128)(2,1)S(1)}, bf16[3,3,64,512]{3,2,1,0:T(8,128)(2,1)}, u32[]{:S(2)}, u32[]{:S(2)}) %collective-permute-start.75) | collective-permute-done | bytes 589856 | tf_op jit(solution)/shard_map/ppermute | solution.py:457
  520.8 9.2 %collective-permute-done.76.refs_6_.refs_3_ = bf16[3,3,64,512]{3,2,1,0:T(8,128)(2,1)} collective-permute-done((bf16[3,3,64,512]{3,2,1,0:T(8,128)(2,1)S(1)}, bf16[3,3,64,512]{3,2,1,0:T(8,128)(2,1)}, u32[]{:S(2)}, u32[]{:S(2)}) %collective-permute-start.76) | collective-permute-done | bytes 589856 | tf_op jit(solution)/shard_map/ppermute | solution.py:457
  (470 shorter events, 242.0 us)
Async XLA Ops:
  7.2 237.2 %all-gather.6.cloned.1.call-start = ((), (), s32[]{:S(2)}) async-start(), calls=%async_computation.4 | async-start | bytes 11796480 | tf_op jit(solution)/shard_map/all_gather | solution.py:669
  7.3 32.2 %collective-permute-start.1 = (f32[2,32]{1,0:T(2,128)}, f32[2,32]{1,0:T(2,128)S(1)}, u32[]{:S(2)}, u32[]{:S(2)}) collective-permute-start(f32[2,32]{1,0:T(2,128)} %param.17), channel_id=1, source_target_pairs={{0,1},{1,0},{2,3},{3,2},{4,5},{5,4},{6,7},{7,6},{8,9},{9,8},{10,11... | collective-permute-start | bytes 776 | tf_op jit(solution)/shard_map/ppermute | solution.py:457
  10.3 31.9 %collective-permute-start.7 = (bf16[512,1024]{1,0:T(8,128)(2,1)}, bf16[512,1024]{1,0:T(8,128)(2,1)S(1)}, u32[]{:S(2)}, u32[]{:S(2)}) collective-permute-start(bf16[512,1024]{1,0:T(8,128)(2,1)} %param.13), channel_id=1, source_target_pairs={{0,1},{1,0},{2,3},{3,2},{4,5},{5,4},{6,7},{7,6},{8,9},{9,8},{10,11... | collective-permute-start | bytes 3145736 | tf_op jit(solution)/shard_map/ppermute | solution.py:457
  15.7 29.5 %collective-permute-start.14 = (bf16[3,3,64,512]{3,2,1,0:T(8,128)(2,1)}, bf16[3,3,64,512]{3,2,1,0:T(8,128)(2,1)S(1)}, u32[]{:S(2)}, u32[]{:S(2)}) collective-permute-start(bf16[3,3,64,512]{3,2,1,0:T(8,128)(2,1)} %get-tuple-element.69), channel_id=1, source_target_pairs={{0,2},{2,0},{4,6},{6,4},{8,10},{10,8},{12,14},{14,12},{16,18},{18,... | collective-permute-start | bytes 1769480 | tf_op jit(solution)/shard_map/ppermute | solution.py:457
  15.8 29.5 %collective-permute-start.15 = (bf16[3,3,64,512]{3,2,1,0:T(8,128)(2,1)}, bf16[3,3,64,512]{3,2,1,0:T(8,128)(2,1)}, u32[]{:S(2)}, u32[]{:S(2)}) collective-permute-start(bf16[3,3,64,512]{3,2,1,0:T(8,128)(2,1)} %get-tuple-element.70), channel_id=1, source_target_pairs={{0,4},{2,6},{4,0},{6,2},{8,12},{10,14},{12,8},{14,10},{16,20},{18,... | collective-permute-start | bytes 1769480 | tf_op jit(solution)/shard_map/ppermute | solution.py:457
  17.9 27.4 %collective-permute-start.16 = (bf16[3,3,64,512]{3,2,1,0:T(8,128)(2,1)}, bf16[3,3,64,512]{3,2,1,0:T(8,128)(2,1)}, u32[]{:S(2)}, u32[]{:S(2)}) collective-permute-start(bf16[3,3,64,512]{3,2,1,0:T(8,128)(2,1)} %get-tuple-element.71), channel_id=1, source_target_pairs={{0,6},{2,4},{4,2},{6,0},{8,14},{10,12},{12,10},{14,8},{16,22},{18,... | collective-permute-start | bytes 1769480 | tf_op jit(solution)/shard_map/ppermute | solution.py:457
  49.9 235.1 %all-gather.8.cloned.1.call-start = ((), (), s32[]{:S(2)}) async-start(), calls=%async_computation.5 | async-start | bytes 3932160 | tf_op jit(solution)/shard_map/all_gather | solution.py:669
  58.9 30.9 %collective-permute-start = (bf16[4,64,1536]{2,1,0:T(8,128)(2,1)}, bf16[4,64,1536]{2,1,0:T(8,128)(2,1)}, u32[]{:S(2)}, u32[]{:S(2)}) collective-permute-start(bf16[4,64,1536]{2,1,0:T(8,128)(2,1)} %bitcast.2.refs_0_.refs_4_), channel_id=1, source_target_pairs={{0,2},{2,0},{4,6},{6,4},{8,10},{10,8},{12,14},{14,12},{16,18},{18,... | collective-permute-start | bytes 2359304 | tf_op jit(solution)/shard_map/ppermute | solution.py:457
  85.9 34.6 %collective-permute-start.17 = (bf16[512,1024]{1,0:T(8,128)(2,1)}, bf16[512,1024]{1,0:T(8,128)(2,1)}, u32[]{:S(2)}, u32[]{:S(2)}) collective-permute-start(bf16[512,1024]{1,0:T(8,128)(2,1)} %tie.12), channel_id=1, source_target_pairs={{0,1},{1,0},{2,3},{3,2},{4,5},{5,4},{6,7},{7,6},{8,9},{9,8},{10,11... | collective-permute-start | bytes 3145736 | tf_op jit(solution)/shard_map/ppermute | solution.py:457
  87.4 33.1 %collective-permute-start.18 = (bf16[512,1024]{1,0:T(8,128)(2,1)}, bf16[512,1024]{1,0:T(8,128)(2,1)}, u32[]{:S(2)}, u32[]{:S(2)}) collective-permute-start(bf16[512,1024]{1,0:T(8,128)(2,1)} %tie.12), channel_id=1, source_target_pairs={{0,4},{2,6},{4,0},{6,2},{8,12},{10,14},{12,8},{14,10},{16,20},{18,... | collective-permute-start | bytes 3145736 | tf_op jit(solution)/shard_map/ppermute | solution.py:457
  124.4 35.8 %collective-permute-start.19 = (bf16[512,1024]{1,0:T(8,128)(2,1)}, bf16[512,1024]{1,0:T(8,128)(2,1)S(1)}, u32[]{:S(2)}, u32[]{:S(2)}) collective-permute-start(bf16[512,1024]{1,0:T(8,128)(2,1)} %dynamic-slice_convert_fusion.1), channel_id=1, source_target_pairs={{0,1},{1,0},{2,3},{3,2},{4,5},{5,4},{6,7},{7,6},{8,9},{9,8},{10,11... | collective-permute-start | bytes 3145736 | tf_op jit(solution)/shard_map/ppermute | solution.py:457
  130.2 30.0 %collective-permute-start.21 = (bf16[256,1024]{1,0:T(8,128)(2,1)}, bf16[256,1024]{1,0:T(8,128)(2,1)S(1)}, u32[]{:S(2)}, u32[]{:S(2)}) collective-permute-start(bf16[256,1024]{1,0:T(8,128)(2,1)} %slice.52), channel_id=1, source_target_pairs={{0,1},{1,0},{2,3},{3,2},{4,5},{5,4},{6,7},{7,6},{8,9},{9,8},{10,11... | collective-permute-start | bytes 1572872 | tf_op jit(solution)/shard_map/ppermute | solution.py:457
  131.7 34.5 %collective-permute-start.30 = (bf16[512,1024]{1,0:T(8,128)(2,1)}, bf16[512,1024]{1,0:T(8,128)(2,1)}, u32[]{:S(2)}, u32[]{:S(2)}) collective-permute-start(bf16[512,1024]{1,0:T(8,128)(2,1)} %refs_0_.4), channel_id=1, source_target_pairs={{0,2},{2,0},{4,6},{6,4},{8,10},{10,8},{12,14},{14,12},{16,18},{18,... | collective-permute-start | bytes 3145736 | tf_op jit(solution)/shard_map/ppermute | solution.py:457
  131.7 51.5 %collective-permute-start.27 = (bf16[512,1024]{1,0:T(8,128)(2,1)}, bf16[512,1024]{1,0:T(8,128)(2,1)}, u32[]{:S(2)}, u32[]{:S(2)}) collective-permute-start(bf16[512,1024]{1,0:T(8,128)(2,1)} %collective-permute-done.18.refs_2_.refs_1_.refs_0_), channel_id=1, source_target_pairs={{0,2},{2,0},{4,6},{6,4},{8,10},{10,8},{12,14},{14,12},{16,18},{18,... | collective-permute-start | bytes 3145736 | tf_op jit(solution)/shard_map/ppermute | solution.py:457
  140.8 25.4 %collective-permute-start.31 = (bf16[512,1024]{1,0:T(8,128)(2,1)}, bf16[512,1024]{1,0:T(8,128)(2,1)}, u32[]{:S(2)}, u32[]{:S(2)}) collective-permute-start(bf16[512,1024]{1,0:T(8,128)(2,1)} %collective-permute-done.17.refs_1_), channel_id=1, source_target_pairs={{0,2},{2,0},{4,6},{6,4},{8,10},{10,8},{12,14},{14,12},{16,18},{18,... | collective-permute-start | bytes 3145736 | tf_op jit(solution)/shard_map/ppermute | solution.py:457
  164.1 32.5 %collective-permute-start.22 = (bf16[512,1024]{1,0:T(8,128)(2,1)S(1)}, bf16[512,1024]{1,0:T(8,128)(2,1)S(1)}, u32[]{:S(2)}, u32[]{:S(2)}) collective-permute-start(bf16[512,1024]{1,0:T(8,128)(2,1)S(1)} %multiply_convert_fusion.refs_0_), channel_id=1, source_target_pairs={{0,1},{1,0},{2,3},{3,2},{4,5},{5,4},{6,7},{7,6},{8,9},{9,8},{10,11... | collective-permute-start | bytes 3145736 | tf_op jit(solution)/shard_map/ppermute | solution.py:457
  165.7 30.9 %collective-permute-start.23 = (bf16[512,1024]{1,0:T(8,128)(2,1)S(1)}, bf16[512,1024]{1,0:T(8,128)(2,1)}, u32[]{:S(2)}, u32[]{:S(2)}) collective-permute-start(bf16[512,1024]{1,0:T(8,128)(2,1)S(1)} %multiply_convert_fusion.refs_0_), channel_id=1, source_target_pairs={{0,4},{2,6},{4,0},{6,2},{8,12},{10,14},{12,8},{14,10},{16,20},{18,... | collective-permute-start | bytes 3145736 | tf_op jit(solution)/shard_map/ppermute | solution.py:457
  200.6 274.8 %reduce-scatter.5.cloned.1.call-start = ((), (), s32[]{:S(2)}) async-start(), calls=%async_computation.3 | async-start | bytes 11796480 | tf_op jit(solution)/shard_map/reduce_scatter | solution.py:705
  205.0 32.2 %collective-permute-start.32 = (bf16[512,1024]{1,0:T(8,128)(2,1)}, bf16[512,1024]{1,0:T(8,128)(2,1)S(1)}, u32[]{:S(2)}, u32[]{:S(2)}) collective-permute-start(bf16[512,1024]{1,0:T(8,128)(2,1)} %get-tuple-element.80.refs_0_), channel_id=1, source_target_pairs={{0,2},{2,0},{4,6},{6,4},{8,10},{10,8},{12,14},{14,12},{16,18},{18,... | collective-permute-start | bytes 3145736 | tf_op jit(solution)/shard_map/ppermute | solution.py:457
  285.0 245.6 %reduce-scatter.3.cloned.1.call-start = ((), (), s32[]{:S(2)}) async-start(), calls=%async_computation.2 | async-start | bytes 3932160 | tf_op jit(solution)/shard_map/reduce_scatter | solution.py:705
  317.6 26.0 %collective-permute-start.50 = (bf16[256,1024]{1,0:T(8,128)(2,1)}, bf16[256,1024]{1,0:T(8,128)(2,1)S(1)}, u32[]{:S(2)}, u32[]{:S(2)}) collective-permute-start(bf16[256,1024]{1,0:T(8,128)(2,1)} %put_rows.32), channel_id=1, source_target_pairs={{0,4},{2,6},{4,0},{6,2},{8,12},{10,14},{12,8},{14,10},{16,20},{18,... | collective-permute-start | bytes 1572872 | tf_op jit(solution)/shard_map/ppermute | solution.py:457
  323.9 37.9 %collective-permute-start.52 = (bf16[256,1024]{1,0:T(8,128)(2,1)}, bf16[256,1024]{1,0:T(8,128)(2,1)S(1)}, u32[]{:S(2)}, u32[]{:S(2)}) collective-permute-start(bf16[256,1024]{1,0:T(8,128)(2,1)} %put_rows.33), channel_id=1, source_target_pairs={{0,1},{1,0},{2,3},{3,2},{4,5},{5,4},{6,7},{7,6},{8,9},{9,8},{10,11... | collective-permute-start | bytes 1572872 | tf_op jit(solution)/shard_map/ppermute | solution.py:457
  332.4 30.1 %collective-permute-start.47 = (bf16[256,1024]{1,0:T(8,128)(2,1)}, bf16[256,1024]{1,0:T(8,128)(2,1)S(1)}, u32[]{:S(2)}, u32[]{:S(2)}) collective-permute-start(bf16[256,1024]{1,0:T(8,128)(2,1)} %put_rows.28), channel_id=1, source_target_pairs={{0,4},{2,6},{4,0},{6,2},{8,12},{10,14},{12,8},{14,10},{16,20},{18,... | collective-permute-start | bytes 1572872 | tf_op jit(solution)/shard_map/ppermute | solution.py:457
  366.6 26.2 %collective-permute-start.53 = (bf16[512,1024]{1,0:T(8,128)(2,1)S(1)}, bf16[512,1024]{1,0:T(8,128)(2,1)}, u32[]{:S(2)}, u32[]{:S(2)}) collective-permute-start(bf16[512,1024]{1,0:T(8,128)(2,1)S(1)} %fusion.43), channel_id=1, source_target_pairs={{0,1},{1,0},{2,3},{3,2},{4,5},{5,4},{6,7},{7,6},{8,9},{9,8},{10,11... | collective-permute-start | bytes 3145736 | tf_op jit(solution)/shard_map/ppermute | solution.py:457
  370.4 91.5 %collective-permute-start.42 = (bf16[256,1024]{1,0:T(8,128)(2,1)}, bf16[256,1024]{1,0:T(8,128)(2,1)}, u32[]{:S(2)}, u32[]{:S(2)}) collective-permute-start(bf16[256,1024]{1,0:T(8,128)(2,1)} %put_rows.23), channel_id=1, source_target_pairs={{0,4},{2,6},{4,0},{6,2},{8,12},{10,14},{12,8},{14,10},{16,20},{18,... | collective-permute-start | bytes 1572872 | tf_op jit(solution)/shard_map/ppermute | solution.py:457
  374.7 88.4 %collective-permute-start.43 = (bf16[256,1024]{1,0:T(8,128)(2,1)}, bf16[256,1024]{1,0:T(8,128)(2,1)}, u32[]{:S(2)}, u32[]{:S(2)}) collective-permute-start(bf16[256,1024]{1,0:T(8,128)(2,1)} %put_rows.24), channel_id=1, source_target_pairs={{0,1},{1,0},{2,3},{3,2},{4,5},{5,4},{6,7},{7,6},{8,9},{9,8},{10,11... | collective-permute-start | bytes 1572872 | tf_op jit(solution)/shard_map/ppermute | solution.py:457
  397.2 30.6 %collective-permute-start.61 = (bf16[4,2,64,512]{3,2,0,1:T(8,128)(2,1)S(1)}, bf16[4,2,64,512]{3,2,0,1:T(8,128)(2,1)}, u32[]{:S(2)}, u32[]{:S(2)}) collective-permute-start(bf16[4,2,64,512]{3,2,0,1:T(8,128)(2,1)S(1)} %fusion.20), channel_id=1, source_target_pairs={{0,2},{2,0},{4,6},{6,4},{8,10},{10,8},{12,14},{14,12},{16,18},{18,... | collective-permute-start | bytes 1572872 | tf_op jit(solution)/shard_map/ppermute | solution.py:457
  427.4 25.9 %collective-permute-start.54 = (bf16[512,1024]{1,0:T(8,128)(2,1)}, bf16[512,1024]{1,0:T(8,128)(2,1)}, u32[]{:S(2)}, u32[]{:S(2)}) collective-permute-start(bf16[512,1024]{1,0:T(8,128)(2,1)} %dynamic-slice_convert_fusion), channel_id=1, source_target_pairs={{0,1},{1,0},{2,3},{3,2},{4,5},{5,4},{6,7},{7,6},{8,9},{9,8},{10,11... | collective-permute-start | bytes 3145736 | tf_op jit(solution)/shard_map/ppermute | solution.py:457
  455.9 29.2 %collective-permute-start.63 = (bf16[64,512]{1,0:T(8,128)(2,1)S(1)}, bf16[64,512]{1,0:T(8,128)(2,1)S(1)}, u32[]{:S(2)}, u32[]{:S(2)}) collective-permute-start(bf16[64,512]{1,0:T(8,128)(2,1)S(1)} %get-tuple-element.143), channel_id=1, source_target_pairs={{0,8},{2,10},{4,12},{6,14},{8,16},{10,18},{12,20},{14,22},{16,24},... | collective-permute-start | bytes 196616 | tf_op jit(solution)/shard_map/ppermute | solution.py:460
  496.7 37.1 %collective-permute-start.68 = (bf16[64,1024]{1,0:T(8,128)(2,1)}, bf16[64,1024]{1,0:T(8,128)(2,1)S(1)}, u32[]{:S(2)}, u32[]{:S(2)}) collective-permute-start(bf16[64,1024]{1,0:T(8,128)(2,1)} %get-tuple-element.139), channel_id=1, source_target_pairs={{0,8},{2,10},{4,12},{6,14},{8,16},{10,18},{12,20},{14,22},{16,24},... | collective-permute-start | bytes 393224 | tf_op jit(solution)/shard_map/ppermute | solution.py:460
  500.4 33.3 %collective-permute-start.69 = (bf16[64,1024]{1,0:T(8,128)(2,1)}, bf16[64,1024]{1,0:T(8,128)(2,1)S(1)}, u32[]{:S(2)}, u32[]{:S(2)}) collective-permute-start(bf16[64,1024]{1,0:T(8,128)(2,1)} %get-tuple-element.138), channel_id=1, source_target_pairs={{0,16},{2,18},{4,20},{6,22},{8,24},{10,26},{12,28},{14,30},{16,0},... | collective-permute-start | bytes 393224 | tf_op jit(solution)/shard_map/ppermute | solution.py:460
  501.0 32.8 %collective-permute-start.70 = (bf16[64,1024]{1,0:T(8,128)(2,1)}, bf16[64,1024]{1,0:T(8,128)(2,1)S(1)}, u32[]{:S(2)}, u32[]{:S(2)}) collective-permute-start(bf16[64,1024]{1,0:T(8,128)(2,1)} %get-tuple-element.137), channel_id=1, source_target_pairs={{0,24},{2,26},{4,28},{6,30},{8,0},{10,2},{12,4},{14,6},{16,8},{18,... | collective-permute-start | bytes 393224 | tf_op jit(solution)/shard_map/ppermute | solution.py:460
  (151 other events, 1508.2 us)
Sparse Core Ops, SparseCore 0:
  50.1 168.0 all-gather.5
  219.7 61.6 all-gather.7
  285.1 161.3 reduce-scatter.4
  448.7 73.6 reduce-scatter.2

commit v5 on v4

--- a/solution.py
+++ b/solution.py
@@ -537,7 +537,7 @@
         core, line = sub & 1, sub >> 1
         sent = lax.dynamic_index_in_dim(values, 1 - core, 2, keepdims=False)
         kept = lax.dynamic_index_in_dim(values, core, 2, keepdims=False)
-        values = halved = kept.astype(F32) + swap(sent.astype(BF), 1).astype(F32)
+        values = kept.astype(F32) + swap(sent.astype(BF), 1).astype(F32)
         sent = lax.dynamic_index_in_dim(values, 1 - line, 1, keepdims=False)
         kept = lax.dynamic_index_in_dim(values, line, 1, keepdims=False)
         values = kept + swap(sent.astype(BF), 2).astype(F32)
@@ -552,7 +552,7 @@
             )
             for r in range(1, planes)
         ]
-        return halved, values, got, lambda got: sum([total] + [part.astype(F32) for part in got])
+        return values, got, lambda got: sum([total] + [part.astype(F32) for part in got])
 
     def gain_scatter(values):
         values = values.reshape(2, planes, SUB, tp, -1)
@@ -731,13 +731,15 @@
         return move(at, (part,), shapes, SUB, plan, others)
 
     hidden_low = sequence_gather(own_low)
-    _, _, got_grad_out, finish_out = weight_scatter(dot(hidden_low, attended, 0, 1))
+    _, got_grad_out, finish_out = weight_scatter(dot(hidden_low, attended, 0, 1))
     attended_grad = dot(out_w, hidden_low, 0, 1).astype(BF)
     qkv_grad = attend_back(qkv, attended_grad, attended, logs, segments, heads_kv, group)
     grad_qkv = dot(first_low, qkv_grad, 0, 1)
     first_part = dot(qkv_grad, qkv_w, 0, 1)
+    early = [rows_out(part, first_part) for part in sums[:-1]]
     if tp == 2:
         got = swap(part_of(first_part, 1 - at_tp).astype(BF), 1, "tp")
+        got = tie(got, early)
         first_grad = part_of(first_part, at_tp) + got.astype(F32)
     else:
         first_grad = sequence_scatter(first_part)
@@ -745,15 +747,15 @@
     grad_tokens = grad_hidden + back_one
     mixed = (hidden + finish_out_sum(tie(got_out, first_gain))).astype(BF)
     grad_gains, got_gains, finish_gains = gain_scatter(jnp.stack([first_gain, second_gain]))
-    halved, grad_qkv, got_qkv, finish_qkv = weight_scatter(grad_qkv)
-
-    early = [swap_all(rows_out(part, halved)) for part in sums[:-1]]
-    late = rows_out(sums[-1], (grad_qkv, grad_gains, early))
+    grad_qkv, got_qkv, finish_qkv = weight_scatter(grad_qkv)
+
+    expert_grads = None
+    for number, pieces in enumerate(early):
+        pieces = swap_all(tie(pieces, grad_gains))
+        expert_grads = place(at, pieces, chunks[number][0], experts, expert_grads)
+    late = rows_out(sums[-1], (grad_qkv, grad_gains, expert_grads))
     got_grad_out, got_qkv, got_gains = tie((got_grad_out, got_qkv, got_gains), late[1:])
     late = swap_all(late)
-    expert_grads = None
-    for number, pieces in enumerate(early):
-        expert_grads = place(at, pieces, chunks[number][0], experts, expert_grads)
     expert_grads = place(at, late, chunks[-1][0], experts, expert_grads)
     grad_out = finish_out(got_grad_out)
     grad_gains = finish_gains(got_gains)

time: 564 us -> 569 us (level)
  waiting for transfers between devices: 114 us -> 124 us
    ppermute x68, waiting for transfers between devices: 101 us -> 118 us  [swap(): return lax.ppermute(values, axis, [(i, i ^ mask) for i in range(size)])]
    ppermute x12, waiting for transfers between devices: 12.9 us -> 5.99 us  [shift(): lax.ppermute(values, 'fsdp', [(i, (i + planes_on * SUB) % fsdp) for i in...]
    unnamed x209 -> x205, local copies, waits for them, and re-layouts: 29.8 us -> 27.9 us
  transfers between devices with their start and end apart: 84 -> 84, of which waited for: 24 -> 21; matrix products, arithmetic and copies ran while one was open for 14% -> 13% of each run, Pallas kernels for 42% -> 41%
where the time goes in v5:
time: 569 us; the launch traced here: 562 us
  Pallas kernels  239 us (42%)
  waiting for transfers between devices  124 us (22%)
  starting transfers between devices  67.6 us (12%)
  local copies, waits for them, and re-layouts  42.9 us (8%)
  other arithmetic  31.6 us (6%)
  matrix products  21.4 us (4%)
  blocking collectives  20.4 us (4%)
  between operations  15.3 us (3%)
    ppermute x68, waiting for transfers between devices, swap(): return lax.ppermute(values, axis, [(i, i ^ mask) for i in range(size)])  118 us
    pallas_call x18, Pallas kernels, put(): pl.pallas_call(functools.partial(put_kernel, start, weighted, bool(addend...  69.7 us
    pallas_call x2, Pallas kernels, run_experts(): pl.pallas_call(expert_kernel, grid=(count,), in_specs=[rows, rows, block]...  57.4 us
    ppermute x68, starting transfers between devices, swap(): return lax.ppermute(values, axis, [(i, i ^ mask) for i in range(size)])  45.5 us
    pallas_call x8, Pallas kernels, pick(): pl.pallas_call(functools.partial(pick_kernel, weighted, len(parts)), grid...  44.1 us
    unnamed x205, local copies, waits for them, and re-layouts  27.9 us
    pallas_call x6, Pallas kernels, move(): pl.pallas_call(functools.partial(move_kernel, plan, len(operands)), in_sp...  22.6 us
    ppermute x12, starting transfers between devices, shift(): lax.ppermute(values, 'fsdp', [(i, (i + planes_on * SUB) % fsdp) for i in...  21.9 us
  transfers between devices with their start and end apart: 84, of which 21 were waited for; matrix products, arithmetic and copies ran while one was open for 13% of the time, Pallas kernels for 41%

profile of v5, /device:TPU:0, one launch (start us, length us, event | category | flops | bytes accessed | tf_op | source)
XLA Modules:
  0.0 562.0 jit_solution(6022947557783372413)
XLA Ops:
  10.9 4.8 move.7
  18.4 20.4 %all-gather = bf16[256,1536]{1,0:T(8,128)(2,1)} all-gather(bf16[64,1536]{1,0:T(8,128)(2,1)S(1)} %pad_maximum_fusion), channel_id=2, replica_groups={{0,8,16,24},{2,10,18,26},{4,12,20,28},{6,14,22,30},{1,9,17,25},{3,11,19..., dimensions={0}, use_global_device_ids=true | all-gather | bytes 983040 | tf_op jit(solution)/shard_map/all_gather | solution.py:587
  65.9 6.0 %collective-permute-done.9 = f32[2,256]{1,0:T(2,128)S(1)} collective-permute-done((f32[2,256]{1,0:T(2,128)S(1)}, f32[2,256]{1,0:T(2,128)S(1)}, u32[]{:S(2)}, u32[]{:S(2)}) %collective-permute-start.9) | collective-permute-done | bytes 2080 | tf_op jit(solution)/shard_map/ppermute | solution.py:460
  72.6 12.4 %collective-permute-done.5.refs_2_ = bf16[4,64,1536]{2,1,0:T(8,128)(2,1)S(1)} collective-permute-done((bf16[4,64,1536]{2,1,0:T(8,128)(2,1)}, bf16[4,64,1536]{2,1,0:T(8,128)(2,1)S(1)}, u32[]{:S(2)}, u32[]{:S(2)}) %collective-permute-start.5) | collective-permute-done | bytes 786464 | tf_op jit(solution)/shard_map/ppermute | solution.py:457
  97.0 5.3 convolution_convert_fusion.qkv_ref
  102.3 18.2 %attend.1 = (bf16[512,1024]{1,0:T(8,128)(2,1)}, f32[4,2,1024]{2,1,0:T(2,128)}) custom-call(bf16[1024,1024]{1,0:T(8,128)(2,1)} %convolution_convert_fusion.qkv_ref, s32[1,1024]{1,0:T(1,128)} %bitcast.117, s32[1024,1]{1,0:T(8,128)} %copy.81.seg_col), custom_call_target="tpu_custom_call" | custom-call | flops 6442450944 | bytes 4194304 | tf_op jit(solution)/shard_map/attend/pallas_call | solution.py:125
  132.2 8.5 %collective-permute-done.20.refs_2_.refs_1_ = bf16[256,1024]{1,0:T(8,128)(2,1)S(1)} collective-permute-done((bf16[256,1024]{1,0:T(8,128)(2,1)}, bf16[256,1024]{1,0:T(8,128)(2,1)S(1)}, u32[]{:S(2)}, u32[]{:S(2)}) %collective-permute-start.20) | collective-permute-done | bytes 524320 | tf_op jit(solution)/shard_map/ppermute | solution.py:457
  140.7 19.4 %collective-permute-done.21.refs_3_.refs_2_ = bf16[256,1024]{1,0:T(8,128)(2,1)S(1)} collective-permute-done((bf16[256,1024]{1,0:T(8,128)(2,1)}, bf16[256,1024]{1,0:T(8,128)(2,1)S(1)}, u32[]{:S(2)}, u32[]{:S(2)}) %collective-permute-start.21) | collective-permute-done | bytes 524320 | tf_op jit(solution)/shard_map/ppermute | solution.py:457
  167.3 5.5 pick_rows.8.refs_2_
  172.8 5.5 pick_rows.9.refs_3_
  178.3 5.6 pick_rows.10.refs_3_
  186.4 5.5 pick_rows.11.refs_6_.slot_grad
  191.9 4.7 collective-permute-done.25.refs_4_
  205.9 12.2 %collective-permute-done.33.refs_1_ = bf16[256,1024]{1,0:T(8,128)(2,1)S(1)} collective-permute-done((bf16[256,1024]{1,0:T(8,128)(2,1)S(1)}, bf16[256,1024]{1,0:T(8,128)(2,1)S(1)}, u32[]{:S(2)}, u32[]{:S(2)}) %collective-permute-start.33) | collective-permute-done | bytes 524320 | tf_op jit(solution)/shard_map/ppermute | solution.py:457
  219.4 5.7 %pick_rows.12.refs_2_ = bf16[4,4,256,1024]{3,2,1,0:T(8,128)(2,1)} custom-call(f32[2,4,256]{2,1,0:T(4,128)} %get-tuple-element.157.refs_1_.refs_6_.slot_ref.refs_0_, bf16[512,1024]{1,0:T(8,128)(2,1)} %copy-done.17, bf16[512,1024]{1,0:T(8,128)(2,1)} %get-tuple-element.85.refs_1_), custom_call_target="tpu_custom_call" | custom-call | flops 2147483648 | bytes 4194304 | tf_op jit(solution)/shard_map/pick_rows/pallas_call | solution.py:254
  227.1 5.5 pick_rows.13.refs_3_
  232.6 5.5 pick_rows.14.refs_3_
  239.0 5.5 pick_rows.15.picked
  244.5 40.5 %experts.2 = (bf16[3,4,256,1024]{3,2,1,0:T(8,128)(2,1)}, bf16[3,4,256,1024]{3,2,1,0:T(8,128)(2,1)}, bf16[4,3,3,256,512]{4,3,2,1,0:T(8,128)(2,1)}) custom-call(bf16[4,4,256,1024]{3,2,1,0:T(8,128)(2,1)} %pick_rows.15.picked, bf16[4,4,256,1024]{3,2,1,0:T(8,128)(2,1)} %pick_rows.11.refs_6_.slot_grad, bf16[4,3,3,256,512]{4,3,2,1,0:T(8,128)(2,1)} %bitcast.127), custom_call_target="tpu_custom_call" | custom-call | flops 28991029248 | bytes 44040192 | tf_op jit(solution)/shard_map/experts/pallas_call | solution.py:358
  285.1 16.9 %experts.3 = (bf16[1,4,256,1024]{3,2,1,0:T(8,128)(2,1)}, bf16[1,4,256,1024]{3,2,1,0:T(8,128)(2,1)}, bf16[4,1,3,256,512]{4,3,2,1,0:T(8,128)(2,1)}) custom-call(bf16[4,4,256,1024]{3,2,1,0:T(8,128)(2,1)} %pick_rows.15.picked, bf16[4,4,256,1024]{3,2,1,0:T(8,128)(2,1)} %pick_rows.11.refs_6_.slot_grad, bf16[4,1,3,256,512]{4,3,2,1,0:T(8,128)(2,1)} %bitcast.128), custom_call_target="tpu_custom_call" | custom-call | flops 9663676416 | bytes 14680064 | tf_op jit(solution)/shard_map/experts/pallas_call | solution.py:358
  302.0 5.3 put_rows.27
  307.8 5.3 put_rows.18
  346.9 5.6 put_rows.22
  352.6 6.6 %collective-permute-done.51 = bf16[256,1024]{1,0:T(8,128)(2,1)S(1)} collective-permute-done((bf16[256,1024]{1,0:T(8,128)(2,1)S(1)}, bf16[256,1024]{1,0:T(8,128)(2,1)S(1)}, u32[]{:S(2)}, u32[]{:S(2)}) %collective-permute-start.51) | collective-permute-done | bytes 524320 | tf_op jit(solution)/shard_map/ppermute | solution.py:457
  363.7 5.6 put_rows.20
  376.2 11.4 %collective-permute-done.53 = bf16[512,1024]{1,0:T(8,128)(2,1)} collective-permute-done((bf16[512,1024]{1,0:T(8,128)(2,1)S(1)}, bf16[512,1024]{1,0:T(8,128)(2,1)}, u32[]{:S(2)}, u32[]{:S(2)}) %collective-permute-start.53) | collective-permute-done | bytes 1048608 | tf_op jit(solution)/shard_map/ppermute | solution.py:457
  394.8 20.0 %attend_back.1 = bf16[1024,1024]{1,0:T(8,128)(2,1)} custom-call(bf16[1024,1024]{1,0:T(8,128)(2,1)} %convolution_convert_fusion.qkv_ref, bf16[512,1024]{1,0:T(8,128)(2,1)} %convolution_convert_fusion.1.grad_ref, bf16[512,1024]{1,0:T(8,128)(2,1)} %tie.15.refs_4_.out_ref, f32[4,2,1024]{2,1,0:T(2,128)} %get-tuple-element.98.log_ref, s32[1,1024]{1,0:T(1,128)} %bitcast.118, ...), custom_call_target="tpu_custom_call" | custom-call | flops 16106127360 | bytes 8388608 | tf_op jit(solution)/shard_map/attend_back/pallas_call | solution.py:189
  466.2 8.2 %collective-permute-done.45.refs_3_ = bf16[256,1024]{1,0:T(8,128)(2,1)} collective-permute-done((bf16[256,1024]{1,0:T(8,128)(2,1)}, bf16[256,1024]{1,0:T(8,128)(2,1)}, u32[]{:S(2)}, u32[]{:S(2)}) %collective-permute-start.45) | collective-permute-done | bytes 524320 | tf_op jit(solution)/shard_map/ppermute | solution.py:457
  488.1 6.3 %collective-permute-done.56 = bf16[256,1024]{1,0:T(8,128)(2,1)S(1)} collective-permute-done((bf16[256,1024]{1,0:T(8,128)(2,1)}, bf16[256,1024]{1,0:T(8,128)(2,1)S(1)}, u32[]{:S(2)}, u32[]{:S(2)}) %collective-permute-start.56) | collective-permute-done | bytes 524320 | tf_op jit(solution)/shard_map/ppermute | solution.py:457
  499.4 9.4 %collective-permute-done.75.refs_2_ = bf16[3,3,64,512]{3,2,1,0:T(8,128)(2,1)} collective-permute-done((bf16[3,3,64,512]{3,2,1,0:T(8,128)(2,1)}, bf16[3,3,64,512]{3,2,1,0:T(8,128)(2,1)}, u32[]{:S(2)}, u32[]{:S(2)}) %collective-permute-start.75) | collective-permute-done | bytes 589856 | tf_op jit(solution)/shard_map/ppermute | solution.py:457
  510.9 8.0 %collective-permute-done.76.refs_3_ = bf16[3,3,64,512]{3,2,1,0:T(8,128)(2,1)} collective-permute-done((bf16[3,3,64,512]{3,2,1,0:T(8,128)(2,1)}, bf16[3,3,64,512]{3,2,1,0:T(8,128)(2,1)}, u32[]{:S(2)}, u32[]{:S(2)}) %collective-permute-start.76) | collective-permute-done | bytes 589856 | tf_op jit(solution)/shard_map/ppermute | solution.py:457
  522.0 6.0 %fusion.10 = (f32[512,1024]{1,0:T(8,128)}, bf16[512,1024]{1,0:T(8,128)(2,1)}) fusion(bf16[512,1024]{1,0:T(8,128)(2,1)S(1)} %copy-done.10, f32[512]{0:T(512)S(1)} %broadcast_multiply_fusion, f32[1024]{0:T(1024)S(1)} %bitcast.114, f32[512]{0:T(512)S(1)} %copy-done.80, bf16[512,1024]{1,0:T(8,128)(2,1)} %tie.20, f32[1024,1024]{1,0:T(8,128)S(1)} %copy-done.3, ...), kind=kLoop, calls=%fused_computation.17 | loop fusion | flops 16777216 | bytes 16793604 | tf_op jit(solution)/shard_map/add | solution.py:747
  (467 shorter events, 235.7 us)
Async XLA Ops:
  7.2 237.3 %all-gather.6.cloned.1.call-start = ((), (), s32[]{:S(2)}) async-start(), calls=%async_computation.4 | async-start | bytes 11796480 | tf_op jit(solution)/shard_map/all_gather | solution.py:669
  7.3 32.2 %collective-permute-start.1 = (f32[2,32]{1,0:T(2,128)}, f32[2,32]{1,0:T(2,128)S(1)}, u32[]{:S(2)}, u32[]{:S(2)}) collective-permute-start(f32[2,32]{1,0:T(2,128)} %param.17), channel_id=1, source_target_pairs={{0,1},{1,0},{2,3},{3,2},{4,5},{5,4},{6,7},{7,6},{8,9},{9,8},{10,11... | collective-permute-start | bytes 776 | tf_op jit(solution)/shard_map/ppermute | solution.py:457
  10.3 31.8 %collective-permute-start.7 = (bf16[512,1024]{1,0:T(8,128)(2,1)}, bf16[512,1024]{1,0:T(8,128)(2,1)S(1)}, u32[]{:S(2)}, u32[]{:S(2)}) collective-permute-start(bf16[512,1024]{1,0:T(8,128)(2,1)} %param.13), channel_id=1, source_target_pairs={{0,1},{1,0},{2,3},{3,2},{4,5},{5,4},{6,7},{7,6},{8,9},{9,8},{10,11... | collective-permute-start | bytes 3145736 | tf_op jit(solution)/shard_map/ppermute | solution.py:457
  15.7 29.5 %collective-permute-start.14 = (bf16[3,3,64,512]{3,2,1,0:T(8,128)(2,1)}, bf16[3,3,64,512]{3,2,1,0:T(8,128)(2,1)S(1)}, u32[]{:S(2)}, u32[]{:S(2)}) collective-permute-start(bf16[3,3,64,512]{3,2,1,0:T(8,128)(2,1)} %get-tuple-element.73), channel_id=1, source_target_pairs={{0,2},{2,0},{4,6},{6,4},{8,10},{10,8},{12,14},{14,12},{16,18},{18,... | collective-permute-start | bytes 1769480 | tf_op jit(solution)/shard_map/ppermute | solution.py:457
  15.8 29.5 %collective-permute-start.15 = (bf16[3,3,64,512]{3,2,1,0:T(8,128)(2,1)}, bf16[3,3,64,512]{3,2,1,0:T(8,128)(2,1)}, u32[]{:S(2)}, u32[]{:S(2)}) collective-permute-start(bf16[3,3,64,512]{3,2,1,0:T(8,128)(2,1)} %get-tuple-element.74), channel_id=1, source_target_pairs={{0,4},{2,6},{4,0},{6,2},{8,12},{10,14},{12,8},{14,10},{16,20},{18,... | collective-permute-start | bytes 1769480 | tf_op jit(solution)/shard_map/ppermute | solution.py:457
  17.8 27.4 %collective-permute-start.16 = (bf16[3,3,64,512]{3,2,1,0:T(8,128)(2,1)}, bf16[3,3,64,512]{3,2,1,0:T(8,128)(2,1)}, u32[]{:S(2)}, u32[]{:S(2)}) collective-permute-start(bf16[3,3,64,512]{3,2,1,0:T(8,128)(2,1)} %get-tuple-element.75), channel_id=1, source_target_pairs={{0,6},{2,4},{4,2},{6,0},{8,14},{10,12},{12,10},{14,8},{16,22},{18,... | collective-permute-start | bytes 1769480 | tf_op jit(solution)/shard_map/ppermute | solution.py:457
  49.9 235.2 %all-gather.8.cloned.1.call-start = ((), (), s32[]{:S(2)}) async-start(), calls=%async_computation.5 | async-start | bytes 3932160 | tf_op jit(solution)/shard_map/all_gather | solution.py:669
  58.9 30.9 %collective-permute-start = (bf16[4,64,1536]{2,1,0:T(8,128)(2,1)}, bf16[4,64,1536]{2,1,0:T(8,128)(2,1)}, u32[]{:S(2)}, u32[]{:S(2)}) collective-permute-start(bf16[4,64,1536]{2,1,0:T(8,128)(2,1)} %bitcast.2.refs_0_.refs_4_), channel_id=1, source_target_pairs={{0,2},{2,0},{4,6},{6,4},{8,10},{10,8},{12,14},{14,12},{16,18},{18,... | collective-permute-start | bytes 2359304 | tf_op jit(solution)/shard_map/ppermute | solution.py:457
  85.9 34.6 %collective-permute-start.17 = (bf16[512,1024]{1,0:T(8,128)(2,1)}, bf16[512,1024]{1,0:T(8,128)(2,1)}, u32[]{:S(2)}, u32[]{:S(2)}) collective-permute-start(bf16[512,1024]{1,0:T(8,128)(2,1)} %tie.14), channel_id=1, source_target_pairs={{0,1},{1,0},{2,3},{3,2},{4,5},{5,4},{6,7},{7,6},{8,9},{9,8},{10,11... | collective-permute-start | bytes 3145736 | tf_op jit(solution)/shard_map/ppermute | solution.py:457
  87.4 33.1 %collective-permute-start.18 = (bf16[512,1024]{1,0:T(8,128)(2,1)}, bf16[512,1024]{1,0:T(8,128)(2,1)}, u32[]{:S(2)}, u32[]{:S(2)}) collective-permute-start(bf16[512,1024]{1,0:T(8,128)(2,1)} %tie.14), channel_id=1, source_target_pairs={{0,4},{2,6},{4,0},{6,2},{8,12},{10,14},{12,8},{14,10},{16,20},{18,... | collective-permute-start | bytes 3145736 | tf_op jit(solution)/shard_map/ppermute | solution.py:457
  124.3 35.8 %collective-permute-start.19 = (bf16[512,1024]{1,0:T(8,128)(2,1)}, bf16[512,1024]{1,0:T(8,128)(2,1)S(1)}, u32[]{:S(2)}, u32[]{:S(2)}) collective-permute-start(bf16[512,1024]{1,0:T(8,128)(2,1)} %dynamic-slice_convert_fusion.1), channel_id=1, source_target_pairs={{0,1},{1,0},{2,3},{3,2},{4,5},{5,4},{6,7},{7,6},{8,9},{9,8},{10,11... | collective-permute-start | bytes 3145736 | tf_op jit(solution)/shard_map/ppermute | solution.py:457
  130.2 29.9 %collective-permute-start.21 = (bf16[256,1024]{1,0:T(8,128)(2,1)}, bf16[256,1024]{1,0:T(8,128)(2,1)S(1)}, u32[]{:S(2)}, u32[]{:S(2)}) collective-permute-start(bf16[256,1024]{1,0:T(8,128)(2,1)} %slice.52), channel_id=1, source_target_pairs={{0,1},{1,0},{2,3},{3,2},{4,5},{5,4},{6,7},{7,6},{8,9},{9,8},{10,11... | collective-permute-start | bytes 1572872 | tf_op jit(solution)/shard_map/ppermute | solution.py:457
  131.7 35.0 %collective-permute-start.30 = (bf16[512,1024]{1,0:T(8,128)(2,1)}, bf16[512,1024]{1,0:T(8,128)(2,1)}, u32[]{:S(2)}, u32[]{:S(2)}) collective-permute-start(bf16[512,1024]{1,0:T(8,128)(2,1)} %refs_0_.4), channel_id=1, source_target_pairs={{0,2},{2,0},{4,6},{6,4},{8,10},{10,8},{12,14},{14,12},{16,18},{18,... | collective-permute-start | bytes 3145736 | tf_op jit(solution)/shard_map/ppermute | solution.py:457
  131.7 52.2 %collective-permute-start.27 = (bf16[512,1024]{1,0:T(8,128)(2,1)}, bf16[512,1024]{1,0:T(8,128)(2,1)}, u32[]{:S(2)}, u32[]{:S(2)}) collective-permute-start(bf16[512,1024]{1,0:T(8,128)(2,1)} %collective-permute-done.18.refs_2_.refs_1_.refs_0_), channel_id=1, source_target_pairs={{0,2},{2,0},{4,6},{6,4},{8,10},{10,8},{12,14},{14,12},{16,18},{18,... | collective-permute-start | bytes 3145736 | tf_op jit(solution)/shard_map/ppermute | solution.py:457
  140.7 26.1 %collective-permute-start.31 = (bf16[512,1024]{1,0:T(8,128)(2,1)}, bf16[512,1024]{1,0:T(8,128)(2,1)}, u32[]{:S(2)}, u32[]{:S(2)}) collective-permute-start(bf16[512,1024]{1,0:T(8,128)(2,1)} %collective-permute-done.17.refs_1_), channel_id=1, source_target_pairs={{0,2},{2,0},{4,6},{6,4},{8,10},{10,8},{12,14},{14,12},{16,18},{18,... | collective-permute-start | bytes 3145736 | tf_op jit(solution)/shard_map/ppermute | solution.py:457
  164.7 32.5 %collective-permute-start.22 = (bf16[512,1024]{1,0:T(8,128)(2,1)S(1)}, bf16[512,1024]{1,0:T(8,128)(2,1)S(1)}, u32[]{:S(2)}, u32[]{:S(2)}) collective-permute-start(bf16[512,1024]{1,0:T(8,128)(2,1)S(1)} %multiply_convert_fusion.refs_0_), channel_id=1, source_target_pairs={{0,1},{1,0},{2,3},{3,2},{4,5},{5,4},{6,7},{7,6},{8,9},{9,8},{10,11... | collective-permute-start | bytes 3145736 | tf_op jit(solution)/shard_map/ppermute | solution.py:457
  166.2 30.9 %collective-permute-start.23 = (bf16[512,1024]{1,0:T(8,128)(2,1)S(1)}, bf16[512,1024]{1,0:T(8,128)(2,1)S(1)}, u32[]{:S(2)}, u32[]{:S(2)}) collective-permute-start(bf16[512,1024]{1,0:T(8,128)(2,1)S(1)} %multiply_convert_fusion.refs_0_), channel_id=1, source_target_pairs={{0,4},{2,6},{4,0},{6,2},{8,12},{10,14},{12,8},{14,10},{16,20},{18,... | collective-permute-start | bytes 3145736 | tf_op jit(solution)/shard_map/ppermute | solution.py:457
  201.5 251.6 %reduce-scatter.3.cloned.1.call-start = ((), (), s32[]{:S(2)}) async-start(), calls=%async_computation.2 | async-start | bytes 11796480 | tf_op jit(solution)/shard_map/reduce_scatter | solution.py:705
  205.9 32.2 %collective-permute-start.32 = (bf16[512,1024]{1,0:T(8,128)(2,1)S(1)}, bf16[512,1024]{1,0:T(8,128)(2,1)S(1)}, u32[]{:S(2)}, u32[]{:S(2)}) collective-permute-start(bf16[512,1024]{1,0:T(8,128)(2,1)S(1)} %copy-done.15), channel_id=1, source_target_pairs={{0,2},{2,0},{4,6},{6,4},{8,10},{10,8},{12,14},{14,12},{16,18},{18,... | collective-permute-start | bytes 3145736 | tf_op jit(solution)/shard_map/ppermute | solution.py:457
  285.0 251.0 %reduce-scatter.5.cloned.1.call-start = ((), (), s32[]{:S(2)}) async-start(), calls=%async_computation.3 | async-start | bytes 3932160 | tf_op jit(solution)/shard_map/reduce_scatter | solution.py:705
  369.2 61.6 %collective-permute-start.40 = (bf16[1024,1024]{1,0:T(8,128)(2,1)}, bf16[1024,1024]{1,0:T(8,128)(2,1)}, u32[]{:S(2)}, u32[]{:S(2)}) collective-permute-start(bf16[1024,1024]{1,0:T(8,128)(2,1)} %put_rows.20), channel_id=1, source_target_pairs={{0,2},{2,0},{4,6},{6,4},{8,10},{10,8},{12,14},{14,12},{16,18},{18,... | collective-permute-start | bytes 6291464 | tf_op jit(solution)/shard_map/ppermute | solution.py:457
  372.6 92.0 %collective-permute-start.42 = (bf16[256,1024]{1,0:T(8,128)(2,1)}, bf16[256,1024]{1,0:T(8,128)(2,1)}, u32[]{:S(2)}, u32[]{:S(2)}) collective-permute-start(bf16[256,1024]{1,0:T(8,128)(2,1)} %put_rows.23), channel_id=1, source_target_pairs={{0,4},{2,6},{4,0},{6,2},{8,12},{10,14},{12,8},{14,10},{16,20},{18,... | collective-permute-start | bytes 1572872 | tf_op jit(solution)/shard_map/ppermute | solution.py:457
  390.5 36.1 %collective-permute-start.61 = (bf16[4,2,64,512]{3,2,0,1:T(8,128)(2,1)S(1)}, bf16[4,2,64,512]{3,2,0,1:T(8,128)(2,1)S(1)}, u32[]{:S(2)}, u32[]{:S(2)}) collective-permute-start(bf16[4,2,64,512]{3,2,0,1:T(8,128)(2,1)S(1)} %fusion.20), channel_id=1, source_target_pairs={{0,2},{2,0},{4,6},{6,4},{8,10},{10,8},{12,14},{14,12},{16,18},{18,... | collective-permute-start | bytes 1572872 | tf_op jit(solution)/shard_map/ppermute | solution.py:457
  421.5 27.1 %collective-permute-start.66 = (bf16[4,2,64,1024]{3,2,0,1:T(8,128)(2,1)}, bf16[4,2,64,1024]{3,2,0,1:T(8,128)(2,1)}, u32[]{:S(2)}, u32[]{:S(2)}) collective-permute-start(bf16[4,2,64,1024]{3,2,0,1:T(8,128)(2,1)} %fusion.15), channel_id=1, source_target_pairs={{0,2},{2,0},{4,6},{6,4},{8,10},{10,8},{12,14},{14,12},{16,18},{18,... | collective-permute-start | bytes 3145736 | tf_op jit(solution)/shard_map/ppermute | solution.py:457
  425.9 31.1 %collective-permute-start.54 = (bf16[512,1024]{1,0:T(8,128)(2,1)}, bf16[512,1024]{1,0:T(8,128)(2,1)}, u32[]{:S(2)}, u32[]{:S(2)}) collective-permute-start(bf16[512,1024]{1,0:T(8,128)(2,1)} %dynamic-slice_convert_fusion), channel_id=1, source_target_pairs={{0,1},{1,0},{2,3},{3,2},{4,5},{5,4},{6,7},{7,6},{8,9},{9,8},{10,11... | collective-permute-start | bytes 3145736 | tf_op jit(solution)/shard_map/ppermute | solution.py:457
  430.8 33.9 %collective-permute-start.43 = (bf16[256,1024]{1,0:T(8,128)(2,1)}, bf16[256,1024]{1,0:T(8,128)(2,1)}, u32[]{:S(2)}, u32[]{:S(2)}) collective-permute-start(bf16[256,1024]{1,0:T(8,128)(2,1)} %put_rows.24), channel_id=1, source_target_pairs={{0,1},{1,0},{2,3},{3,2},{4,5},{5,4},{6,7},{7,6},{8,9},{9,8},{10,11... | collective-permute-start | bytes 1572872 | tf_op jit(solution)/shard_map/ppermute | solution.py:457
  482.4 26.5 %collective-permute-start.75 = (bf16[3,3,64,512]{3,2,1,0:T(8,128)(2,1)}, bf16[3,3,64,512]{3,2,1,0:T(8,128)(2,1)}, u32[]{:S(2)}, u32[]{:S(2)}) collective-permute-start(bf16[3,3,64,512]{3,2,1,0:T(8,128)(2,1)} %get-tuple-element.111), channel_id=1, source_target_pairs={{0,4},{2,6},{4,0},{6,2},{8,12},{10,14},{12,8},{14,10},{16,20},{18,... | collective-permute-start | bytes 1769480 | tf_op jit(solution)/shard_map/ppermute | solution.py:457
  483.8 35.1 %collective-permute-start.76 = (bf16[3,3,64,512]{3,2,1,0:T(8,128)(2,1)}, bf16[3,3,64,512]{3,2,1,0:T(8,128)(2,1)}, u32[]{:S(2)}, u32[]{:S(2)}) collective-permute-start(bf16[3,3,64,512]{3,2,1,0:T(8,128)(2,1)} %get-tuple-element.112), channel_id=1, source_target_pairs={{0,6},{2,4},{4,2},{6,0},{8,14},{10,12},{12,10},{14,8},{16,22},{18,... | collective-permute-start | bytes 1769480 | tf_op jit(solution)/shard_map/ppermute | solution.py:457
  494.4 37.7 %collective-permute-start.64 = (bf16[64,512]{1,0:T(8,128)(2,1)}, bf16[64,512]{1,0:T(8,128)(2,1)}, u32[]{:S(2)}, u32[]{:S(2)}) collective-permute-start(bf16[64,512]{1,0:T(8,128)(2,1)} %get-tuple-element.150), channel_id=1, source_target_pairs={{0,16},{2,18},{4,20},{6,22},{8,24},{10,26},{12,28},{14,30},{16,0},... | collective-permute-start | bytes 196616 | tf_op jit(solution)/shard_map/ppermute | solution.py:460
  496.7 35.4 %collective-permute-start.65 = (bf16[64,512]{1,0:T(8,128)(2,1)}, bf16[64,512]{1,0:T(8,128)(2,1)}, u32[]{:S(2)}, u32[]{:S(2)}) collective-permute-start(bf16[64,512]{1,0:T(8,128)(2,1)} %get-tuple-element.149), channel_id=1, source_target_pairs={{0,24},{2,26},{4,28},{6,30},{8,0},{10,2},{12,4},{14,6},{16,8},{18,... | collective-permute-start | bytes 196616 | tf_op jit(solution)/shard_map/ppermute | solution.py:460
  499.4 33.7 %collective-permute-start.68 = (bf16[64,1024]{1,0:T(8,128)(2,1)}, bf16[64,1024]{1,0:T(8,128)(2,1)S(1)}, u32[]{:S(2)}, u32[]{:S(2)}) collective-permute-start(bf16[64,1024]{1,0:T(8,128)(2,1)} %get-tuple-element.147), channel_id=1, source_target_pairs={{0,8},{2,10},{4,12},{6,14},{8,16},{10,18},{12,20},{14,22},{16,24},... | collective-permute-start | bytes 393224 | tf_op jit(solution)/shard_map/ppermute | solution.py:460
  508.8 30.1 %collective-permute-start.69 = (bf16[64,1024]{1,0:T(8,128)(2,1)}, bf16[64,1024]{1,0:T(8,128)(2,1)S(1)}, u32[]{:S(2)}, u32[]{:S(2)}) collective-permute-start(bf16[64,1024]{1,0:T(8,128)(2,1)} %get-tuple-element.146), channel_id=1, source_target_pairs={{0,16},{2,18},{4,20},{6,22},{8,24},{10,26},{12,28},{14,30},{16,0},... | collective-permute-start | bytes 393224 | tf_op jit(solution)/shard_map/ppermute | solution.py:460
  (149 other events, 1529.3 us)
Sparse Core Ops, SparseCore 0:
  50.0 168.0 all-gather.5
  219.6 61.6 all-gather.7
  285.1 161.5 reduce-scatter.2
  448.9 70.0 reduce-scatter.4
